TPU v7x, 32 devices: a whole 2x2x4 slice. The times are simulated.
32 devices in a mesh: pipe: 2 (over y), dp: 16 (over z, x, core).
Axes of the slice: x: 2, y: 2, z: 4, core: 2. Of those that a mesh axis runs over, the one named last changes fastest.
Arguments:
- features: bfloat16 [32, 336, 512], P('dp'), may hold values from -6 to 6
- plan: int32 [16, 2], P('dp'), may hold values from 0 to 1, each once within a row
- trunk_weight: bfloat16 [2, 3, 3, 512, 512], replicated, may hold values from -0.125 to 0.125
- trunk_gain: float32 [2, 512], replicated, may hold values from 0.1 to 1.9
- trunk_shift: float32 [2, 512], replicated, may hold values from -3 to 3
- head_weight: bfloat16 [2, 512, 1792], replicated, may hold values from -0.25 to 0.25
- norm_scale: float32 [2, 512], replicated, may hold values from 0.1 to 1.9
- merging_weight: float32 [2, 3, 1792], replicated, may hold values from -3 to 3
- merged_cotangent: bfloat16 [32, 64, 1792], P('dp'), may hold values from -6 to 6
Outputs:
- merged_maps: bfloat16 [32, 64, 1792], P('dp', None, 'pipe')
- features_grad: float32 [32, 336, 512], P('dp', None, 'pipe')
- trunk_weight_grad: float32 [2, 3, 3, 512, 512], replicated
- head_weight_grad: float32 [2, 512, 1792], replicated
- norm_scale_grad: float32 [2, 512], replicated
- merging_weight_grad: float32 [2, 3, 1792], replicated
Inputs may be any that keep to these rules, and one draw needn't show every extreme that they name: `plan`: each row names every micro-batch's image once.
All inputs are finite; a program needn't handle non-finite values.
Results may differ from a plain program's by a relative error of at most 0.0074.
Values may be sent and summed in bfloat16 or wider, within the bound.
No kernel may reach another device: no remote copies, remote signals or barrier semaphores. Data moves between devices by JAX's collectives and lax.ppermute only.
A program may use at most 192 MiB of HBM per device.

v0:
```python
from functools import partial

import jax
import jax.numpy as jnp
from jax import lax
from jax.sharding import PartitionSpec as P

SIDE = 16


epsilon = 1e-06


def as_sent(shard):

    def short(part):
        return part.astype(jnp.bfloat16) if part.dtype == jnp.float32 else part

    return jax.tree.map(short, shard)


def from_behind(block, axis, distance):
    devices = range(lax.axis_size(axis))
    route = [(i - distance, i) for i in devices if i - distance in devices]
    return lax.ppermute(block, axis, route)


def split_scales(flat_rows, grid_side):
    finest_end = grid_side * grid_side
    middle_end = finest_end + (grid_side // 2) ** 2
    return [
        flat_rows[:finest_end].reshape(grid_side, grid_side, -1),
        flat_rows[finest_end:middle_end].reshape(grid_side // 2, grid_side // 2, -1),
        flat_rows[middle_end:].reshape(grid_side // 4, grid_side // 4, -1),
    ]


def patches(scale_grid):
    extent = scale_grid.shape[0]
    padded = jnp.pad(scale_grid, ((1, 1), (1, 1), (0, 0)))
    pieces = [
        padded[row_off : row_off + extent, col_off : col_off + extent]
        for row_off in range(3)
        for col_off in range(3)
    ]
    return jnp.concatenate(pieces, axis=-1).reshape(extent * extent, -1)


def unpatch(column_grad, extent, channels):
    blocks = column_grad.reshape(extent, extent, 9, channels)
    summed = jnp.zeros((extent + 2, extent + 2, channels), jnp.float32)
    for offset in range(9):
        row_off = offset // 3
        col_off = offset % 3
        summed = summed + jnp.pad(
            blocks[:, :, offset], ((row_off, 2 - row_off), (col_off, 2 - col_off), (0, 0))
        )
    return summed[1:-1, 1:-1].reshape(extent * extent, channels)


def gelu_affine(pre_act, gain_row, shift_row):
    return jax.nn.gelu(gain_row * pre_act + shift_row, approximate=True)


def norm_fn(tap_value, scale_row):
    return (
        tap_value
        * lax.rsqrt(jnp.mean(tap_value * tap_value, axis=-1, keepdims=True) + epsilon)
        * scale_row
    )


def merge_maps(head_maps, weights_merge, grid_side):
    middle = grid_side // 2
    summed = 0.0
    for tap_num in range(len(head_maps)):
        finest, medium, coarse = split_scales(head_maps[tap_num], grid_side)
        pooled = finest.reshape(middle, 2, middle, 2, -1).mean(axis=(1, 3))
        spread = jnp.repeat(jnp.repeat(coarse, 2, axis=0), 2, axis=1)
        summed = (
            summed
            + weights_merge[tap_num, 0] * pooled
            + weights_merge[tap_num, 1] * medium
            + weights_merge[tap_num, 2] * spread
        )
    return summed.reshape(middle * middle, -1)


def trunk_forward(sample, weights, gain_rows, shifts, grid_side):
    outputs = []
    for scale_grid in split_scales(sample, grid_side):
        extent = scale_grid.shape[0]
        hidden = scale_grid
        for layer_num in range(weights.shape[0]):
            pre_act = jnp.dot(
                patches(hidden), weights[layer_num], preferred_element_type=jnp.float32
            )
            hidden = (
                gelu_affine(pre_act, gain_rows[layer_num], shifts[layer_num])
                .astype(jnp.bfloat16)
                .reshape(extent, extent, -1)
            )
        outputs.append(hidden.reshape(extent * extent, -1))
    return jnp.concatenate(outputs, axis=0)


def trunk_backward(sample, tap_grad, weights, gain_rows, shifts, grid_side):
    layer_count = weights.shape[0]
    channels = sample.shape[-1]
    weight_grads = [jnp.zeros(weights.shape[1:], jnp.float32) for layer_num in range(layer_count)]
    input_parts = []
    for scale_grid, grad_grid in zip(
        split_scales(sample, grid_side), split_scales(tap_grad, grid_side)
    ):
        extent = scale_grid.shape[0]
        unfolded_list = []
        pullbacks = []
        hidden = scale_grid
        for layer_num in range(layer_count):
            unfolded = patches(hidden)
            pre_act = jnp.dot(unfolded, weights[layer_num], preferred_element_type=jnp.float32)
            activated, pullback = jax.vjp(
                partial(gelu_affine, gain_row=gain_rows[layer_num], shift_row=shifts[layer_num]),
                pre_act,
            )
            unfolded_list.append(unfolded)
            pullbacks.append(pullback)
            hidden = activated.astype(jnp.bfloat16).reshape(extent, extent, -1)
        upstream = grad_grid.reshape(extent * extent, -1).astype(jnp.float32)
        for layer_num in reversed(range(layer_count)):
            pre_grad = pullbacks[layer_num](upstream)[0].astype(jnp.bfloat16)
            weight_grads[layer_num] = weight_grads[layer_num] + lax.dot_general(
                unfolded_list[layer_num],
                pre_grad,
                (((0,), (0,)), ((), ())),
                preferred_element_type=jnp.float32,
            )
            col_grad = lax.dot_general(
                pre_grad,
                weights[layer_num],
                (((1,), (1,)), ((), ())),
                preferred_element_type=jnp.float32,
            )
            upstream = unpatch(col_grad, extent, channels)
        input_parts.append(upstream)
    return (jnp.stack(weight_grads), jnp.concatenate(input_parts, axis=0))


def tap_heads(sample, tap_rows, cotangent, head_weight, norm_scale, merging_weight, grid_side):
    tap_list = [sample.astype(jnp.float32), tap_rows.astype(jnp.float32)]
    low_normed = []
    norm_pulls = []
    head_maps = []
    for tap_num in range(len(tap_list)):
        normed, norm_pull = jax.vjp(norm_fn, tap_list[tap_num], norm_scale[tap_num])
        rounded = normed.astype(jnp.bfloat16)
        low_normed.append(rounded)
        norm_pulls.append(norm_pull)
        head_maps.append(jnp.dot(rounded, head_weight[tap_num], preferred_element_type=jnp.float32))
    merged_sum, merge_pull = jax.vjp(
        partial(merge_maps, grid_side=grid_side), head_maps, merging_weight
    )
    head_grads, merging_part = merge_pull(cotangent.astype(jnp.float32))
    weight_parts = []
    scale_parts = []
    tap_grads = []
    for tap_num in range(len(tap_list)):
        low_grad = head_grads[tap_num].astype(jnp.bfloat16)
        weight_parts.append(
            lax.dot_general(
                low_normed[tap_num],
                low_grad,
                (((0,), (0,)), ((), ())),
                preferred_element_type=jnp.float32,
            )
        )
        normed_grad = lax.dot_general(
            low_grad,
            head_weight[tap_num],
            (((1,), (1,)), ((), ())),
            preferred_element_type=jnp.float32,
        )
        tap_grad, scale_grad = norm_pulls[tap_num](normed_grad)
        tap_grads.append(tap_grad)
        scale_parts.append(scale_grad)
    return (
        merged_sum.astype(jnp.bfloat16),
        jnp.stack(weight_parts),
        jnp.stack(scale_parts),
        merging_part,
        tap_grads[0],
        tap_grads[1].astype(jnp.bfloat16),
    )


def body(
    features,
    plan,
    trunk_weight,
    trunk_gain,
    trunk_shift,
    head_weight,
    norm_scale,
    merging_weight,
    merged_cotangent,
):
    micro_count = features.shape[0]
    pixel_count = features.shape[1]
    channels = features.shape[2]
    head_width = head_weight.shape[2]
    grid_side = SIDE
    weights = trunk_weight.reshape(trunk_weight.shape[0], 9 * channels, channels)
    section_index = lax.axis_index("pipe")
    empty_rows = jnp.zeros((pixel_count, channels), jnp.bfloat16)

    def select_image(micro_num):
        return lax.dynamic_index_in_dim(features, plan[0, micro_num], 0, keepdims=False)

    def into_slot(micro_num, contribution):
        one_hot = (jnp.arange(micro_count, dtype=jnp.int32) == plan[0, micro_num]).astype(
            jnp.float32
        )
        return one_hot[:, None, None] * contribution[None]

    def run_tick(carried, inbox_tap, inbox_grad, forward_num, middle_num, backward_num):

        def first_section(carried):
            trunk_grad, head_grad, scale_grad, merging_grad, input_grad, merged_out = carried
            sent_tap = empty_rows
            if forward_num is not None:
                sent_tap = trunk_forward(
                    select_image(forward_num), weights, trunk_gain, trunk_shift, grid_side
                )
            if backward_num is not None:
                weight_part, input_part = trunk_backward(
                    select_image(backward_num),
                    inbox_grad,
                    weights,
                    trunk_gain,
                    trunk_shift,
                    grid_side,
                )
                trunk_grad = trunk_grad + weight_part
                input_grad = input_grad + into_slot(backward_num, input_part)
            return (
                (trunk_grad, head_grad, scale_grad, merging_grad, input_grad, merged_out),
                sent_tap,
                empty_rows,
            )

        def second_section(carried):
            trunk_grad, head_grad, scale_grad, merging_grad, input_grad, merged_out = carried
            sent_grad = empty_rows
            if middle_num is not None:
                merged_part, weight_part, scale_part, merging_part, feature_part, tap_grad = (
                    tap_heads(
                        select_image(middle_num),
                        inbox_tap,
                        merged_cotangent[middle_num],
                        head_weight,
                        norm_scale,
                        merging_weight,
                        grid_side,
                    )
                )
                head_grad = head_grad + weight_part
                scale_grad = scale_grad + scale_part
                merging_grad = merging_grad + merging_part
                input_grad = input_grad + into_slot(middle_num, feature_part)
                merged_out = merged_out.at[middle_num].set(merged_part)
                sent_grad = tap_grad
            return (
                (trunk_grad, head_grad, scale_grad, merging_grad, input_grad, merged_out),
                empty_rows,
                sent_grad,
            )

        carried, sent_tap, sent_grad = lax.cond(
            section_index == 0, first_section, second_section, carried
        )
        if forward_num is not None:
            inbox_tap = from_behind(as_sent(sent_tap), "pipe", 1).astype(sent_tap.dtype)
        if middle_num is not None:
            inbox_grad = jax.tree.map(
                lambda part, own: part.astype(own.dtype),
                from_behind(as_sent(sent_grad), "pipe", -1),
                sent_grad,
            )
        return (carried, inbox_tap, inbox_grad)

    carried = (
        jnp.zeros(weights.shape, jnp.float32),
        jnp.zeros(head_weight.shape, jnp.float32),
        jnp.zeros(norm_scale.shape, jnp.float32),
        jnp.zeros(merging_weight.shape, jnp.float32),
        jnp.zeros((micro_count, pixel_count, channels), jnp.float32),
        jnp.zeros((micro_count, merged_cotangent.shape[1], head_width), jnp.bfloat16),
    )
    timeline = []
    for micro_num in range(micro_count):
        timeline = timeline + [
            (micro_num, None, None),
            (None, micro_num, None),
            (None, None, micro_num),
        ]
    inbox_tap = empty_rows
    inbox_grad = empty_rows
    for forward_num, middle_num, backward_num in timeline:
        carried, inbox_tap, inbox_grad = run_tick(
            carried, inbox_tap, inbox_grad, forward_num, middle_num, backward_num
        )
    trunk_grad, head_grad, scale_grad, merging_grad, input_grad, merged_out = carried
    half_width = head_width // 2
    returned = from_behind(merged_out[:, :, :half_width], "pipe", -1)
    merged_maps = jnp.where(section_index == 0, returned, merged_out[:, :, half_width:])
    features_grad = lax.psum_scatter(input_grad, "pipe", scatter_dimension=2, tiled=True)
    trunk_rows = trunk_grad.reshape(-1, channels)
    head_rows = head_grad.reshape(-1, head_width)
    scale_flat = scale_grad.reshape(-1)
    merging_flat = merging_grad.reshape(-1)
    shares = (
        lax.psum_scatter(trunk_rows, ("pipe", "dp"), scatter_dimension=0, tiled=True),
        lax.psum_scatter(head_rows, ("pipe", "dp"), scatter_dimension=0, tiled=True),
        lax.psum_scatter(scale_flat, ("pipe", "dp"), scatter_dimension=0, tiled=True),
        lax.psum_scatter(merging_flat, ("pipe", "dp"), scatter_dimension=0, tiled=True),
    )
    summed_all = (
        lax.all_gather(shares[0], ("pipe", "dp"), axis=0, tiled=True),
        lax.all_gather(shares[1], ("pipe", "dp"), axis=0, tiled=True),
        lax.all_gather(shares[2], ("pipe", "dp"), axis=0, tiled=True),
        lax.all_gather(shares[3], ("pipe", "dp"), axis=0, tiled=True),
    )
    return (
        merged_maps,
        features_grad,
        summed_all[0].reshape(trunk_weight.shape),
        summed_all[1].reshape(head_weight.shape),
        summed_all[2].reshape(norm_scale.shape),
        summed_all[3].reshape(merging_weight.shape),
    )


def solution(mesh):
    placed = (P("dp", None, None), P("dp", None), P(), P(), P(), P(), P(), P(), P("dp", None, None))
    return jax.shard_map(
        body,
        mesh=mesh,
        in_specs=placed,
        out_specs=(P("dp", None, "pipe"), P("dp", None, "pipe"), P(), P(), P(), P()),
        check_vma=False,
    )
```

profile of v0, /device:TPU:0, one launch (start us, length us, event | category | flops | bytes accessed | tf_op | source)
XLA Modules:
  0.0 831.0 jit_solution(251897491578529574)
XLA Ops:
  8.1 21.6 %conditional.7 = (bf16[336,512]{1,0:T(8,128)(2,1)S(1)}) conditional(s32[]{:T(128)} %convert_element_type.454, () %tuple.61, (f32[2,512]{1,0:T(2,128)}, s32[1,2]{1,0:T(1,128)}, bf16[2,336,512]{2,1,0:T(8,128)(2,1)}, bf16[2,4608,512]{2,1,0:T(8,128)(2,1)}, f32[2,512]{1,0:T(2,128)}) %tuple.377), branch_computations={%region_2.3_spmd, %region_3.4_spmd} | conditional | flops 3175710720 | bytes 95101080 | solution.py:278
  13.4 3.1 fusion.269
  16.8 3.2 fusion.281
  20.3 4.0 fusion.229
  31.7 8.5 %collective-permute-done.1 = bf16[336,512]{1,0:T(8,128)(2,1)S(1)} collective-permute-done((bf16[336,512]{1,0:T(8,128)(2,1)}, bf16[336,512]{1,0:T(8,128)(2,1)S(1)}, u32[]{:S(2)}, u32[]{:S(2)}) %collective-permute-start.1) | collective-permute-done | bytes 344096 | tf_op jit(solution)/shard_map/ppermute | solution.py:25
  40.2 11.6 %conditional.8 = (f32[2,512,1792]{2,1,0:T(8,128)}, f32[2,512]{1,0:T(2,128)S(1)}, f32[2,3,1792]{2,1,0:T(4,128)}, f32[2,336,512]{2,1,0:T(8,128)S(1)}, bf16[2,64,17...) conditional(s32[]{:T(128)} %convert_element_type.454, (s32[1,2]{1,0:T(1,128)}, bf16[2,336,512]{2,1,0:T(8,128)(2,1)}, ...), branch_computations={%region_4.23_spmd, %region_23.24_spmd} | conditional | flops 3722479104 | bytes 164811984 | solution.py:278
  48.3 3.5 broadcast_in_dim.72
  53.1 22.7 %conditional.6 = (bf16[336,512]{1,0:T(8,128)(2,1)S(1)}) conditional(s32[]{:T(128)} %convert_element_type.454, () %tuple.59, (f32[2,512]{1,0:T(2,128)}, s32[1,2]{1,0:T(1,128)}, bf16[2,336,512]{2,1,0:T(8,128)(2,1)}, bf16[2,4608,512]{2,1,0:T(8,128)(2,1)}, f32[2,512]{1,0:T(2,128)}) %tuple.378), branch_computations={%region_0.0_spmd, %region_1.2_spmd} | conditional | flops 3175710720 | bytes 95101096 | solution.py:278
  59.6 3.1 fusion.127
  63.1 3.2 fusion.139
  66.5 4.1 fusion.87
  76.6 32.7 %collective-permute-start = (bf16[336,512]{1,0:T(8,128)(2,1)}, bf16[336,512]{1,0:T(8,128)(2,1)S(1)}, u32[]{:S(2)}, u32[]{:S(2)}) collective-permute-start(bf16[336,512]{1,0:T(8,128)(2,1)} %copy-done.50), channel_id=1, source_target_pairs={{0,16},{1,17},{2,18},{3,19},{4,20},{5,21},{6,22},{7,23},{8,24},{9,... | collective-permute-start | bytes 1032200 | tf_op jit(solution)/shard_map/ppermute | solution.py:25
  109.2 5.0 collective-permute-done.2
  114.2 92.1 %conditional.9 = (f32[2,4608,512]{2,1,0:T(8,128)}, f32[2,336,512]{2,1,0:T(8,128)S(1)}) conditional(s32[]{:T(128)} %convert_element_type.454, f32[2,336,512]{2,1,0:T(8,128)S(1)} %get-tuple-element.207, (s32[1,2]{1,0:T(1,128)}, bf16[2,336,512]{2,1,0:T(8,128)(2,1)}, f32[2,512]{1,0:T(2,128)}, bf16[336,512]{1,0:T(8,128)(2,1)}, ...), branch_computations={%region_24.25_spmd, %region_25.26_spmd} | conditional | flops 9540804608 | bytes 396926144 | solution.py:278
  121.1 3.7 multiply_convert_fusion.2
  125.2 3.2 fusion.402
  129.3 3.6 fusion.317
  133.2 3.5 fusion.359
  140.8 2.7 fusion.335
  146.4 5.1 add_bitcast_fusion
  151.5 6.6 fusion.715
  160.6 3.7 fusion.420
  165.2 3.9 fusion.397
  169.1 3.8 fusion.723
  185.9 5.0 add_bitcast_fusion.1
  190.9 15.2 %pad_maximum_fusion.2 = f32[2,4608,512]{2,1,0:T(8,128)} fusion(f32[1,4608,512]{2,1,0:T(8,128)} %add_bitcast_fusion, f32[1,4608,512]{2,1,0:T(8,128)} %add_bitcast_fusion.1), kind=kLoop, calls=%fused_computation.412 | loop fusion | flops 4718592 | bytes 37748736 | tf_op jit(solution)/shard_map/cond/branch_1_fun/stack | solution.py:146
  206.3 25.0 %conditional.10 = (f32[2,512,1792]{2,1,0:T(8,128)}, f32[2,512]{1,0:T(2,128)}, f32[2,3,1792]{2,1,0:T(4,128)}, f32[2,336,512]{2,1,0:T(8,128)S(1)}, bf16[2,64,1792]{2,1,0:T(8,128)(2,1)}, /*index=5*/bf16[336,512]{1,0:T(8,128)(2,1)}) conditional(s32[]{:T(128)} %convert_element_type.454, (s32[1,2]{1,0:T(1,128)}, bf16[2,336,512]{2,1,0:T(8,128)(2,1)}, ...), branch_computations={%region_26.45_spmd, %region_45.46_spmd} | conditional | flops 3724669952 | bytes 177738736 | solution.py:278
  224.0 6.6 copy.738
  233.6 9.9 %collective-permute-done.4 = bf16[336,512]{1,0:T(8,128)(2,1)S(1)} collective-permute-done((bf16[336,512]{1,0:T(8,128)(2,1)S(1)}, bf16[336,512]{1,0:T(8,128)(2,1)S(1)}, u32[]{:S(2)}, u32[]{:S(2)}) %collective-permute-start.4) | collective-permute-done | bytes 344096 | tf_op jit(solution)/shard_map/ppermute | solution.py:25
  243.5 91.7 %conditional.11 = ((f32[2,4608,512]{2,1,0:T(8,128)}, f32[2,336,512]{2,1,0:T(8,128)S(1)})) conditional(s32[]{:T(128)} %convert_element_type.454, (f32[2,4608,512]{2,1,0:T(8,128)}, f32[2,336,512]{2,1,0:T(8,128)S(1)}) %tuple.67, (s32[1,2]{1,0:T(1,128)S(1)}, bf16[2,336,512]{2,1,0:T(8,128)(2,1)S(1)}, f32[2,512]{1,0:T(2,128)S(1)}, ...), branch_computations={%region_46.47_spmd, %region_47.48_spmd} | conditional | flops 9545523200 | bytes 406043264 | solution.py:278
  247.6 3.7 multiply_convert_fusion.5
  251.6 3.1 fusion.549
  255.6 3.5 fusion.464
  259.4 3.5 fusion.506
  270.9 5.1 add_bitcast_fusion.2
  276.0 6.6 fusion.718
  285.8 3.7 fusion.567
  289.6 4.2 fusion.544
  293.8 3.8 fusion.729
  309.5 5.0 add_bitcast_fusion.3
  314.5 20.5 %maximum_add_fusion = f32[2,4608,512]{2,1,0:T(8,128)} fusion(f32[2,4608,512]{2,1,0:T(8,128)} %get-tuple-element.174, f32[1,4608,512]{2,1,0:T(8,128)} %add_bitcast_fusion.2, f32[1,4608,512]{2,1,0:T(8,128)} %add_bitcast_fusion.3), kind=kLoop, calls=%fused_computation.759 | loop fusion | flops 9437184 | bytes 56623104 | tf_op jit(solution)/shard_map/cond/branch_1_fun/add | solution.py:243
  336.3 43.5 %reduce-scatter.8.cloned.1.call-done = f32[32,1792]{1,0:T(8,128)} async-done(((f32[1024,1792]{1,0:T(8,128)}), f32[32,1792]{1,0:T(8,128)}) %reduce-scatter.8.cloned.1.call-update) | async-done | bytes 229392 | tf_op jit(solution)/shard_map/reduce_scatter | solution.py:323
  379.9 210.8 %reduce-scatter.6.cloned.1.call-done = f32[288,512]{1,0:T(8,128)} async-done(((f32[9216,512]{1,0:T(8,128)}), f32[288,512]{1,0:T(8,128)}) %reduce-scatter.6.cloned.1.call-update) | async-done | bytes 589840 | tf_op jit(solution)/shard_map/reduce_scatter | solution.py:322
  594.4 41.1 %all-reduce.162 = (f32[1024]{0:T(1024)S(1)}, f32[10752]{0:T(1024)S(1)}) all-reduce(f32[1024]{0:T(1024)S(1)} %bitcast.1580, f32[10752]{0:T(1024)S(1)} %reshape.954), channel_id=5, replica_groups=mesh['pipe'=2,'dp'=16] {'pipe','dp'}, use_global_device_ids=true, to_apply=%region_51.52.clone | all-reduce | flops 11776 | bytes 94208
  636.0 41.8 %all-reduce.161 = (f32[1024]{0:T(1024)S(1)}, f32[10752]{0:T(1024)S(1)}) all-reduce(f32[1024]{0:T(1024)S(1)} %dynamic-slice_dynamic-update-slice_fusion.1, f32[10752]{0:T(1024)S(1)} %dynamic-slice_dynamic-update-slice_fusion), channel_id=1, replica_groups=mesh['pipe'=2,'dp'=16] {'pipe','dp'}, use_global_device_ids=true, to_apply=%add.157 | all-reduce | flops 11776 | bytes 94208
  680.7 124.6 %all-gather.3.cloned.1.call-done = f32[9216,512]{1,0:T(8,128)} async-done(((f32[288,512]{1,0:T(8,128)}), f32[9216,512]{1,0:T(8,128)}) %all-gather.3.cloned.1.call-update) | async-done | bytes 18874384 | tf_op jit(solution)/shard_map/all_gather | solution.py:328
  805.2 15.4 %copy.752 = f32[2,3,3,512,512]{4,3,2,1,0:T(8,128)} copy(f32[2,3,3,512,512]{4,3,2,1,0:T(8,128)} %bitcast.1435) | data formatting | bytes 37748736
  820.6 3.0 copy.753
  (580 shorter events, 90.4 us)
Async XLA Ops:
  8.0 371.8 %reduce-scatter.8.cloned.1.call-start = ((), (), s32[]{:S(2)}) async-start(), calls=%async_computation.6 | async-start | bytes 7569408 | tf_op jit(solution)/shard_map/reduce_scatter | solution.py:323
  8.1 32.2 %copy-start.16 = (bf16[2,64,1792]{2,1,0:T(8,128)(2,1)S(1)}, bf16[2,64,1792]{2,1,0:T(8,128)(2,1)}, u32[]{:S(2)}) copy-start(bf16[2,64,1792]{2,1,0:T(8,128)(2,1)} %param.33) | copy-start | bytes 1376260
  8.1 32.2 %copy-start.51 = (f32[2,3,1792]{2,0,1:T(2,128)S(1)}, f32[2,3,1792]{2,0,1:T(2,128)}, u32[]{:S(2)}) copy-start(f32[2,3,1792]{2,0,1:T(2,128)} %param.32) | copy-start | bytes 129028
  16.8 3.3 copy-start.4
  16.8 7.8 copy-start
  30.4 9.8 %collective-permute-start.1 = (bf16[336,512]{1,0:T(8,128)(2,1)}, bf16[336,512]{1,0:T(8,128)(2,1)S(1)}, u32[]{:S(2)}, u32[]{:S(2)}) collective-permute-start(bf16[336,512]{1,0:T(8,128)(2,1)} %copy-done.49), channel_id=1, source_target_pairs={{0,16},{1,17},{2,18},{3,19},{4,20},{5,21},{6,22},{7,23},{8,24},{9,... | collective-permute-start | bytes 1032200 | tf_op jit(solution)/shard_map/ppermute | solution.py:25
  51.8 62.4 %collective-permute-start.2 = (bf16[336,512]{1,0:T(8,128)(2,1)}, bf16[336,512]{1,0:T(8,128)(2,1)}, u32[]{:S(2)}, u32[]{:S(2)}) collective-permute-start(bf16[336,512]{1,0:T(8,128)(2,1)} %get-tuple-element.208), channel_id=1, source_target_pairs={{16,0},{17,1},{18,2},{19,3},{20,4},{21,5},{22,6},{23,7},{24,8},{25... | collective-permute-start | bytes 1032200 | tf_op jit(solution)/shard_map/ppermute | solution.py:25
  63.0 3.3 copy-start.6
  63.0 7.8 copy-start.1
  76.6 129.8 %collective-permute-start = (bf16[336,512]{1,0:T(8,128)(2,1)}, bf16[336,512]{1,0:T(8,128)(2,1)S(1)}, u32[]{:S(2)}, u32[]{:S(2)}) collective-permute-start(bf16[336,512]{1,0:T(8,128)(2,1)} %copy-done.50), channel_id=1, source_target_pairs={{0,16},{1,17},{2,18},{3,19},{4,20},{5,21},{6,22},{7,23},{8,24},{9,... | collective-permute-start | bytes 1032200 | tf_op jit(solution)/shard_map/ppermute | solution.py:25
  118.5 10.7 %copy-start.88 = (f32[1,512]{1,0:T(1,128)}, f32[1,512]{1,0:T(1,128)S(1)}, u32[]{:S(2)}) copy-start(f32[1,512]{1,0:T(1,128)S(1)} %get-tuple-element.519) | copy-start | bytes 6148 | tf_op jit(solution)/shard_map/cond
  118.5 10.7 %copy-start.115 = (f32[1,512]{1,0:T(1,128)}, f32[1,512]{1,0:T(1,128)S(1)}, u32[]{:S(2)}) copy-start(f32[1,512]{1,0:T(1,128)S(1)} %get-tuple-element.526) | copy-start | bytes 6148 | tf_op jit(solution)/shard_map/cond
  118.5 14.7 %copy-start.111 = (f32[1,512]{1,0:T(1,128)}, f32[1,512]{1,0:T(1,128)S(1)}, u32[]{:S(2)}) copy-start(f32[1,512]{1,0:T(1,128)S(1)} %get-tuple-element.518) | copy-start | bytes 6148 | tf_op jit(solution)/shard_map/cond
  118.5 14.7 %copy-start.113 = (f32[1,512]{1,0:T(1,128)}, f32[1,512]{1,0:T(1,128)S(1)}, u32[]{:S(2)}) copy-start(f32[1,512]{1,0:T(1,128)S(1)} %get-tuple-element.527) | copy-start | bytes 6148 | tf_op jit(solution)/shard_map/cond
  121.1 3.7 copy-start.42
  125.2 3.2 copy-start.44
  125.2 3.8 copy-start.7
  129.0 8.3 %slice-start = ((s8[9437184]{0:T(1024)(128)(4,1)}), s8[4194304]{0:T(1024)(128)(4,1)S(1)}, s32[]{:S(2)}) async-start(s8[9437184]{0:T(1024)(128)(4,1)} %bitcast.1430), calls=%async_computation.8 | async-start | bytes 8388608 | tf_op jit(solution)/shard_map/cond
  129.2 3.6 copy-start.37
  132.9 3.9 copy-start.39
  132.9 4.4 slice-start.1
  133.2 4.1 slice-start.2
  136.8 6.8 copy-start.72
  151.5 6.6 copy-start.108
  158.1 2.4 copy-start.93
  160.5 4.7 copy-start.73
  173.7 2.7 slice-start.8
  174.0 2.4 slice-start.9
  231.3 12.2 %copy-start.3 = (bf16[2,336,512]{2,1,0:T(8,128)(2,1)S(1)}, bf16[2,336,512]{2,1,0:T(8,128)(2,1)}, u32[]{:S(2)}) copy-start(bf16[2,336,512]{2,1,0:T(8,128)(2,1)} %param.25) | copy-start | bytes 2064388
  231.3 12.2 %copy-start.75 = (f32[2,512]{1,0:T(2,128)S(1)}, f32[2,512]{1,0:T(2,128)}, u32[]{:S(2)}) copy-start(f32[2,512]{1,0:T(2,128)} %param.28) | copy-start | bytes 12292
  231.3 12.2 %copy-start.76 = (f32[2,512]{1,0:T(2,128)S(1)}, f32[2,512]{1,0:T(2,128)}, u32[]{:S(2)}) copy-start(f32[2,512]{1,0:T(2,128)} %param.29) | copy-start | bytes 12292
  231.3 12.2 %copy-start.110 = (s32[1,2]{1,0:T(1,128)S(1)}, s32[1,2]{1,0:T(1,128)}, u32[]{:S(2)}) copy-start(s32[1,2]{1,0:T(1,128)} %param.26) | copy-start | bytes 28
  231.4 359.3 %reduce-scatter.6.cloned.1.call-start = ((), (), s32[]{:S(2)}) async-start(), calls=%async_computation.4 | async-start | bytes 19464192 | tf_op jit(solution)/shard_map/reduce_scatter | solution.py:322
  232.3 11.2 %collective-permute-start.4 = (bf16[336,512]{1,0:T(8,128)(2,1)S(1)}, bf16[336,512]{1,0:T(8,128)(2,1)S(1)}, u32[]{:S(2)}, u32[]{:S(2)}) collective-permute-start(bf16[336,512]{1,0:T(8,128)(2,1)S(1)} %copy-done.48), channel_id=1, source_target_pairs={{16,0},{17,1},{18,2},{19,3},{20,4},{21,5},{22,6},{23,7},{24,8},{25... | collective-permute-start | bytes 1032200 | tf_op jit(solution)/shard_map/ppermute | solution.py:25
  243.5 15.9 %copy-start.121 = (bf16[336,512]{1,0:T(8,128)(2,1)}, bf16[336,512]{1,0:T(8,128)(2,1)S(1)}, u32[]{:S(2)}) copy-start(bf16[336,512]{1,0:T(8,128)(2,1)S(1)} %get-tuple-element.178) | copy-start | bytes 1032196 | tf_op jit(solution)/shard_map/cond
  247.2 37.7 %copy-start.91 = (f32[1,512]{1,0:T(1,128)}, f32[1,512]{1,0:T(1,128)S(1)}, u32[]{:S(2)}) copy-start(f32[1,512]{1,0:T(1,128)S(1)} %get-tuple-element.617) | copy-start | bytes 6148 | tf_op jit(solution)/shard_map/cond
  251.6 3.2 copy-start.46
  255.4 8.1 slice-start.3
  259.1 4.4 slice-start.4
  259.4 4.1 slice-start.5
  262.9 5.1 copy-start.74
  276.0 6.6 copy-start.109
  336.3 257.2 %copy-start.82 = (f32[2,512]{1,0:T(2,128)S(1)}, f32[2,512]{1,0:T(2,128)}, u32[]{:S(2)}) copy-start(f32[2,512]{1,0:T(2,128)} %get-tuple-element.218) | copy-start | bytes 12292
  336.3 344.4 %all-gather.5.cloned.1.call-start = ((), (), s32[]{:S(2)}) async-start(), calls=%async_computation.7 | async-start | bytes 7569408 | tf_op jit(solution)/shard_map/all_gather | solution.py:329
  379.8 425.4 %all-gather.3.cloned.1.call-start = ((), (), s32[]{:S(2)}) async-start(), calls=%async_computation.5 | async-start | bytes 19464192 | tf_op jit(solution)/shard_map/all_gather | solution.py:328
  590.7 214.5 %reduce-scatter.4.cloned.1.call-start = ((), (), s32[]{:S(2)}) async-start(), calls=%async_computation.3 | async-start | bytes 2064384 | tf_op jit(solution)/shard_map/reduce_scatter | solution.py:316
  592.2 86.8 %collective-permute-start.3 = (bf16[2,64,896]{2,1,0:T(8,128)(2,1)S(1)}, bf16[2,64,896]{2,1,0:T(8,128)(2,1)S(1)}, u32[]{:S(2)}, u32[]{:S(2)}) collective-permute-start(bf16[2,64,896]{2,1,0:T(8,128)(2,1)S(1)} %slice.1331), channel_id=1, source_target_pairs={{16,0},{17,1},{18,2},{19,3},{20,4},{21,5},{22,6},{23,7},{24,8},{25... | collective-permute-start | bytes 688136 | tf_op jit(solution)/shard_map/ppermute | solution.py:25
  805.2 15.4 %copy-start.15 = (f32[1024,1792]{1,0:T(8,128)S(1)}, f32[1024,1792]{1,0:T(8,128)}, u32[]{:S(2)}) copy-start(f32[1024,1792]{1,0:T(8,128)} %all-gather.5.cloned.1.call-done) | copy-start | bytes 22020100
  (31 other events, 39.4 us)
Sparse Core Ops, SparseCore 0:
  231.5 148.3 reduce-scatter.7
  387.9 202.6 reduce-scatter.5
  594.0 84.7 all-gather.4
  682.0 123.1 all-gather.2
Sparse Core Ops, SparseCore 1:
  594.0 23.7 reduce-scatter.3
where the time goes:
time: 837 us; the launch traced here: 831 us
  waiting for transfers between devices  403 us (48%)
  matrix products  128 us (15%)
  blocking collectives  82.9 us (10%)
  local copies, waits for them, and re-layouts  81.9 us (10%)
  other arithmetic  46.3 us (6%)
  starting transfers between devices  38 us (5%)
  loops' own time  35.3 us (4%)
  between operations  15.7 us (2%)
    reduce_scatter x1, waiting for transfers between devices, body(): lax.psum_scatter(trunk_rows, ('pipe', 'dp'), scatter_dimension=0, tiled=T...  211 us
    all_gather x1, waiting for transfers between devices, body(): lax.all_gather(shares[0], ('pipe', 'dp'), axis=0, tiled=True)  125 us
    unnamed x2, blocking collectives  82.9 us
    reduce_scatter x1, waiting for transfers between devices, body(): lax.psum_scatter(head_rows, ('pipe', 'dp'), scatter_dimension=0, tiled=True)  43.5 us
    ppermute x5, starting transfers between devices, from_behind(): return lax.ppermute(block, axis, route)  37.8 us
    dot_general x12, matrix products, trunk_backward(): jnp.dot(unfolded, weights[layer_num], preferred_element_type=jnp.float32)  36.1 us
    another operation x6, loops' own time, run_tick(): lax.cond(section_index == 0, first_section, second_section, carried)  35.3 us
    dot_general x12, matrix products, trunk_backward(): lax.dot_general(pre_grad, weights[layer_num], (((1,), (1,)), ((), ())), p...  31.8 us
  transfers between devices with their start and end apart: 10, of which 6 were waited for; matrix products, arithmetic and copies ran while one was open for 23% of the time, Pallas kernels for 0%

commit v1 on v0

v1 whole, which is shorter than its diff:
```python
from functools import partial

import jax
import jax.numpy as jnp
from jax import lax
from jax.experimental import pallas as pl
from jax.experimental.pallas import tpu as pltpu
from jax.sharding import PartitionSpec as P

SIDE = 16
EPSILON = 1e-06
F32 = jnp.float32
BF16 = jnp.bfloat16
AXES = ("pipe", "dp")
VMEM_BYTES = 50 * 1024 * 1024


def spec(memory):
    return pl.BlockSpec(memory_space=memory)


def params():
    return pltpu.CompilerParams(vmem_limit_bytes=VMEM_BYTES)


def grids(side):
    first = 0
    found = []
    for extent in (side, side // 2, side // 4):
        found.append((first, extent))
        first += extent * extent
    return found


def rows_of(side):
    return side * side + (side // 2) ** 2 + (side // 4) ** 2


def iota(shape, dim):
    return lax.broadcasted_iota(jnp.int32, shape, dim)


def edge_masks(side):
    row = iota((rows_of(side), 1), 0)
    first = jnp.zeros(row.shape, jnp.bool_)
    last = jnp.zeros(row.shape, jnp.bool_)
    for start, extent in grids(side):
        inside = (row >= start) & (row < start + extent * extent)
        column = (row - start) & (extent - 1)
        first = first | (inside & (column == 0))
        last = last | (inside & (column == extent - 1))
    return first, last


def column_shifts(value, side, target):
    first, last = edge_masks(side)
    rows = value.shape[0]
    target[0] = jnp.where(first, 0.0, pltpu.roll(value, 1, 0))
    target[1] = value
    target[2] = jnp.where(last, 0.0, pltpu.roll(value, rows - 1, 0))


def row_shift(shifted, b, a, side):
    parts = []
    width = shifted.shape[2]
    for start, extent in grids(side):
        count = extent * extent
        if a == 1:
            part = shifted[b, start : start + count, :]
        elif extent % 8 == 0:
            blank = jnp.zeros((extent, width), F32)
            if a == 0:
                part = jnp.concatenate([blank, shifted[b, start : start + count - extent, :]], axis=0)
            else:
                part = jnp.concatenate([shifted[b, start + extent : start + count, :], blank], axis=0)
        else:
            whole = shifted[b, start : start + count, :]
            row = iota((count, 1), 0)
            if a == 0:
                part = jnp.where(row < extent, 0.0, pltpu.roll(whole, extent, 0))
            else:
                part = jnp.where(row >= count - extent, 0.0, pltpu.roll(whole, count - extent, 0))
        parts.append(part.astype(BF16))
    return parts


def put_row_shift(target, row_start, lane_start, shifted, b, a, side):
    width = shifted.shape[2]
    for (start, extent), part in zip(grids(side), row_shift(shifted, b, a, side)):
        target[
            row_start + start : row_start + start + extent * extent, lane_start : lane_start + width
        ] = part


def dot(left, right):
    return lax.dot_general(left, right, (((1,), (0,)), ((), ())), preferred_element_type=F32)


def dot_last(left, right):
    return lax.dot_general(left, right, (((1,), (1,)), ((), ())), preferred_element_type=F32)


def block_of(index, extent):
    return (index // extent // 2) * (extent // 2) + (index % extent) // 2


def pool_matrix(extent, value):
    count = extent * extent
    shape = (count // 4, count)
    return jnp.where(block_of(iota(shape, 1), extent) == iota(shape, 0), value, 0.0).astype(BF16)


def spread_matrix(extent):
    count = extent * extent
    shape = (count, count // 4)
    return jnp.where(block_of(iota(shape, 0), extent) == iota(shape, 1), 1.0, 0.0).astype(BF16)


def spread(matrix, value):
    high = value.astype(BF16)
    low = (value - high.astype(F32)).astype(BF16)
    return dot(matrix, high) + dot(matrix, low)


def gelu_and_slope(z):
    root = 0.7978845608028654
    inner = root * (z + 0.044715 * z * z * z)
    t = jnp.tanh(inner)
    half = 0.5 * (1.0 + t)
    slope = half + 0.5 * z * (1.0 - t * t) * (root * (1.0 + 3 * 0.044715 * z * z))
    return z * half, slope


def head_cotangents(cot, coarse_cot, weights):
    return jnp.concatenate(
        [
            (weights[0:1] * cot).astype(BF16),
            (weights[1:2] * cot).astype(BF16),
            (weights[2:3] * coarse_cot).astype(BF16),
        ],
        axis=0,
    )


def copies(pairs, sems):
    made = [
        pltpu.make_async_copy(source, target, sems.at[num])
        for num, (source, target) in enumerate(pairs)
    ]
    for one in made:
        one.start()
    return made


def section_kernel(
    side,
    info,
    features,
    trunk_weight,
    head_weight,
    cotangent,
    gain,
    shift,
    scale,
    merging,
    own_out,
    send_out,
    slope_out,
    tap_grad_out,
    merged_out,
    small_out,
    feed,
    weights,
    heads,
    cot_ref,
    shifted,
    patch,
    sems,
):
    rows = rows_of(side)
    mid = (side // 2) ** 2
    fine = side * side
    coarse = (side // 4) ** 2
    channels = feed.shape[1]
    half = channels // 2
    width = heads.shape[2]
    core = info[1]
    made = copies(
        [(features.at[info[0]], feed)]
        + [
            (
                trunk_weight.at[num // 3, pl.ds(num % 3 * 3 * channels, 3 * channels)],
                weights.at[num],
            )
            for num in range(6)
        ]
        + [(cotangent.at[info[2]], cot_ref)]
        + [(head_weight.at[num], heads.at[num]) for num in range(2)],
        sems,
    )
    made[0].wait()

    def conv(value, layer):
        column_shifts(value, side, shifted)
        total = jnp.zeros((rows, channels), F32)
        for a in range(3):
            for b in range(3):
                put_row_shift(patch, 0, b * channels, shifted, b, a, side)
            made[1 + 3 * layer + a].wait()
            total = total + dot(patch[...], weights[3 * layer + a])
        return total

    def put_halves(first, value):
        count = value.shape[0]
        left = value[:, :half]
        right = value[:, half:]
        own_out[first : first + count, :] = jnp.where(core == 0, left, right)
        send_out[first : first + count, :] = jnp.where(core == 0, right, left)

    low_feed = feed[...]
    feed_value = low_feed.astype(F32)
    put_halves(0, low_feed)
    z1 = gain[0:1, :] * conv(feed_value, 0) + shift[0:1, :]
    act1, slope1 = gelu_and_slope(z1)
    slope_out[...] = slope1 * gain[0:1, :]
    low_act = act1.astype(BF16)
    put_halves(rows, low_act)
    z2 = gain[1:2, :] * conv(low_act.astype(F32), 1) + shift[1:2, :]
    trunk_out, slope2 = gelu_and_slope(z2)
    taps = [feed_value, trunk_out.astype(BF16).astype(F32)]

    made[7].wait()
    cot_low = cot_ref[...]
    cot = cot_low.astype(F32)
    coarse_cot = dot(pool_matrix(side // 2, 1.0), cot_low)
    pool = pool_matrix(side, 0.25)
    wide = spread_matrix(side)
    merged = jnp.zeros((mid, width), F32)
    coarse_merged = jnp.zeros((coarse, width), F32)
    scale_rows = []
    stacked = 2 * mid + coarse
    for k in range(2):
        tap = taps[k]
        scale_row = scale[k : k + 1, :]
        r = lax.rsqrt(jnp.mean(tap * tap, axis=-1, keepdims=True) + EPSILON)
        normed = (tap * r * scale_row).astype(BF16)
        pooled = dot(pool, normed[:fine]).astype(BF16)
        rows_k = jnp.concatenate([pooled, normed[fine:]], axis=0)
        put_halves(2 * rows + k * stacked, rows_k)
        made[8 + k].wait()
        product = dot(rows_k, heads[k])
        weights_k = merging[k]
        merged = merged + weights_k[0:1] * product[:mid] + weights_k[1:2] * product[mid : 2 * mid]
        coarse_merged = coarse_merged + weights_k[2:3] * product[2 * mid :]
        small_out[3 * k : 3 * k + 1, :] = jnp.sum(cot * product[:mid], axis=0, keepdims=True)
        small_out[3 * k + 1 : 3 * k + 2, :] = jnp.sum(
            cot * product[mid : 2 * mid], axis=0, keepdims=True
        )
        small_out[3 * k + 2 : 3 * k + 3, :] = jnp.sum(
            coarse_cot * product[2 * mid :], axis=0, keepdims=True
        )
        grads = head_cotangents(cot, coarse_cot, weights_k)
        back = dot_last(grads, heads[k])
        back = jnp.concatenate([spread(wide, 0.25 * back[:mid]), back[mid:]], axis=0)
        upstream = back * scale_row
        tap_grad = r * (
            upstream - tap * (r * r) * jnp.mean(upstream * tap, axis=-1, keepdims=True)
        )
        scale_rows.append(jnp.sum(back * tap * r, axis=0, keepdims=True))
        if k == 0:
            tap_grad_out[...] = tap_grad
    small_out[6:7, :] = jnp.concatenate(
        scale_rows + [jnp.zeros((1, width - 2 * channels), F32)], axis=1
    )
    small_out[7:8, :] = jnp.zeros((1, width), F32)
    merged = merged + spread(spread_matrix(side // 2), coarse_merged)
    merged_out[...] = merged.astype(BF16)
    grad2 = (tap_grad.astype(BF16).astype(F32) * slope2 * gain[1:2, :]).astype(BF16)
    first = 2 * rows + 2 * stacked
    for target in (own_out, send_out):
        target[first : first + rows, :] = grad2[:, :half]
        target[first + rows : first + 2 * rows, :] = grad2[:, half:]
        for num in range(width // half):
            target[first + 2 * rows + num * mid : first + 2 * rows + (num + 1) * mid, :] = cot_low[
                :, num * half : (num + 1) * half
            ]


def section(info, features, trunk_weight, head_weight, cotangent, gain, shift, scale, merging):
    side = SIDE
    rows = rows_of(side)
    channels = features.shape[2]
    half = channels // 2
    width = head_weight.shape[2]
    mid = cotangent.shape[1]
    sent = 2 * rows + 2 * (2 * mid + (side // 4) ** 2) + 2 * rows + width // half * mid
    vmem = spec(pltpu.VMEM)
    hbm = spec(pl.ANY)
    return pl.pallas_call(
        partial(section_kernel, side),
        out_shape=(
            jax.ShapeDtypeStruct((sent, half), BF16),
            jax.ShapeDtypeStruct((sent, half), BF16),
            jax.ShapeDtypeStruct((rows, channels), F32),
            jax.ShapeDtypeStruct((rows, channels), F32),
            jax.ShapeDtypeStruct((mid, width), BF16),
            jax.ShapeDtypeStruct((8, width), F32),
        ),
        in_specs=[spec(pltpu.SMEM), hbm, hbm, hbm, hbm, vmem, vmem, vmem, vmem],
        out_specs=(vmem,) * 6,
        scratch_shapes=[
            pltpu.VMEM((rows, channels), BF16),
            pltpu.VMEM((6, 3 * channels, channels), BF16),
            pltpu.VMEM((2, channels, width), BF16),
            pltpu.VMEM((mid, width), BF16),
            pltpu.VMEM((3, rows, channels), F32),
            pltpu.VMEM((rows, 3 * channels), BF16),
            pltpu.SemaphoreType.DMA((10,)),
        ],
        compiler_params=params(),
        name="section",
    )(info, features, trunk_weight, head_weight, cotangent, gain, shift, scale, merging)


def back_kernel(side, layer, grad, trunk_weight, factor, *rest):
    if layer == 0:
        pick, own_out, send_out, weights, shifted, patch, sems = rest
    else:
        grad_out, weights, shifted, patch, sems = rest
    channels = trunk_weight.shape[2]
    half = channels // 2
    rows = rows_of(side)
    made = copies(
        [
            (trunk_weight.at[layer, pl.ds(num * 3 * channels, 3 * channels)], weights.at[num])
            for num in range(3)
        ],
        sems,
    )
    value = jnp.concatenate([grad[:rows, :], grad[rows:, :]], axis=1).astype(F32)
    column_shifts(value, side, shifted)
    total = jnp.zeros((rows, channels), F32)
    for a in range(3):
        for b in range(3):
            put_row_shift(patch, 0, b * channels, shifted, 2 - b, 2 - a, side)
        made[a].wait()
        for b in range(3):
            total = total + dot_last(
                patch[:, b * channels : (b + 1) * channels],
                weights[a, b * channels : (b + 1) * channels, :],
            )
    if layer == 0:
        total = total + factor[...]
        left, right = total[:, :half], total[:, half:]
        own_out[...] = jnp.where(pick[0] == 0, left, right)
        send_out[...] = jnp.where(pick[0] == 0, right, left).astype(BF16)
    else:
        low = (total * factor[...]).astype(BF16)
        grad_out[:rows, :] = low[:, :half]
        grad_out[rows:, :] = low[:, half:]


def back(layer, grad, trunk_weight, factor, pick=None):
    side = SIDE
    rows = rows_of(side)
    channels = trunk_weight.shape[2]
    half = channels // 2
    vmem = spec(pltpu.VMEM)
    in_specs = [vmem, spec(pl.ANY), vmem]
    operands = [grad, trunk_weight, factor]
    if layer == 0:
        in_specs.append(spec(pltpu.SMEM))
        operands.append(pick)
        out_shape = (
            jax.ShapeDtypeStruct((rows, half), F32),
            jax.ShapeDtypeStruct((rows, half), BF16),
        )
        out_specs = (vmem, vmem)
    else:
        out_shape = jax.ShapeDtypeStruct((2 * rows, half), BF16)
        out_specs = vmem
    return pl.pallas_call(
        partial(back_kernel, side, layer),
        out_shape=out_shape,
        in_specs=in_specs,
        out_specs=out_specs,
        scratch_shapes=[
            pltpu.VMEM((3, 3 * channels, channels), BF16),
            pltpu.VMEM((3, rows, channels), F32),
            pltpu.VMEM((rows, 3 * channels), BF16),
            pltpu.SemaphoreType.DMA((3,)),
        ],
        compiler_params=params(),
        name="back",
    )(*operands)


def trunk_grad_kernel(
    side, parts, at_x, at_g, info, own_x, other_x, own_g, other_g, out, xs, gs, shifted, patch, sems
):
    rows = rows_of(side)
    half = xs.shape[1]
    first = at_g + info[0] * rows
    made = copies(
        [
            (own_g.at[pl.ds(first, rows)], gs.at[pl.ds(0, rows)]),
            (other_g.at[pl.ds(first, rows)], gs.at[pl.ds(rows, rows)]),
            (own_x.at[pl.ds(at_x, rows)], xs.at[pl.ds(0, rows)]),
            (other_x.at[pl.ds(at_x, rows)], xs.at[pl.ds(rows, rows)]),
        ],
        sems,
    )
    for image in range(2):
        made[image].wait()
        column_shifts(gs[image * rows : (image + 1) * rows, :].astype(F32), side, shifted)
        for a in range(3):
            for b in range(3):
                put_row_shift(
                    patch, image * rows, (3 * a + b) * half, shifted, 2 - b, 2 - a, side
                )
    made[2].wait()
    made[3].wait()
    turned = xs[...].T
    size = half // parts
    for offset in range(9):
        product = dot(turned, patch[:, offset * half : (offset + 1) * half]).astype(BF16)
        for lane in range(2):
            for part in range(parts):
                place = (lane * parts + part) ^ info[1]
                out[place, offset * size : (offset + 1) * size, :] = product[
                    part * size : (part + 1) * size, lane * (half // 2) : (lane + 1) * (half // 2)
                ]


def trunk_grad(blocks, at_x, at_g, pick, low_bits, own_x, other_x, own_g, other_g):
    side = SIDE
    rows = rows_of(side)
    half = own_x.shape[1]
    parts = blocks // 4
    hbm = spec(pl.ANY)
    return pl.pallas_call(
        partial(trunk_grad_kernel, side, parts, at_x, at_g),
        out_shape=jax.ShapeDtypeStruct((blocks // 2, 9 * (half // parts), half // 2), BF16),
        in_specs=[spec(pltpu.SMEM), hbm, hbm, hbm, hbm],
        out_specs=spec(pltpu.VMEM),
        scratch_shapes=[
            pltpu.VMEM((2 * rows, half), BF16),
            pltpu.VMEM((2 * rows, half), BF16),
            pltpu.VMEM((3, rows, half), F32),
            pltpu.VMEM((2 * rows, 9 * half), BF16),
            pltpu.SemaphoreType.DMA((4,)),
        ],
        compiler_params=params(),
        name="trunk_grad",
    )(jnp.stack([pick, low_bits]), own_x, other_x, own_g, other_g)


def head_grad_kernel(
    side, parts, at_n, at_c, info, own, other, merging, out, ns, cots, sems
):
    mid = (side // 2) ** 2
    stacked = 2 * mid + (side // 4) ** 2
    half = ns.shape[1]
    width = out.shape[2] * 2
    lanes = width // half
    pick = info[0]
    made = copies(
        [
            (source.at[pl.ds(at_c, lanes * mid)], cots.at[num])
            for num, source in enumerate((own, other))
        ]
        + [
            (
                source.at[pl.ds(at_n + pick * stacked, stacked)],
                ns.at[pl.ds(num * stacked, stacked)],
            )
            for num, source in enumerate((own, other))
        ],
        sems,
    )
    weights = merging[pick]
    sums = pool_matrix(side // 2, 1.0)
    grads = []
    for image in range(2):
        made[image].wait()
        cot_low = jnp.concatenate(
            [cots[image, num * mid : (num + 1) * mid, :] for num in range(lanes)], axis=1
        )
        grads.append(head_cotangents(cot_low.astype(F32), dot(sums, cot_low), weights))
    made[2].wait()
    made[3].wait()
    product = dot(ns[...].T, jnp.concatenate(grads, axis=0)).astype(BF16)
    size = half // parts
    for lane in range(2):
        for part in range(parts):
            place = (lane * parts + part) ^ info[1]
            out[place] = product[
                part * size : (part + 1) * size, lane * (width // 2) : (lane + 1) * (width // 2)
            ]


def head_grad(blocks, at_n, at_c, pick, low_bits, own, other, merging, mid):
    side = SIDE
    half = own.shape[1]
    width = merging.shape[2]
    parts = blocks // 4
    hbm = spec(pl.ANY)
    stacked = 2 * mid + (side // 4) ** 2
    return pl.pallas_call(
        partial(head_grad_kernel, side, parts, at_n, at_c),
        out_shape=jax.ShapeDtypeStruct((blocks // 2, half // parts, width // 2), BF16),
        in_specs=[spec(pltpu.SMEM), hbm, hbm, spec(pltpu.VMEM)],
        out_specs=spec(pltpu.VMEM),
        scratch_shapes=[
            pltpu.VMEM((2 * stacked, half), BF16),
            pltpu.VMEM((2, width // half * mid, half), BF16),
            pltpu.SemaphoreType.DMA((4,)),
        ],
        compiler_params=params(),
        name="head_grad",
    )(jnp.stack([pick, low_bits]), own, other, merging)


def widen_trunk_kernel(parts, place, own, other, *rest):
    out = rest[-1]
    size = out.shape[2] // parts

    def write(source, low):
        for part in range(parts):
            start = pl.multiple_of((part ^ low) * size, size)
            for offset in range(9):
                out[0, offset, pl.ds(start, size), :] = source[
                    part, offset * size : (offset + 1) * size, :
                ].astype(F32)

    @pl.when(pl.program_id(0) == 0)
    def _():
        write(own, place[2])

    @pl.when(pl.program_id(0) == 1)
    def _():
        write(other, place[5])


def widen_heads_kernel(parts, place, own, other, out):
    size = out.shape[1] // parts

    def write(source, low):
        for part in range(parts):
            start = pl.multiple_of((part ^ low) * size, size)
            out[0, pl.ds(start, size), :] = source[part].astype(F32)

    @pl.when(pl.program_id(0) == 0)
    def _():
        write(own, place[2])

    @pl.when(pl.program_id(0) == 1)
    def _():
        write(other, place[5])


def source_specs(parts, shape):
    return [
        pl.BlockSpec((parts,) + shape, lambda i, j, place: (jnp.where(i == 0, j, 3), 0, 0)),
        pl.BlockSpec((parts,) + shape, lambda i, j, place: (jnp.where(i == 1, j, 0), 0, 0)),
    ]


def widen_trunk(place, own, other, layer, layers, before):
    parts = own.shape[0] // 4
    lanes = own.shape[2]
    half = 2 * lanes
    operands = [place, own, other]
    in_specs = source_specs(parts, own.shape[1:])
    aliases = {}
    if before is not None:
        operands.append(before)
        in_specs.append(spec(pl.ANY))
        aliases = {3: 0}
    return pl.pallas_call(
        partial(widen_trunk_kernel, parts),
        grid_spec=pltpu.PrefetchScalarGridSpec(
            num_scalar_prefetch=1,
            grid=(2, 4),
            in_specs=in_specs,
            out_specs=pl.BlockSpec(
                (1, 9, half, lanes),
                lambda i, j, place: (layer, 0, place[3 * i], j ^ place[3 * i + 1]),
            ),
        ),
        out_shape=jax.ShapeDtypeStruct((layers, 9, 2 * half, 2 * half), F32),
        input_output_aliases=aliases,
        compiler_params=params(),
        name="widen_trunk",
    )(*operands)


def widen_heads(place, own, other):
    parts = own.shape[0] // 4
    size, lanes = own.shape[1:]
    half = size * parts
    return pl.pallas_call(
        partial(widen_heads_kernel, parts),
        grid_spec=pltpu.PrefetchScalarGridSpec(
            num_scalar_prefetch=1,
            grid=(2, 4),
            in_specs=source_specs(parts, own.shape[1:]),
            out_specs=pl.BlockSpec(
                (1, half, lanes),
                lambda i, j, place: (
                    (j ^ place[3 * i + 1]) // 2,
                    place[3 * i],
                    (j ^ place[3 * i + 1]) % 2,
                ),
            ),
        ),
        out_shape=jax.ShapeDtypeStruct((2, 2 * half, 2 * lanes), F32),
        compiler_params=params(),
        name="widen_heads",
    )(place, own, other)


def stage_bits(dp):
    size = dp.bit_length() - 1
    bits = [1, size] + list(range(2, size))
    stages = []
    for num in range(0, len(bits), 2):
        pair = bits[num : num + 2]
        stages += [tuple(pair), tuple(pair[::-1])] if len(pair) == 2 else [(pair[0], pair[0])]
    return stages


def swap_over(block, devices, bits):
    route = [(i, i ^ (1 << bits[i & 1])) for i in range(devices)]
    return lax.ppermute(block, AXES, route)


def summed(keep, received):
    return (keep.astype(F32) + received.astype(F32)).astype(BF16)


def body(
    features,
    plan,
    trunk_weight,
    trunk_gain,
    trunk_shift,
    head_weight,
    norm_scale,
    merging_weight,
    merged_cotangent,
):
    dp = lax.axis_size("dp")
    devices = lax.axis_size("pipe") * dp
    layers = trunk_weight.shape[0]
    channels = features.shape[2]
    rows = features.shape[1]
    half = channels // 2
    mid = merged_cotangent.shape[1]
    width = head_weight.shape[2]
    pipe = lax.axis_index("pipe")
    index = pipe * dp + lax.axis_index("dp")
    core = index & 1
    stages = stage_bits(dp)
    blocks = 1 << len(stages)

    def bits_of(which):
        total = 0
        for stage in stages:
            total = total * 2 + ((index >> stage[which]) & 1)
        return total

    own_bits = jnp.where(core == 0, bits_of(0), bits_of(1))
    other_bits = jnp.where(core == 0, bits_of(1), bits_of(0))
    top_bit = own_bits // (blocks // 2)
    low_bits = own_bits % (blocks // 2)
    parts = blocks // 4
    place = jnp.stack(
        [core, own_bits // parts, own_bits % parts, 1 - core, other_bits // parts, other_bits % parts]
    )
    weights = trunk_weight.reshape(layers, 9 * channels, channels)
    slot = plan[0, pipe]

    own, send, slope, tap_grad, merged, small = section(
        jnp.stack([slot, core, pipe]),
        features,
        weights,
        head_weight,
        merged_cotangent,
        trunk_gain,
        trunk_shift,
        norm_scale,
        merging_weight,
    )
    other = swap_over(send, devices, (0, 0))
    at_n = 2 * rows
    stacked = 2 * mid + (SIDE // 4) ** 2
    at_g = at_n + 2 * stacked
    at_c = at_g + 2 * rows

    def first_stage(make):
        return make(1 - top_bit), make(top_bit)

    def scatter(send, keep):
        received = swap_over(send, devices, stages[0])
        for stage in stages[1:]:
            count = keep.shape[0] // 2
            total = summed(keep, received)
            keep = total[:count]
            received = swap_over(total[count:], devices, stage)
        return summed(keep, received)

    def gather(block):
        for stage in reversed(stages):
            block = jnp.concatenate([block, swap_over(block, devices, stage)], axis=0)
        return block, swap_over(block, devices, (0, 0))

    head_parts = first_stage(
        lambda pick: head_grad(
            blocks, at_n, at_c, pick, low_bits, own, other, merging_weight, mid
        )
    )
    last_parts = first_stage(
        lambda pick: trunk_grad(blocks, rows, at_g, pick, low_bits, own, other, own, other)
    )
    grad1 = back(1, lax.slice_in_dim(own, at_g, at_g + 2 * rows), weights, slope)
    other_grad1 = swap_over(grad1, devices, (0, 0))
    first_parts = first_stage(
        lambda pick: trunk_grad(blocks, 0, 0, pick, low_bits, own, other, grad1, other_grad1)
    )
    own_feed, sent_feed = back(0, grad1, weights, tap_grad, pipe[None])

    heads = gather(scatter(*head_parts))
    last = gather(scatter(*last_parts))
    first = gather(scatter(*first_parts))

    small_all = lax.all_gather(small, AXES, axis=0, tiled=False)
    small_sum = jnp.sum(small_all, axis=0)

    trunk_out = widen_trunk(place, *last, 1, layers, None)
    trunk_out = widen_trunk(place, *first, 0, layers, trunk_out)
    head_out = widen_heads(place, *heads)

    over_pipe = [(0, 1), (1, 0)]
    left, right = merged[:, : width // 2], merged[:, width // 2 :]
    own_merged = jnp.where(pipe == 0, left, right)
    other_merged = lax.ppermute(jnp.where(pipe == 0, right, left), "pipe", over_pipe)
    other_feed = lax.ppermute(sent_feed, "pipe", over_pipe).astype(F32)

    def in_order(is_first, one, two):
        return jnp.where(is_first, jnp.stack([one, two]), jnp.stack([two, one]))

    return (
        in_order(pipe == 0, own_merged, other_merged),
        in_order(slot == 0, own_feed, other_feed),
        trunk_out.reshape(trunk_weight.shape),
        head_out,
        small_sum[6, : 2 * channels].reshape(2, channels),
        small_sum[:6].reshape(2, 3, width),
    )


def solution(mesh):
    placed = (P("dp", None, None), P("dp", None), P(), P(), P(), P(), P(), P(), P("dp", None, None))
    return jax.shard_map(
        body,
        mesh=mesh,
        in_specs=placed,
        out_specs=(P("dp", None, "pipe"), P("dp", None, "pipe"), P(), P(), P(), P()),
        check_vma=False,
    )
```

time: 837 us -> 255 us (0.30)
  waiting for transfers between devices: 403 us -> 92.1 us
  matrix products: 128 us -> 0 us
  blocking collectives: 82.9 us -> 0 us
  local copies, waits for them, and re-layouts: 81.9 us -> 16.9 us
  Pallas kernels: 0 us -> 59.1 us
  loops' own time: 35.3 us -> 0 us
  other arithmetic: 46.3 us -> 17.8 us
  starting transfers between devices: 38 us -> 53.3 us
    reduce_scatter x3 -> x0, waiting for transfers between devices: 254 us -> none  [the longest x1 211 us: body(): lax.psum_scatter(trunk_rows, ('pipe', 'dp'), scatter_dimension=0, tiled=T...]
    dot_general x48 -> x0, matrix products: 128 us -> none  [the longest x12 36.1 us: trunk_backward(): jnp.dot(unfolded, weights[layer_num], preferred_element_type=jnp.float32)]
    all_gather x2 -> x1, waiting for transfers between devices: 125 us -> 0.01 us  [body(): small_all = lax.all_gather(small, AXES, axis=0, tiled=False)]
    unnamed x2 -> x0, blocking collectives: 82.9 us -> none
    ppermute x5 -> x31, waiting for transfers between devices: 23.4 us -> 92.1 us  [the longest x29 89.6 us: swap_over(): return lax.ppermute(block, AXES, route)]
    pallas_call x0 -> x12, Pallas kernels: none -> 59.1 us  [the longest x2 17.2 us: widen_trunk(): pl.pallas_call(partial(widen_trunk_kernel, parts), grid_spec=pltpu.Prefet...]
    another operation x6 -> x0, loops' own time: 35.3 us -> none  [run_tick(): lax.cond(section_index == 0, first_section, second_section, carried)]
    add x23 -> x0, other arithmetic: 24.6 us -> none  [the longest x1 20.5 us: first_section(): trunk_grad = trunk_grad + weight_part]
  transfers between devices with their start and end apart: 10 -> 32, of which waited for: 6 -> 17; matrix products, arithmetic and copies ran while one was open for 23% -> 11% of each run, Pallas kernels for 0% -> 14%
where the time goes in v1:
time: 255 us; the launch traced here: 254 us
  waiting for transfers between devices  92.1 us (36%)
  Pallas kernels  59.1 us (23%)
  starting transfers between devices  53.3 us (21%)
  other arithmetic  17.8 us (7%)
  local copies, waits for them, and re-layouts  16.9 us (7%)
  between operations  14.4 us (6%)
    ppermute x29, waiting for transfers between devices, swap_over(): return lax.ppermute(block, AXES, route)  89.6 us
    ppermute x29, starting transfers between devices, swap_over(): return lax.ppermute(block, AXES, route)  51.2 us
    pallas_call x2, Pallas kernels, widen_trunk(): pl.pallas_call(partial(widen_trunk_kernel, parts), grid_spec=pltpu.Prefet...  17.2 us
    unnamed x31, local copies, waits for them, and re-layouts  13.6 us
    pallas_call x1, Pallas kernels, section(): pl.pallas_call(partial(section_kernel, side), out_shape=(jax.ShapeDtypeSt...  11.7 us
    pallas_call x4, Pallas kernels, trunk_grad(): pl.pallas_call(partial(trunk_grad_kernel, side, parts, at_x, at_g), out_s...  11.3 us
    pallas_call x1, Pallas kernels, widen_heads(): pl.pallas_call(partial(widen_heads_kernel, parts), grid_spec=pltpu.Prefet...  7.22 us
    concatenate x9, other arithmetic, gather(): block = jnp.concatenate([block, swap_over(block, devices, stage)], axis=0)  7.03 us
  transfers between devices with their start and end apart: 32, of which 17 were waited for; matrix products, arithmetic and copies ran while one was open for 11% of the time, Pallas kernels for 14%

profile of v1, /device:TPU:0, one launch (start us, length us, event | category | flops | bytes accessed | tf_op | source)
XLA Modules:
  0.0 253.5 jit_solution(14070490113031643914)
XLA Ops:
  14.3 11.7 %section.1 = (bf16[2080,256]{1,0:T(8,128)(2,1)S(1)}, bf16[2080,256]{1,0:T(8,128)(2,1)}, f32[336,512]{1,0:T(8,128)S(1)}, f32[336,512]{1,0:T(8,128)S(1)}, bf16[64,1792]{1,0:T(8,128)(2,1)S(1)}, /*index=5*/f32[8,1792]{1,0:T(8,128)}) custom-call(s32[3]{0:T(128)S(1)} %pad_add_fusion.info, bf16[2,336,512]{2,1,0:T(8,128)(2,1)S(1)} %copy-done, ...), custom_call_target="tpu_custom_call" | custom-call | tf_op jit(solution)/shard_map/section/pallas_call | solution.py:299
  26.6 3.4 %back.2.grad.own_g = bf16[672,256]{1,0:T(8,128)(2,1)S(1)} custom-call(bf16[672,256]{1,0:T(8,128)(2,1)S(1)} %slice.71.grad, bf16[2,4608,512]{2,1,0:T(8,128)(2,1)} %bitcast.26, f32[336,512]{1,0:T(8,128)S(1)} %get-tuple-element.16.factor), custom_call_target="tpu_custom_call" | custom-call | tf_op jit(solution)/shard_map/back/pallas_call | solution.py:382
  31.7 2.8 %trunk_grad.5 = bf16[8,576,128]{2,1,0:T(8,128)(2,1)S(1)} custom-call(s32[2]{0:T(128)S(1)} %pad_add_fusion.2.info, bf16[2080,256]{1,0:T(8,128)(2,1)S(1)} %get-tuple-element.15.own_x.own_g.own, bf16[2080,256]{1,0:T(8,128)(2,1)S(1)} %collective-permute-done.2.other_x.other_g.other, bf16[672,256]{1,0:T(8,128)(2,1)S(1)} %back.2.grad.own_g, ...), custom_call_target="tpu_custom_call" | custom-call | tf_op jit(solution)/shard_map/trunk_grad/pallas_call | solution.py:441
  34.5 2.7 %collective-permute-start.4 = (bf16[8,576,128]{2,1,0:T(8,128)(2,1)S(1)}, bf16[8,576,128]{2,1,0:T(8,128)(2,1)S(1)}, u32[]{:S(2)}, u32[]{:S(2)}) collective-permute-start(bf16[8,576,128]{2,1,0:T(8,128)(2,1)S(1)} %trunk_grad.5), channel_id=1, source_target_pairs={{0,2},{1,17},{2,0},{3,19},{4,6},{5,21},{6,4},{7,23},{8,10},{9,25},... | collective-permute-start | bytes 3538952 | tf_op jit(solution)/shard_map/ppermute | solution.py:635
  37.2 2.8 %trunk_grad.7 = bf16[8,576,128]{2,1,0:T(8,128)(2,1)S(1)} custom-call(s32[2]{0:T(128)S(1)} %pad_add_fusion.2.info, bf16[2080,256]{1,0:T(8,128)(2,1)S(1)} %get-tuple-element.15.own_x.own_g.own, bf16[2080,256]{1,0:T(8,128)(2,1)S(1)} %collective-permute-done.2.other_x.other_g.other, bf16[2080,256]{1,0:T(8,128)(2,1)S(1)} %get-tuple-element.15.own_x.own_g.own, ...), custom_call_target="tpu_custom_call" | custom-call | tf_op jit(solution)/shard_map/trunk_grad/pallas_call | solution.py:441
  40.1 2.4 head_grad.3
  42.5 2.1 collective-permute-start.22
  44.6 3.0 %trunk_grad.4 = bf16[8,576,128]{2,1,0:T(8,128)(2,1)S(1)} custom-call(s32[2]{0:T(128)S(1)} %pad_add_fusion.1.info, bf16[2080,256]{1,0:T(8,128)(2,1)S(1)} %get-tuple-element.15.own_x.own_g.own, bf16[2080,256]{1,0:T(8,128)(2,1)S(1)} %collective-permute-done.2.other_x.other_g.other, bf16[672,256]{1,0:T(8,128)(2,1)S(1)} %back.2.grad.own_g, ...), custom_call_target="tpu_custom_call" | custom-call | tf_op jit(solution)/shard_map/trunk_grad/pallas_call | solution.py:441
  47.6 2.8 %trunk_grad.6 = bf16[8,576,128]{2,1,0:T(8,128)(2,1)S(1)} custom-call(s32[2]{0:T(128)S(1)} %pad_add_fusion.1.info, bf16[2080,256]{1,0:T(8,128)(2,1)S(1)} %get-tuple-element.15.own_x.own_g.own, bf16[2080,256]{1,0:T(8,128)(2,1)S(1)} %collective-permute-done.2.other_x.other_g.other, bf16[2080,256]{1,0:T(8,128)(2,1)S(1)} %get-tuple-element.15.own_x.own_g.own, ...), custom_call_target="tpu_custom_call" | custom-call | tf_op jit(solution)/shard_map/trunk_grad/pallas_call | solution.py:441
  51.7 2.1 collective-permute-start.5
  53.9 16.5 %collective-permute-done.13 = bf16[8,576,128]{2,1,0:T(8,128)(2,1)S(1)} collective-permute-done((bf16[8,576,128]{2,1,0:T(8,128)(2,1)S(1)}, bf16[8,576,128]{2,1,0:T(8,128)(2,1)S(1)}, u32[]{:S(2)}, u32[]{:S(2)}) %collective-permute-start.13) | collective-permute-done | bytes 1179680 | tf_op jit(solution)/shard_map/ppermute | solution.py:635
  70.7 2.1 collective-permute-start.14
  72.8 2.4 head_grad.2
  75.2 11.3 %collective-permute-done.22 = bf16[8,64,896]{2,1,0:T(8,128)(2,1)S(1)} collective-permute-done((bf16[8,64,896]{2,1,0:T(8,128)(2,1)S(1)}, bf16[8,64,896]{2,1,0:T(8,128)(2,1)S(1)}, u32[]{:S(2)}, u32[]{:S(2)}) %collective-permute-start.22) | collective-permute-done | bytes 917536 | tf_op jit(solution)/shard_map/ppermute | solution.py:635
  86.8 2.1 collective-permute-start.23
  89.1 1.6 collective-permute-start.6
  91.5 3.9 %collective-permute-done.23 = bf16[4,64,896]{2,1,0:T(8,128)(2,1)S(1)} collective-permute-done((bf16[4,64,896]{2,1,0:T(8,128)(2,1)S(1)}, bf16[4,64,896]{2,1,0:T(8,128)(2,1)S(1)}, u32[]{:S(2)}, u32[]{:S(2)}) %collective-permute-start.23) | collective-permute-done | bytes 458784 | tf_op jit(solution)/shard_map/ppermute | solution.py:635
  95.5 2.1 collective-permute-start.24
  98.3 3.6 %collective-permute-start.7 = (bf16[1,576,128]{2,1,0:T(8,128)(2,1)S(1)}, bf16[1,576,128]{2,1,0:T(8,128)(2,1)S(1)}, u32[]{:S(2)}, u32[]{:S(2)}) collective-permute-start(bf16[1,576,128]{2,1,0:T(8,128)(2,1)S(1)} %slice.97), channel_id=1, source_target_pairs={{0,8},{1,5},{2,10},{3,7},{4,12},{5,1},{6,14},{7,3},{8,0},{9,13},{1... | collective-permute-start | bytes 442376 | tf_op jit(solution)/shard_map/ppermute | solution.py:635
  101.9 2.7 %collective-permute-done.15 = bf16[2,576,128]{2,1,0:T(8,128)(2,1)S(1)} collective-permute-done((bf16[2,576,128]{2,1,0:T(8,128)(2,1)S(1)}, bf16[2,576,128]{2,1,0:T(8,128)(2,1)S(1)}, u32[]{:S(2)}, u32[]{:S(2)}) %collective-permute-start.15) | collective-permute-done | bytes 294944 | tf_op jit(solution)/shard_map/ppermute | solution.py:635
  104.7 8.4 %collective-permute-start.16 = (bf16[1,576,128]{2,1,0:T(8,128)(2,1)S(1)}, bf16[1,576,128]{2,1,0:T(8,128)(2,1)S(1)}, u32[]{:S(2)}, u32[]{:S(2)}) collective-permute-start(bf16[1,576,128]{2,1,0:T(8,128)(2,1)S(1)} %slice.103), channel_id=1, source_target_pairs={{0,8},{1,5},{2,10},{3,7},{4,12},{5,1},{6,14},{7,3},{8,0},{9,13},{1... | collective-permute-start | bytes 442376 | tf_op jit(solution)/shard_map/ppermute | solution.py:635
  113.8 2.6 %collective-permute-start.8 = (bf16[1,576,128]{2,1,0:T(8,128)(2,1)S(1)}, bf16[1,576,128]{2,1,0:T(8,128)(2,1)S(1)}, u32[]{:S(2)}, u32[]{:S(2)}) collective-permute-start(bf16[1,576,128]{2,1,0:T(8,128)(2,1)S(1)} %get-tuple-element.33), channel_id=1, source_target_pairs={{0,8},{1,5},{2,10},{3,7},{4,12},{5,1},{6,14},{7,3},{8,0},{9,13},{1... | collective-permute-start | bytes 442376 | tf_op jit(solution)/shard_map/ppermute | solution.py:635
  117.1 3.1 %collective-permute-start.17 = (bf16[1,576,128]{2,1,0:T(8,128)(2,1)S(1)}, bf16[1,576,128]{2,1,0:T(8,128)(2,1)S(1)}, u32[]{:S(2)}, u32[]{:S(2)}) collective-permute-start(bf16[1,576,128]{2,1,0:T(8,128)(2,1)S(1)} %get-tuple-element.31), channel_id=1, source_target_pairs={{0,8},{1,5},{2,10},{3,7},{4,12},{5,1},{6,14},{7,3},{8,0},{9,13},{1... | collective-permute-start | bytes 442376 | tf_op jit(solution)/shard_map/ppermute | solution.py:635
  120.4 13.2 %collective-permute-done.17 = bf16[1,576,128]{2,1,0:T(8,128)(2,1)S(1)} collective-permute-done((bf16[1,576,128]{2,1,0:T(8,128)(2,1)S(1)}, bf16[1,576,128]{2,1,0:T(8,128)(2,1)S(1)}, u32[]{:S(2)}, u32[]{:S(2)}) %collective-permute-start.17) | collective-permute-done | bytes 147488 | tf_op jit(solution)/shard_map/ppermute | solution.py:635
  136.1 2.6 %collective-permute-start.26 = (bf16[1,64,896]{2,1,0:T(8,128)(2,1)S(1)}, bf16[1,64,896]{2,1,0:T(8,128)(2,1)S(1)}, u32[]{:S(2)}, u32[]{:S(2)}) collective-permute-start(bf16[1,64,896]{2,1,0:T(8,128)(2,1)S(1)} %get-tuple-element.29), channel_id=1, source_target_pairs={{0,8},{1,5},{2,10},{3,7},{4,12},{5,1},{6,14},{7,3},{8,0},{9,13},{1... | collective-permute-start | bytes 344072 | tf_op jit(solution)/shard_map/ppermute | solution.py:635
  138.7 6.5 %collective-permute-done.18 = bf16[2,576,128]{2,1,0:T(8,128)(2,1)S(1)} collective-permute-done((bf16[2,576,128]{2,1,0:T(8,128)(2,1)S(1)}, bf16[2,576,128]{2,1,0:T(8,128)(2,1)S(1)}, u32[]{:S(2)}, u32[]{:S(2)}) %collective-permute-start.18) | collective-permute-done | bytes 294944 | tf_op jit(solution)/shard_map/ppermute | solution.py:635
  146.7 2.2 collective-permute-done.9
  150.7 6.3 %collective-permute-done.27 = bf16[2,64,896]{2,1,0:T(8,128)(2,1)} collective-permute-done((bf16[2,64,896]{2,1,0:T(8,128)(2,1)}, bf16[2,64,896]{2,1,0:T(8,128)(2,1)}, u32[]{:S(2)}, u32[]{:S(2)}) %collective-permute-start.27) | collective-permute-done | bytes 229408 | tf_op jit(solution)/shard_map/ppermute | solution.py:635
  158.1 2.0 collective-permute-start.28
  162.4 4.8 %collective-permute-done.10 = bf16[4,576,128]{2,1,0:T(8,128)(2,1)} collective-permute-done((bf16[4,576,128]{2,1,0:T(8,128)(2,1)}, bf16[4,576,128]{2,1,0:T(8,128)(2,1)}, u32[]{:S(2)}, u32[]{:S(2)}) %collective-permute-start.10) | collective-permute-done | bytes 589856 | tf_op jit(solution)/shard_map/ppermute | solution.py:635
  168.4 2.5 collective-permute-start.11
  172.2 4.7 %collective-permute-done.28 = bf16[4,64,896]{2,1,0:T(8,128)(2,1)S(1)} collective-permute-done((bf16[4,64,896]{2,1,0:T(8,128)(2,1)S(1)}, bf16[4,64,896]{2,1,0:T(8,128)(2,1)S(1)}, u32[]{:S(2)}, u32[]{:S(2)}) %collective-permute-start.28) | collective-permute-done | bytes 458784 | tf_op jit(solution)/shard_map/ppermute | solution.py:635
  178.0 2.5 collective-permute-start.29
  182.0 2.0 constant_dynamic-update-slice_fusion.1
  184.0 1.9 constant_dynamic-update-slice_fusion.6
  187.0 5.2 %collective-permute-done.11 = bf16[8,576,128]{2,1,0:T(8,128)(2,1)S(1)} collective-permute-done((bf16[8,576,128]{2,1,0:T(8,128)(2,1)S(1)}, bf16[8,576,128]{2,1,0:T(8,128)(2,1)S(1)}, u32[]{:S(2)}, u32[]{:S(2)}) %collective-permute-start.11) | collective-permute-done | bytes 1179680 | tf_op jit(solution)/shard_map/ppermute | solution.py:635
  193.3 1.9 collective-permute-start.12
  196.4 8.9 %collective-permute-done.29 = bf16[8,64,896]{2,1,0:T(8,128)(2,1)S(1)} collective-permute-done((bf16[8,64,896]{2,1,0:T(8,128)(2,1)S(1)}, bf16[8,64,896]{2,1,0:T(8,128)(2,1)S(1)}, u32[]{:S(2)}, u32[]{:S(2)}) %collective-permute-start.29) | collective-permute-done | bytes 917536 | tf_op jit(solution)/shard_map/ppermute | solution.py:635
  205.5 1.8 collective-permute-start.30
  208.3 3.5 %back.3 = (f32[336,256]{1,0:T(8,128)S(1)}, bf16[336,256]{1,0:T(8,128)(2,1)S(1)}) custom-call(bf16[672,256]{1,0:T(8,128)(2,1)S(1)} %back.2.grad.own_g, bf16[2,4608,512]{2,1,0:T(8,128)(2,1)} %bitcast.27, f32[336,512]{1,0:T(8,128)S(1)} %copy-done.2, s32[1]{0:T(128)} %bitcast.2.rest_0_), custom_call_target="tpu_custom_call" | custom-call | tf_op jit(solution)/shard_map/back/pallas_call | solution.py:382
  211.7 1.8 collective-permute-start.1
  213.6 1.7 maximum_select_fusion.1
  215.3 2.5 collective-permute-done.1
  217.8 1.6 maximum_select_fusion
  219.4 1.6 bitcast_reduce_fusion
  222.3 7.2 %widen_heads.1 = f32[2,512,1792]{2,1,0:T(8,128)} custom-call(s32[6]{0:T(128)S(1)} %stack.104.place, bf16[16,64,896]{2,1,0:T(8,128)(2,1)S(1)} %constant_dynamic-update-slice_fusion.10.own, bf16[16,64,896]{2,1,0:T(8,128)(2,1)} %collective-permute-done.30.other), custom_call_target="tpu_custom_call" | custom-call | tf_op jit(solution)/shard_map/widen_heads/pallas_call | solution.py:602
  229.5 8.6 %widen_trunk.2.rest_0_ = f32[2,9,512,512]{3,2,1,0:T(8,128)} custom-call(s32[6]{0:T(128)S(1)} %stack.104.place, bf16[16,576,128]{2,1,0:T(8,128)(2,1)} %constant_dynamic-update-slice_fusion.5.own, bf16[16,576,128]{2,1,0:T(8,128)(2,1)} %collective-permute-done.21.other), custom_call_target="tpu_custom_call" | custom-call | tf_op jit(solution)/shard_map/widen_trunk/pallas_call | solution.py:580
  238.1 8.6 %widen_trunk.3 = f32[2,9,512,512]{3,2,1,0:T(8,128)} custom-call(s32[6]{0:T(128)S(1)} %stack.104.place, bf16[16,576,128]{2,1,0:T(8,128)(2,1)} %constant_dynamic-update-slice_fusion.own, bf16[16,576,128]{2,1,0:T(8,128)(2,1)} %collective-permute-done.12.other, f32[2,9,512,512]{3,2,1,0:T(8,128)} %widen_trunk.2.rest_0_), custom_call_target="tpu_custom_call", output_to_operand_aliasing={{}: (3, {})} | custom-call | tf_op jit(solution)/shard_map/widen_trunk/pallas_call | solution.py:580
  (107 shorter events, 34.9 us)
Async XLA Ops:
  7.2 212.3 %all-gather.3.cloned.1.call-start = ((), (), s32[]{:S(2)}) async-start(), calls=%async_computation | async-start | bytes 1892352 | tf_op jit(solution)/shard_map/all_gather | solution.py:737
  10.1 1.1 copy-start
  11.2 1.0 copy-start.3
  12.2 0.7 copy-start.4
  12.9 0.7 copy-start.5
  13.6 0.7 copy-start.6
  26.0 4.0 %copy-start.1 = (f32[336,512]{1,0:T(8,128)}, f32[336,512]{1,0:T(8,128)S(1)}, u32[]{:S(2)}) copy-start(f32[336,512]{1,0:T(8,128)S(1)} %get-tuple-element.17.factor) | copy-start | bytes 2064388
  26.0 5.7 %collective-permute-start.2 = (bf16[2080,256]{1,0:T(8,128)(2,1)}, bf16[2080,256]{1,0:T(8,128)(2,1)S(1)}, u32[]{:S(2)}, u32[]{:S(2)}) collective-permute-start(bf16[2080,256]{1,0:T(8,128)(2,1)} %get-tuple-element.20), channel_id=1, source_target_pairs={{0,1},{1,0},{2,3},{3,2},{4,5},{5,4},{6,7},{7,6},{8,9},{9,8},{10,11... | collective-permute-start | bytes 3194888 | tf_op jit(solution)/shard_map/ppermute | solution.py:635
  30.0 1.7 collective-permute-start.3
  34.5 16.9 %collective-permute-start.4 = (bf16[8,576,128]{2,1,0:T(8,128)(2,1)S(1)}, bf16[8,576,128]{2,1,0:T(8,128)(2,1)S(1)}, u32[]{:S(2)}, u32[]{:S(2)}) collective-permute-start(bf16[8,576,128]{2,1,0:T(8,128)(2,1)S(1)} %trunk_grad.5), channel_id=1, source_target_pairs={{0,2},{1,17},{2,0},{3,19},{4,6},{5,21},{6,4},{7,23},{8,10},{9,25},... | collective-permute-start | bytes 3538952 | tf_op jit(solution)/shard_map/ppermute | solution.py:635
  40.0 30.4 %collective-permute-start.13 = (bf16[8,576,128]{2,1,0:T(8,128)(2,1)S(1)}, bf16[8,576,128]{2,1,0:T(8,128)(2,1)S(1)}, u32[]{:S(2)}, u32[]{:S(2)}) collective-permute-start(bf16[8,576,128]{2,1,0:T(8,128)(2,1)S(1)} %trunk_grad.7), channel_id=1, source_target_pairs={{0,2},{1,17},{2,0},{3,19},{4,6},{5,21},{6,4},{7,23},{8,10},{9,25},... | collective-permute-start | bytes 3538952 | tf_op jit(solution)/shard_map/ppermute | solution.py:635
  42.5 44.0 %collective-permute-start.22 = (bf16[8,64,896]{2,1,0:T(8,128)(2,1)S(1)}, bf16[8,64,896]{2,1,0:T(8,128)(2,1)S(1)}, u32[]{:S(2)}, u32[]{:S(2)}) collective-permute-start(bf16[8,64,896]{2,1,0:T(8,128)(2,1)S(1)} %head_grad.3), channel_id=1, source_target_pairs={{0,2},{1,17},{2,0},{3,19},{4,6},{5,21},{6,4},{7,23},{8,10},{9,25},... | collective-permute-start | bytes 2752520 | tf_op jit(solution)/shard_map/ppermute | solution.py:635
  51.7 37.2 %collective-permute-start.5 = (bf16[4,576,128]{2,1,0:T(8,128)(2,1)S(1)}, bf16[4,576,128]{2,1,0:T(8,128)(2,1)S(1)}, u32[]{:S(2)}, u32[]{:S(2)}) collective-permute-start(bf16[4,576,128]{2,1,0:T(8,128)(2,1)S(1)} %slice.93), channel_id=1, source_target_pairs={{0,16},{1,3},{2,18},{3,1},{4,20},{5,7},{6,22},{7,5},{8,24},{9,11},... | collective-permute-start | bytes 1769480 | tf_op jit(solution)/shard_map/ppermute | solution.py:635
  70.7 20.0 %collective-permute-start.14 = (bf16[4,576,128]{2,1,0:T(8,128)(2,1)S(1)}, bf16[4,576,128]{2,1,0:T(8,128)(2,1)S(1)}, u32[]{:S(2)}, u32[]{:S(2)}) collective-permute-start(bf16[4,576,128]{2,1,0:T(8,128)(2,1)S(1)} %slice.99), channel_id=1, source_target_pairs={{0,16},{1,3},{2,18},{3,1},{4,20},{5,7},{6,22},{7,5},{8,24},{9,11},... | collective-permute-start | bytes 1769480 | tf_op jit(solution)/shard_map/ppermute | solution.py:635
  86.8 8.6 %collective-permute-start.23 = (bf16[4,64,896]{2,1,0:T(8,128)(2,1)S(1)}, bf16[4,64,896]{2,1,0:T(8,128)(2,1)S(1)}, u32[]{:S(2)}, u32[]{:S(2)}) collective-permute-start(bf16[4,64,896]{2,1,0:T(8,128)(2,1)S(1)} %slice.105), channel_id=1, source_target_pairs={{0,16},{1,3},{2,18},{3,1},{4,20},{5,7},{6,22},{7,5},{8,24},{9,11},... | collective-permute-start | bytes 1376264 | tf_op jit(solution)/shard_map/ppermute | solution.py:635
  89.1 9.1 %collective-permute-start.6 = (bf16[2,576,128]{2,1,0:T(8,128)(2,1)S(1)}, bf16[2,576,128]{2,1,0:T(8,128)(2,1)S(1)}, u32[]{:S(2)}, u32[]{:S(2)}) collective-permute-start(bf16[2,576,128]{2,1,0:T(8,128)(2,1)S(1)} %slice.95), channel_id=1, source_target_pairs={{0,4},{1,9},{2,6},{3,11},{4,0},{5,13},{6,2},{7,15},{8,12},{9,1},{1... | collective-permute-start | bytes 884744 | tf_op jit(solution)/shard_map/ppermute | solution.py:635
  90.9 13.6 %collective-permute-start.15 = (bf16[2,576,128]{2,1,0:T(8,128)(2,1)S(1)}, bf16[2,576,128]{2,1,0:T(8,128)(2,1)S(1)}, u32[]{:S(2)}, u32[]{:S(2)}) collective-permute-start(bf16[2,576,128]{2,1,0:T(8,128)(2,1)S(1)} %slice.101), channel_id=1, source_target_pairs={{0,4},{1,9},{2,6},{3,11},{4,0},{5,13},{6,2},{7,15},{8,12},{9,1},{1... | collective-permute-start | bytes 884744 | tf_op jit(solution)/shard_map/ppermute | solution.py:635
  95.5 24.7 %collective-permute-start.24 = (bf16[2,64,896]{2,1,0:T(8,128)(2,1)S(1)}, bf16[2,64,896]{2,1,0:T(8,128)(2,1)S(1)}, u32[]{:S(2)}, u32[]{:S(2)}) collective-permute-start(bf16[2,64,896]{2,1,0:T(8,128)(2,1)S(1)} %slice.107), channel_id=1, source_target_pairs={{0,4},{1,9},{2,6},{3,11},{4,0},{5,13},{6,2},{7,15},{8,12},{9,1},{1... | collective-permute-start | bytes 688136 | tf_op jit(solution)/shard_map/ppermute | solution.py:635
  98.3 14.7 %collective-permute-start.7 = (bf16[1,576,128]{2,1,0:T(8,128)(2,1)S(1)}, bf16[1,576,128]{2,1,0:T(8,128)(2,1)S(1)}, u32[]{:S(2)}, u32[]{:S(2)}) collective-permute-start(bf16[1,576,128]{2,1,0:T(8,128)(2,1)S(1)} %slice.97), channel_id=1, source_target_pairs={{0,8},{1,5},{2,10},{3,7},{4,12},{5,1},{6,14},{7,3},{8,0},{9,13},{1... | collective-permute-start | bytes 442376 | tf_op jit(solution)/shard_map/ppermute | solution.py:635
  104.7 11.7 %collective-permute-start.16 = (bf16[1,576,128]{2,1,0:T(8,128)(2,1)S(1)}, bf16[1,576,128]{2,1,0:T(8,128)(2,1)S(1)}, u32[]{:S(2)}, u32[]{:S(2)}) collective-permute-start(bf16[1,576,128]{2,1,0:T(8,128)(2,1)S(1)} %slice.103), channel_id=1, source_target_pairs={{0,8},{1,5},{2,10},{3,7},{4,12},{5,1},{6,14},{7,3},{8,0},{9,13},{1... | collective-permute-start | bytes 442376 | tf_op jit(solution)/shard_map/ppermute | solution.py:635
  113.8 21.3 %collective-permute-start.8 = (bf16[1,576,128]{2,1,0:T(8,128)(2,1)S(1)}, bf16[1,576,128]{2,1,0:T(8,128)(2,1)S(1)}, u32[]{:S(2)}, u32[]{:S(2)}) collective-permute-start(bf16[1,576,128]{2,1,0:T(8,128)(2,1)S(1)} %get-tuple-element.33), channel_id=1, source_target_pairs={{0,8},{1,5},{2,10},{3,7},{4,12},{5,1},{6,14},{7,3},{8,0},{9,13},{1... | collective-permute-start | bytes 442376 | tf_op jit(solution)/shard_map/ppermute | solution.py:635
  117.1 29.0 %copy-start.7 = (bf16[1,576,128]{2,1,0:T(8,128)(2,1)}, bf16[1,576,128]{2,1,0:T(8,128)(2,1)S(1)}, u32[]{:S(2)}) copy-start(bf16[1,576,128]{2,1,0:T(8,128)(2,1)S(1)} %get-tuple-element.31) | copy-start | bytes 442372
  117.1 16.5 %collective-permute-start.17 = (bf16[1,576,128]{2,1,0:T(8,128)(2,1)S(1)}, bf16[1,576,128]{2,1,0:T(8,128)(2,1)S(1)}, u32[]{:S(2)}, u32[]{:S(2)}) collective-permute-start(bf16[1,576,128]{2,1,0:T(8,128)(2,1)S(1)} %get-tuple-element.31), channel_id=1, source_target_pairs={{0,8},{1,5},{2,10},{3,7},{4,12},{5,1},{6,14},{7,3},{8,0},{9,13},{1... | collective-permute-start | bytes 442376 | tf_op jit(solution)/shard_map/ppermute | solution.py:635
  120.3 15.8 %collective-permute-start.25 = (bf16[1,64,896]{2,1,0:T(8,128)(2,1)S(1)}, bf16[1,64,896]{2,1,0:T(8,128)(2,1)S(1)}, u32[]{:S(2)}, u32[]{:S(2)}) collective-permute-start(bf16[1,64,896]{2,1,0:T(8,128)(2,1)S(1)} %slice.109), channel_id=1, source_target_pairs={{0,8},{1,5},{2,10},{3,7},{4,12},{5,1},{6,14},{7,3},{8,0},{9,13},{1... | collective-permute-start | bytes 344072 | tf_op jit(solution)/shard_map/ppermute | solution.py:635
  133.7 11.5 %collective-permute-start.18 = (bf16[2,576,128]{2,1,0:T(8,128)(2,1)S(1)}, bf16[2,576,128]{2,1,0:T(8,128)(2,1)S(1)}, u32[]{:S(2)}, u32[]{:S(2)}) collective-permute-start(bf16[2,576,128]{2,1,0:T(8,128)(2,1)S(1)} %pad_maximum_fusion.7), channel_id=1, source_target_pairs={{0,4},{1,9},{2,6},{3,11},{4,0},{5,13},{6,2},{7,15},{8,12},{9,1},{1... | collective-permute-start | bytes 884744 | tf_op jit(solution)/shard_map/ppermute | solution.py:635
  135.1 13.8 %collective-permute-start.9 = (bf16[2,576,128]{2,1,0:T(8,128)(2,1)S(1)}, bf16[2,576,128]{2,1,0:T(8,128)(2,1)S(1)}, u32[]{:S(2)}, u32[]{:S(2)}) collective-permute-start(bf16[2,576,128]{2,1,0:T(8,128)(2,1)S(1)} %pad_maximum_fusion.6), channel_id=1, source_target_pairs={{0,4},{1,9},{2,6},{3,11},{4,0},{5,13},{6,2},{7,15},{8,12},{9,1},{1... | collective-permute-start | bytes 884744 | tf_op jit(solution)/shard_map/ppermute | solution.py:635
  136.1 13.8 %copy-start.8 = (bf16[1,64,896]{2,1,0:T(8,128)(2,1)}, bf16[1,64,896]{2,1,0:T(8,128)(2,1)S(1)}, u32[]{:S(2)}) copy-start(bf16[1,64,896]{2,1,0:T(8,128)(2,1)S(1)} %get-tuple-element.29) | copy-start | bytes 344068
  136.1 13.8 %collective-permute-start.26 = (bf16[1,64,896]{2,1,0:T(8,128)(2,1)S(1)}, bf16[1,64,896]{2,1,0:T(8,128)(2,1)S(1)}, u32[]{:S(2)}, u32[]{:S(2)}) collective-permute-start(bf16[1,64,896]{2,1,0:T(8,128)(2,1)S(1)} %get-tuple-element.29), channel_id=1, source_target_pairs={{0,8},{1,5},{2,10},{3,7},{4,12},{5,1},{6,14},{7,3},{8,0},{9,13},{1... | collective-permute-start | bytes 344072 | tf_op jit(solution)/shard_map/ppermute | solution.py:635
  146.1 14.0 %collective-permute-start.19 = (bf16[4,576,128]{2,1,0:T(8,128)(2,1)}, bf16[4,576,128]{2,1,0:T(8,128)(2,1)}, u32[]{:S(2)}, u32[]{:S(2)}) collective-permute-start(bf16[4,576,128]{2,1,0:T(8,128)(2,1)} %pad_maximum_fusion.4), channel_id=1, source_target_pairs={{0,16},{1,3},{2,18},{3,1},{4,20},{5,7},{6,22},{7,5},{8,24},{9,11},... | collective-permute-start | bytes 1769480 | tf_op jit(solution)/shard_map/ppermute | solution.py:635
  149.8 17.4 %collective-permute-start.10 = (bf16[4,576,128]{2,1,0:T(8,128)(2,1)}, bf16[4,576,128]{2,1,0:T(8,128)(2,1)}, u32[]{:S(2)}, u32[]{:S(2)}) collective-permute-start(bf16[4,576,128]{2,1,0:T(8,128)(2,1)} %pad_maximum_fusion.3), channel_id=1, source_target_pairs={{0,16},{1,3},{2,18},{3,1},{4,20},{5,7},{6,22},{7,5},{8,24},{9,11},... | collective-permute-start | bytes 1769480 | tf_op jit(solution)/shard_map/ppermute | solution.py:635
  150.7 6.3 %collective-permute-start.27 = (bf16[2,64,896]{2,1,0:T(8,128)(2,1)}, bf16[2,64,896]{2,1,0:T(8,128)(2,1)}, u32[]{:S(2)}, u32[]{:S(2)}) collective-permute-start(bf16[2,64,896]{2,1,0:T(8,128)(2,1)} %pad_maximum_fusion.8), channel_id=1, source_target_pairs={{0,4},{1,9},{2,6},{3,11},{4,0},{5,13},{6,2},{7,15},{8,12},{9,1},{1... | collective-permute-start | bytes 688136 | tf_op jit(solution)/shard_map/ppermute | solution.py:635
  158.1 18.9 %collective-permute-start.28 = (bf16[4,64,896]{2,1,0:T(8,128)(2,1)S(1)}, bf16[4,64,896]{2,1,0:T(8,128)(2,1)S(1)}, u32[]{:S(2)}, u32[]{:S(2)}) collective-permute-start(bf16[4,64,896]{2,1,0:T(8,128)(2,1)S(1)} %pad_maximum_fusion.5), channel_id=1, source_target_pairs={{0,16},{1,3},{2,18},{3,1},{4,20},{5,7},{6,22},{7,5},{8,24},{9,11},... | collective-permute-start | bytes 1376264 | tf_op jit(solution)/shard_map/ppermute | solution.py:635
  161.2 15.7 %copy-start.9 = (bf16[1,64,896]{2,1,0:T(8,128)(2,1)S(1)}, bf16[1,64,896]{2,1,0:T(8,128)(2,1)}, u32[]{:S(2)}) copy-start(bf16[1,64,896]{2,1,0:T(8,128)(2,1)} %copy-done.8) | copy-start | bytes 344068
  161.3 24.6 %collective-permute-start.20 = (bf16[8,576,128]{2,1,0:T(8,128)(2,1)S(1)}, bf16[8,576,128]{2,1,0:T(8,128)(2,1)S(1)}, u32[]{:S(2)}, u32[]{:S(2)}) collective-permute-start(bf16[8,576,128]{2,1,0:T(8,128)(2,1)S(1)} %pad_maximum_fusion.1), channel_id=1, source_target_pairs={{0,2},{1,17},{2,0},{3,19},{4,6},{5,21},{6,4},{7,23},{8,10},{9,25},... | collective-permute-start | bytes 3538952 | tf_op jit(solution)/shard_map/ppermute | solution.py:635
  168.4 23.7 %collective-permute-start.11 = (bf16[8,576,128]{2,1,0:T(8,128)(2,1)S(1)}, bf16[8,576,128]{2,1,0:T(8,128)(2,1)S(1)}, u32[]{:S(2)}, u32[]{:S(2)}) collective-permute-start(bf16[8,576,128]{2,1,0:T(8,128)(2,1)S(1)} %pad_maximum_fusion), channel_id=1, source_target_pairs={{0,2},{1,17},{2,0},{3,19},{4,6},{5,21},{6,4},{7,23},{8,10},{9,25},... | collective-permute-start | bytes 3538952 | tf_op jit(solution)/shard_map/ppermute | solution.py:635
  178.0 27.3 %collective-permute-start.29 = (bf16[8,64,896]{2,1,0:T(8,128)(2,1)S(1)}, bf16[8,64,896]{2,1,0:T(8,128)(2,1)S(1)}, u32[]{:S(2)}, u32[]{:S(2)}) collective-permute-start(bf16[8,64,896]{2,1,0:T(8,128)(2,1)S(1)} %pad_maximum_fusion.2), channel_id=1, source_target_pairs={{0,2},{1,17},{2,0},{3,19},{4,6},{5,21},{6,4},{7,23},{8,10},{9,25},... | collective-permute-start | bytes 2752520 | tf_op jit(solution)/shard_map/ppermute | solution.py:635
  187.0 42.6 %collective-permute-start.21 = (bf16[16,576,128]{2,1,0:T(8,128)(2,1)}, bf16[16,576,128]{2,1,0:T(8,128)(2,1)}, u32[]{:S(2)}, u32[]{:S(2)}) collective-permute-start(bf16[16,576,128]{2,1,0:T(8,128)(2,1)} %constant_dynamic-update-slice_fusion.5.own), channel_id=1, source_target_pairs={{0,1},{1,0},{2,3},{3,2},{4,5},{5,4},{6,7},{7,6},{8,9},{9,8},{10,11... | collective-permute-start | bytes 7077896 | tf_op jit(solution)/shard_map/ppermute | solution.py:635
  193.3 44.8 %collective-permute-start.12 = (bf16[16,576,128]{2,1,0:T(8,128)(2,1)}, bf16[16,576,128]{2,1,0:T(8,128)(2,1)}, u32[]{:S(2)}, u32[]{:S(2)}) collective-permute-start(bf16[16,576,128]{2,1,0:T(8,128)(2,1)} %constant_dynamic-update-slice_fusion.own), channel_id=1, source_target_pairs={{0,1},{1,0},{2,3},{3,2},{4,5},{5,4},{6,7},{7,6},{8,9},{9,8},{10,11... | collective-permute-start | bytes 7077896 | tf_op jit(solution)/shard_map/ppermute | solution.py:635
  195.2 13.1 %copy-start.2 = (f32[336,512]{1,0:T(8,128)S(1)}, f32[336,512]{1,0:T(8,128)}, u32[]{:S(2)}) copy-start(f32[336,512]{1,0:T(8,128)} %copy-done.1) | copy-start | bytes 2064388
  205.5 16.8 %collective-permute-start.30 = (bf16[16,64,896]{2,1,0:T(8,128)(2,1)S(1)}, bf16[16,64,896]{2,1,0:T(8,128)(2,1)}, u32[]{:S(2)}, u32[]{:S(2)}) collective-permute-start(bf16[16,64,896]{2,1,0:T(8,128)(2,1)S(1)} %constant_dynamic-update-slice_fusion.10.own), channel_id=1, source_target_pairs={{0,1},{1,0},{2,3},{3,2},{4,5},{5,4},{6,7},{7,6},{8,9},{9,8},{10,11... | collective-permute-start | bytes 5505032 | tf_op jit(solution)/shard_map/ppermute | solution.py:635
  208.0 5.6 %collective-permute-start = (bf16[64,896]{1,0:T(8,128)(2,1)}, bf16[64,896]{1,0:T(8,128)(2,1)}, u32[]{:S(2)}, u32[]{:S(2)}) collective-permute-start(bf16[64,896]{1,0:T(8,128)(2,1)} %get-tuple-element.35), channel_id=1, source_target_pairs={{0,16},{16,0},{1,17},{17,1},{2,18},{18,2},{3,19},{19,3},{4,20},{20... | collective-permute-start | bytes 344072 | tf_op jit(solution)/shard_map/ppermute | solution.py:747
  211.7 6.1 %collective-permute-start.1 = (bf16[336,256]{1,0:T(8,128)(2,1)S(1)}, bf16[336,256]{1,0:T(8,128)(2,1)S(1)}, u32[]{:S(2)}, u32[]{:S(2)}) collective-permute-start(bf16[336,256]{1,0:T(8,128)(2,1)S(1)} %get-tuple-element.19), channel_id=1, source_target_pairs={{0,16},{16,0},{1,17},{17,1},{2,18},{18,2},{3,19},{19,3},{4,20},{20... | collective-permute-start | bytes 516104 | tf_op jit(solution)/shard_map/ppermute | solution.py:748
Sparse Core Ops, SparseCore 0:
  150.8 61.0 all-gather.2

commit v2 on v1

v2 whole, which is shorter than its diff:
```python
from functools import partial

import jax
import jax.numpy as jnp
from jax import lax
from jax.experimental import pallas as pl
from jax.experimental.pallas import tpu as pltpu
from jax.sharding import PartitionSpec as P

SIDE = 16
EPSILON = 1e-06
F32 = jnp.float32
BF16 = jnp.bfloat16
AXES = ("pipe", "dp")
MIB = 1024 * 1024


def device_index(dp):
    return lax.axis_index("pipe") * dp + lax.axis_index("dp")


HEAD, LATE, EARLY = 0, 1, 2


def stage_bits(dp, piece):
    size = dp.bit_length() - 1
    one, two, three, four = 1, size, 2, 3
    if piece == HEAD:
        stages = [(two, three), (one, two), (three, one), (four, four)]
    elif piece == LATE:
        stages = [(one, two), (two, one), (three, three), (four, four)]
    else:
        stages = [(three, one), (one, two), (two, three), (four, four)]
    return stages + [(bit, bit) for bit in range(4, size)]


def block_bits(dp, core, piece):
    index = device_index(dp)
    return [
        jnp.where(core == 0, (index >> first) & 1, (index >> second) & 1)
        for first, second in stage_bits(dp, piece)[:3]
    ]


def own_core(dp):
    return device_index(dp) & 1


class Layout:
    def __init__(self, side, channels, width):
        rows = rows_of(side)
        self.rows = rows
        self.mid = (side // 2) ** 2
        self.stacked = 2 * self.mid + (side // 4) ** 2
        self.lanes = width // (channels // 2)
        self.act = rows
        self.skip = rows
        self.span = 2 * rows
        self.grad = (0, self.span)
        self.normed = self.span + rows
        self.cot = self.normed + 2 * self.stacked
        self.small = self.cot + self.lanes * self.mid
        self.feed = self.small + 16 * self.lanes
        self.total = self.feed + rows


def spec(memory):
    return pl.BlockSpec(memory_space=memory)


def call(
    kernel, name, mib, cost, operands, in_specs, out_shape, out_specs, scratch=(), after=(), aliases=None
):
    count = len(operands)
    extra = len(after)

    def run(*refs):
        kernel(*refs[:count], *refs[count + extra :])

    return pl.pallas_call(
        run,
        out_shape=out_shape,
        in_specs=list(in_specs) + [spec(pl.ANY)] * extra,
        out_specs=out_specs,
        scratch_shapes=list(scratch),
        input_output_aliases=aliases or {},
        compiler_params=pltpu.CompilerParams(vmem_limit_bytes=mib * MIB),
        cost_estimate=pl.CostEstimate(flops=cost, bytes_accessed=1024, transcendentals=0),
        name=name,
    )(*operands, *after)


def grids(side):
    first = 0
    found = []
    for extent in (side, side // 2, side // 4):
        found.append((first, extent))
        first += extent * extent
    return found


def rows_of(side):
    return side * side + (side // 2) ** 2 + (side // 4) ** 2


def iota(shape, dim):
    return lax.broadcasted_iota(jnp.int32, shape, dim)


def edge_masks(side):
    row = iota((rows_of(side), 1), 0)
    first = jnp.zeros(row.shape, jnp.bool_)
    last = jnp.zeros(row.shape, jnp.bool_)
    for start, extent in grids(side):
        inside = (row >= start) & (row < start + extent * extent)
        column = (row - start) & (extent - 1)
        first = first | (inside & (column == 0))
        last = last | (inside & (column == extent - 1))
    return first, last


def column_shifts(value, side, target):
    first, last = edge_masks(side)
    rows = value.shape[0]
    target[0] = jnp.where(first, 0.0, pltpu.roll(value, 1, 0))
    target[1] = value
    target[2] = jnp.where(last, 0.0, pltpu.roll(value, rows - 1, 0))


def row_shift(shifted, b, a, side):
    parts = []
    width = shifted.shape[2]
    for start, extent in grids(side):
        count = extent * extent
        if a == 1:
            part = shifted[b, start : start + count, :]
        elif extent % 8 == 0:
            blank = jnp.zeros((extent, width), F32)
            if a == 0:
                part = jnp.concatenate([blank, shifted[b, start : start + count - extent, :]], axis=0)
            else:
                part = jnp.concatenate([shifted[b, start + extent : start + count, :], blank], axis=0)
        else:
            whole = shifted[b, start : start + count, :]
            row = iota((count, 1), 0)
            if a == 0:
                part = jnp.where(row < extent, 0.0, pltpu.roll(whole, extent, 0))
            else:
                part = jnp.where(row >= count - extent, 0.0, pltpu.roll(whole, count - extent, 0))
        parts.append(part.astype(BF16))
    return parts


def put_row_shift(target, row_start, lane_start, shifted, b, a, side):
    width = shifted.shape[2]
    for (start, extent), part in zip(grids(side), row_shift(shifted, b, a, side)):
        target[
            row_start + start : row_start + start + extent * extent, lane_start : lane_start + width
        ] = part


def dot(left, right):
    return lax.dot_general(left, right, (((1,), (0,)), ((), ())), preferred_element_type=F32)


def dot_last(left, right):
    return lax.dot_general(left, right, (((1,), (1,)), ((), ())), preferred_element_type=F32)


def block_of(index, extent):
    return (index // extent // 2) * (extent // 2) + (index % extent) // 2


def pool_matrix(extent, value):
    count = extent * extent
    shape = (count // 4, count)
    return jnp.where(block_of(iota(shape, 1), extent) == iota(shape, 0), value, 0.0).astype(BF16)


def spread_matrix(extent):
    count = extent * extent
    shape = (count, count // 4)
    return jnp.where(block_of(iota(shape, 0), extent) == iota(shape, 1), 1.0, 0.0).astype(BF16)


def spread(matrix, value):
    high = value.astype(BF16)
    low = (value - high.astype(F32)).astype(BF16)
    return dot(matrix, high) + dot(matrix, low)


def gelu_and_slope(z):
    root = 0.7978845608028654
    inner = root * (z + 0.044715 * z * z * z)
    t = jnp.tanh(inner)
    half = 0.5 * (1.0 + t)
    slope = half + 0.5 * z * (1.0 - t * t) * (root * (1.0 + 3 * 0.044715 * z * z))
    return z * half, slope


def head_cotangents(cot, coarse_cot, weights):
    return jnp.concatenate(
        [
            (weights[0] * cot).astype(BF16),
            (weights[1] * cot).astype(BF16),
            (weights[2] * coarse_cot).astype(BF16),
        ],
        axis=0,
    )


def copies(pairs, sems):
    made = [
        pltpu.make_async_copy(source, target, sems.at[num])
        for num, (source, target) in enumerate(pairs)
    ]
    for one in made:
        one.start()
    return made


def section_kernel(
    side,
    dp,
    plan,
    features,
    trunk_weight,
    head_weight,
    cotangent,
    gain_in,
    shift_in,
    scale_in,
    merging_in,
    own_out,
    send_out,
    pass_out,
    grad_out,
    slope_out,
    tap_grad_out,
    merged_out,
    feed,
    weights,
    heads,
    cot_ref,
    gain,
    shift,
    scale,
    merging,
    shifted,
    patch,
    sems,
):
    rows = rows_of(side)
    fine = side * side
    channels = feed.shape[1]
    half = channels // 2
    width = heads.shape[2]
    at = Layout(side, channels, width)
    mid = at.mid
    pipe = lax.axis_index("pipe")
    core = own_core(dp)
    pick = block_bits(dp, core, LATE)[0]
    made = copies(
        [(features.at[plan[0, pipe]], feed)]
        + [
            (
                trunk_weight.at[num // 3, pl.ds(num % 3 * 3 * channels, 3 * channels)],
                weights.at[num],
            )
            for num in range(6)
        ]
        + [(cotangent.at[pipe], cot_ref)]
        + [(head_weight.at[num], heads.at[num]) for num in range(2)]
        + [(gain_in, gain), (shift_in, shift), (scale_in, scale), (merging_in, merging)],
        sems,
    )
    made[0].wait()

    def conv(value, layer):
        column_shifts(value, side, shifted)
        total = jnp.zeros((rows, channels), F32)
        for a in range(3):
            for b in range(3):
                put_row_shift(patch, 0, b * channels, shifted, b, a, side)
            made[1 + 3 * layer + a].wait()
            total = total + dot(patch[...], weights[3 * layer + a])
        return total

    def put_halves(first, value):
        count = value.shape[0]
        left = value[:, :half]
        right = value[:, half:]
        own_out[first : first + count, :] = jnp.where(core == 0, left, right)
        send_out[first : first + count, :] = jnp.where(core == 0, right, left)

    low_feed = feed[...]
    feed_value = low_feed.astype(F32)
    put_halves(at.feed, low_feed)
    first_pre = conv(feed_value, 0)
    for num in range(10, 14):
        made[num].wait()
    act1, slope1 = gelu_and_slope(gain[0:1, :] * first_pre + shift[0:1, :])
    slope_out[...] = slope1 * gain[0:1, :]
    low_act = act1.astype(BF16)
    put_halves(at.act, low_act)
    z2 = gain[1:2, :] * conv(low_act.astype(F32), 1) + shift[1:2, :]
    trunk_out, slope2 = gelu_and_slope(z2)
    taps = [feed_value, trunk_out.astype(BF16).astype(F32)]

    made[7].wait()
    cot_low = cot_ref[...]
    cot = cot_low.astype(F32)
    coarse_cot = dot(pool_matrix(side // 2, 1.0), cot_low)
    pool = pool_matrix(side, 0.25)
    wide = spread_matrix(side)
    merged = jnp.zeros((mid, width), F32)
    coarse_merged = jnp.zeros((at.stacked - 2 * mid, width), F32)
    small = []
    scale_rows = []
    for k in range(2):
        tap = taps[k]
        scale_row = scale[k : k + 1, :]
        r = lax.rsqrt(jnp.mean(tap * tap, axis=-1, keepdims=True) + EPSILON)
        normed = (tap * r * scale_row).astype(BF16)
        pooled = dot(pool, normed[:fine]).astype(BF16)
        rows_k = jnp.concatenate([pooled, normed[fine:]], axis=0)
        put_halves(at.normed + k * at.stacked, rows_k)
        made[8 + k].wait()
        product = dot(rows_k, heads[k])
        weights_k = [merging[s, k : k + 1, :] for s in range(3)]
        merged = merged + weights_k[0] * product[:mid] + weights_k[1] * product[mid : 2 * mid]
        coarse_merged = coarse_merged + weights_k[2] * product[2 * mid :]
        small.append(jnp.sum(cot * product[:mid], axis=0, keepdims=True))
        small.append(jnp.sum(cot * product[mid : 2 * mid], axis=0, keepdims=True))
        small.append(jnp.sum(coarse_cot * product[2 * mid :], axis=0, keepdims=True))
        grads = head_cotangents(cot, coarse_cot, weights_k)
        back = dot_last(grads, heads[k])
        back = jnp.concatenate([spread(wide, 0.25 * back[:mid]), back[mid:]], axis=0)
        upstream = back * scale_row
        tap_grad = r * (
            upstream - tap * (r * r) * jnp.mean(upstream * tap, axis=-1, keepdims=True)
        )
        scale_rows.append(jnp.sum(back * tap * r, axis=0, keepdims=True))
        if k == 0:
            tap_grad_out[...] = tap_grad
    small.append(
        jnp.concatenate(scale_rows + [jnp.zeros((1, width - 2 * channels), F32)], axis=1)
    )
    small.append(jnp.zeros((1, width), F32))
    small = jnp.concatenate(small, axis=0)
    merged = merged + spread(spread_matrix(side // 2), coarse_merged)
    merged_out[...] = merged.astype(BF16)
    grad2 = (tap_grad.astype(BF16).astype(F32) * slope2 * gain[1:2, :]).astype(BF16)
    high = small.astype(BF16)
    both = jnp.concatenate([high.astype(F32), small - high.astype(F32)], axis=0).astype(BF16)
    for num in range(2):
        grad_out[num * rows : (num + 1) * rows, :] = grad2[:, num * half : (num + 1) * half]
    for target in (own_out, send_out):
        for num in range(2):
            target[at.grad[num] : at.grad[num] + rows, :] = grad2[:, num * half : (num + 1) * half]
        for num in range(at.lanes):
            lanes = slice(num * half, (num + 1) * half)
            target[at.cot + num * mid : at.cot + (num + 1) * mid, :] = cot_low[:, lanes]
            target[at.small + num * 16 : at.small + (num + 1) * 16, :] = both[:, lanes]
    pass_out[...] = own_out[pl.ds(pl.multiple_of((1 - pick) * at.skip, 16), at.span), :]


def section(dp, plan, features, trunk_weight, head_weight, cotangent, gain, shift, scale, merging):
    side = SIDE
    rows = rows_of(side)
    channels = features.shape[2]
    half = channels // 2
    width = head_weight.shape[2]
    mid = cotangent.shape[1]
    at = Layout(side, channels, width)
    vmem = spec(pltpu.VMEM)
    return call(
        partial(section_kernel, side, dp),
        "section",
        60,
        4200000000,
        (plan, features, trunk_weight, head_weight, cotangent, gain, shift, scale, merging),
        [spec(pltpu.SMEM)] + [spec(pl.ANY)] * 8,
        (
            jax.ShapeDtypeStruct((at.total, half), BF16),
            jax.ShapeDtypeStruct((at.total, half), BF16),
            jax.ShapeDtypeStruct((at.span, half), BF16),
            jax.ShapeDtypeStruct((2 * rows, half), BF16),
            jax.ShapeDtypeStruct((rows, channels), F32),
            jax.ShapeDtypeStruct((rows, channels), F32),
            jax.ShapeDtypeStruct((mid, width), BF16),
        ),
        (vmem,) * 7,
        [
            pltpu.VMEM((rows, channels), BF16),
            pltpu.VMEM((6, 3 * channels, channels), BF16),
            pltpu.VMEM((2, channels, width), BF16),
            pltpu.VMEM((mid, width), BF16),
            pltpu.VMEM(gain.shape, F32),
            pltpu.VMEM(shift.shape, F32),
            pltpu.VMEM(scale.shape, F32),
            pltpu.VMEM(merging.shape, F32),
            pltpu.VMEM((3, rows, channels), F32),
            pltpu.VMEM((rows, 3 * channels), BF16),
            pltpu.SemaphoreType.DMA((14,)),
        ],
    )


def back_kernel(side, layer, grad, trunk_weight, factor, *rest):
    if layer == 0:
        merged, own_out, send_out, weights, shifted, patch, sems = rest
    else:
        grad_out, weights, shifted, patch, sems = rest
    channels = trunk_weight.shape[2]
    half = channels // 2
    rows = rows_of(side)
    made = copies(
        [
            (trunk_weight.at[layer, pl.ds(num * 3 * channels, 3 * channels)], weights.at[num])
            for num in range(3)
        ],
        sems,
    )
    value = jnp.concatenate([grad[:rows, :], grad[rows:, :]], axis=1).astype(F32)
    column_shifts(value, side, shifted)
    total = jnp.zeros((rows, channels), F32)
    for a in range(3):
        for b in range(3):
            put_row_shift(patch, 0, b * channels, shifted, 2 - b, 2 - a, side)
        made[a].wait()
        for b in range(3):
            total = total + dot_last(
                patch[:, b * channels : (b + 1) * channels],
                weights[a, b * channels : (b + 1) * channels, :],
            )
    if layer == 1:
        low = (total * factor[...]).astype(BF16)
        grad_out[:rows, :] = low[:, :half]
        grad_out[rows:, :] = low[:, half:]
        return
    pipe = lax.axis_index("pipe")
    total = total + factor[...]
    left, right = total[:, :half], total[:, half:]
    own_out[...] = jnp.where(pipe == 0, left, right)
    sent = jnp.where(pipe == 0, right, left).astype(BF16)
    low_merged = merged[...]
    mid, width = low_merged.shape
    sent_merged = jnp.where(
        pipe == 0, low_merged[:, width // 2 :], low_merged[:, : width // 2]
    )
    for num in range(half // 128):
        send_out[num * rows : (num + 1) * rows, :] = sent[:, num * 128 : (num + 1) * 128]
    first = half // 128 * rows
    for num in range(width // 256):
        send_out[first + num * mid : first + (num + 1) * mid, :] = sent_merged[
            :, num * 128 : (num + 1) * 128
        ]


def back(layer, grad, trunk_weight, factor, merged=None, after=()):
    side = SIDE
    rows = rows_of(side)
    channels = trunk_weight.shape[2]
    half = channels // 2
    vmem = spec(pltpu.VMEM)
    in_specs = [vmem, spec(pl.ANY), vmem]
    operands = [grad, trunk_weight, factor]
    if layer == 0:
        in_specs.append(vmem)
        operands.append(merged)
        out_shape = (
            jax.ShapeDtypeStruct((rows, half), F32),
            jax.ShapeDtypeStruct((half // 128 * rows + merged.size // 256, 128), BF16),
        )
        out_specs = (vmem, vmem)
    else:
        out_shape = jax.ShapeDtypeStruct((2 * rows, half), BF16)
        out_specs = vmem
    return call(
        partial(back_kernel, side, layer),
        "back",
        46,
        1500000000,
        operands,
        in_specs,
        out_shape,
        out_specs,
        [
            pltpu.VMEM((3, 3 * channels, channels), BF16),
            pltpu.VMEM((3, rows, channels), F32),
            pltpu.VMEM((rows, 3 * channels), BF16),
            pltpu.SemaphoreType.DMA((3,)),
        ],
        after,
    )


def through(pairs, held, sems):
    coming = [
        pltpu.make_async_copy(source, slot, sems.at[num])
        for num, (source, slot, target) in enumerate(pairs)
    ]
    going = [
        pltpu.make_async_copy(slot, target, sems.at[len(pairs) + num])
        for num, (source, slot, target) in enumerate(pairs)
    ]
    for one in coming:
        one.start()
    for one, two in zip(coming, going):
        one.wait()
        two.start()
    for two in going:
        two.wait()


def move_kernel(moves, *refs):
    sources, out, held, sems = refs[:-3], refs[-3], refs[-2], refs[-1]
    through(
        [
            (sources[num].at[first()], held.at[pl.ds(place, count)], out.at[pl.ds(place, count)])
            for num, first, place, count in moves
        ],
        held,
        sems,
    )


def far_factors(dp, other, side, width, after):
    half = other.shape[1]
    at = Layout(side, 2 * half, width)

    def rows():
        pick = block_bits(dp, own_core(dp), LATE)[0]
        return pl.ds(pl.multiple_of((1 - pick) * at.skip, 16), at.span)

    return call(
        partial(move_kernel, [(0, rows, 0, at.span)]),
        "far_factors",
        4,
        120000000,
        (other,),
        [spec(pl.ANY)],
        jax.ShapeDtypeStruct((at.span, half), BF16),
        spec(pl.ANY),
        [pltpu.VMEM((at.span, half), BF16), pltpu.SemaphoreType.DMA((2,))],
        after,
    )


def first_factors(dp, own, other, own_grad, other_grad, side, width, after):
    half = other.shape[1]
    at = Layout(side, 2 * half, width)

    def feed():
        return pl.ds(at.feed, at.rows)

    def grad():
        pick = block_bits(dp, own_core(dp), EARLY)[0]
        return pl.ds(pl.multiple_of((1 - pick) * at.rows, 16), at.rows)

    return call(
        partial(
            move_kernel,
            [
                (num, (feed, feed, grad, grad)[num], num * at.rows, at.rows)
                for num in range(4)
            ],
        ),
        "first_factors",
        4,
        540000000,
        (own, other, own_grad, other_grad),
        [spec(pl.ANY)] * 4,
        jax.ShapeDtypeStruct((4 * at.rows, half), BF16),
        spec(pl.ANY),
        [pltpu.VMEM((4 * at.rows, half), BF16), pltpu.SemaphoreType.DMA((8,))],
        after,
    )


def put_trunk_blocks(dp, piece, send, keep, xs, gs, shifted, patch, side, wait_x, wait_g):
    rows = rows_of(side)
    half = xs.shape[1]
    quarter = half // 2
    _, second, third = block_bits(dp, own_core(dp), piece)
    for image in range(4):
        wait_g(image)
        column_shifts(gs[image * rows : (image + 1) * rows, :].astype(F32), side, shifted)
        for a in range(3):
            for b in range(3):
                put_row_shift(
                    patch, image * rows, (3 * a + b) * half, shifted, 2 - b, 2 - a, side
                )
    for image in range(4):
        wait_x(image)
    turned = xs[...].T
    for offset in range(9):
        product = dot(turned, patch[:, offset * half : (offset + 1) * half]).astype(BF16)
        left, right = product[:, :128], product[:, 128:]
        for target, value in (
            (keep, jnp.where(second == 0, left, right)),
            (send, jnp.where(second == 0, right, left)),
        ):
            upper, lower = value[:quarter], value[quarter:]
            row = offset * quarter
            target[row : row + quarter, :] = jnp.where(third == 0, upper, lower)
            row += 9 * quarter
            target[row : row + quarter, :] = jnp.where(third == 0, lower, upper)


def late_grads_kernel(
    side, dp, width, own, other, near, far, send, keep, xs, gs, shifted, patch, sems
):
    half = xs.shape[1]
    at = Layout(side, 2 * half, width)
    rows = at.rows
    pick = block_bits(dp, own_core(dp), LATE)[0]
    grad_at = pick * at.grad[1]
    pairs = []
    for num, source in enumerate((own, other, near, far)):
        back_by = 0 if num < 2 else pick * at.skip

        def some(first):
            return source.at[pl.ds(pl.multiple_of(first - back_by, 16), rows)]

        pairs += [
            (some(grad_at), gs.at[pl.ds(num * rows, rows)]),
            (some(at.act), xs.at[pl.ds(num * rows, rows)]),
        ]
    made = copies(pairs, sems)
    put_trunk_blocks(
        dp,
        LATE,
        send,
        keep,
        xs,
        gs,
        shifted,
        patch,
        side,
        lambda image: made[2 * image + 1].wait(),
        lambda image: made[2 * image].wait(),
    )


def split_pair(value):
    high = value.astype(BF16).astype(F32)
    return jnp.concatenate([high, value - high], axis=0).astype(BF16)


def trunk_scratch(rows, half):
    return [
        pltpu.VMEM((3, rows, half), F32),
        pltpu.VMEM((4 * rows, 9 * half), BF16),
    ]


def late_grads(dp, width, own, other, near, far, after):
    side = SIDE
    rows = rows_of(side)
    half = own.shape[1]
    vmem = spec(pltpu.VMEM)
    shape = jax.ShapeDtypeStruct((9 * half, 128), BF16)
    return call(
        partial(late_grads_kernel, side, dp, width),
        "late_grads",
        28,
        1440000000,
        (own, other, near, far),
        [spec(pl.ANY)] * 4,
        (shape, shape),
        (vmem, vmem),
        [
            pltpu.VMEM((4 * rows, half), BF16),
            pltpu.VMEM((4 * rows, half), BF16),
            *trunk_scratch(rows, half),
            pltpu.SemaphoreType.DMA((8,)),
        ],
        after,
    )


def early_grads_kernel(
    side, dp, width, own, other, own_g, other_g, far, send, keep, xs, gs, shifted, patch, sems
):
    half = xs.shape[1]
    at = Layout(side, 2 * half, width)
    rows = at.rows
    pick = block_bits(dp, own_core(dp), EARLY)[0]
    mine = pl.ds(pl.multiple_of(pick * rows, 16), rows)
    made = copies(
        [
            (own_g.at[mine], gs.at[pl.ds(0, rows)]),
            (other_g.at[mine], gs.at[pl.ds(rows, rows)]),
            (far.at[pl.ds(2 * rows, 2 * rows)], gs.at[pl.ds(2 * rows, 2 * rows)]),
            (own.at[pl.ds(at.feed, rows)], xs.at[pl.ds(0, rows)]),
            (other.at[pl.ds(at.feed, rows)], xs.at[pl.ds(rows, rows)]),
            (far.at[pl.ds(0, 2 * rows)], xs.at[pl.ds(2 * rows, 2 * rows)]),
        ],
        sems,
    )
    put_trunk_blocks(
        dp,
        EARLY,
        send,
        keep,
        xs,
        gs,
        shifted,
        patch,
        side,
        lambda image: made[3 + image].wait() if image < 3 else None,
        lambda image: made[image].wait() if image < 3 else None,
    )


def early_grads(dp, width, own, other, own_g, other_g, far, after):
    side = SIDE
    rows = rows_of(side)
    half = own.shape[1]
    vmem = spec(pltpu.VMEM)
    shape = jax.ShapeDtypeStruct((9 * half, 128), BF16)
    return call(
        partial(early_grads_kernel, side, dp, width),
        "early_grads",
        28,
        1140000000,
        (own, other, own_g, other_g, far),
        [spec(pl.ANY)] * 5,
        (shape, shape),
        (vmem, vmem),
        [
            pltpu.VMEM((4 * rows, half), BF16),
            pltpu.VMEM((4 * rows, half), BF16),
            *trunk_scratch(rows, half),
            pltpu.SemaphoreType.DMA((6,)),
        ],
        after,
    )


def head_grads_kernel(
    side, dp, is_own, own, other, merging_in, out, ns, cots, smalls, merging, sems
):
    half = ns.shape[1]
    width = merging.shape[2]
    at = Layout(side, 2 * half, width)
    mid = at.mid
    pick, second, third = block_bits(dp, own_core(dp), HEAD)
    tap = pick if is_own else 1 - pick
    first = pl.multiple_of(at.normed + tap * at.stacked, 16)
    pairs = [(merging_in, merging)]
    for num, source in enumerate((own, other)):
        pairs += [
            (source.at[pl.ds(at.cot, at.lanes * mid)], cots.at[num]),
            (source.at[pl.ds(first, at.stacked)], ns.at[pl.ds(num * at.stacked, at.stacked)]),
            (source.at[pl.ds(at.small, at.lanes * 16)], smalls.at[num]),
        ]
    made = copies(pairs, sems)
    made[0].wait()
    weights = [merging[s, pl.ds(tap, 1), :] for s in range(3)]
    sums = pool_matrix(side // 2, 1.0)
    grads = []
    for image in range(2):
        made[1 + 3 * image].wait()
        cot_low = jnp.concatenate(
            [cots[image, num * mid : (num + 1) * mid, :] for num in range(at.lanes)], axis=1
        )
        grads.append(head_cotangents(cot_low.astype(F32), dot(sums, cot_low), weights))
    made[2].wait()
    made[5].wait()
    product = dot(ns[...].T, jnp.concatenate(grads, axis=0)).astype(BF16)
    quarter = half // 2
    for lane in range(2):
        for num in range(width // 256):
            column = lane * (width // 2) + num * 128
            for part in range(2):
                row = pl.multiple_of(
                    (((lane ^ second) * 2 + (part ^ third)) * (width // 256) + num) * quarter,
                    quarter,
                )
                out[pl.ds(row, quarter), :] = product[
                    part * quarter : (part + 1) * quarter, column : column + 128
                ]
    made[3].wait()
    made[6].wait()
    total = smalls[0].astype(F32) + smalls[1].astype(F32)
    first = width // 128 * half
    for num in range(at.lanes):
        pair = split_pair(total[num * 16 : num * 16 + 8] + total[num * 16 + 8 : num * 16 + 16])
        for lane in range(half // 128):
            row = first + (num * (half // 128) + lane) * 16
            out[row : row + 16, :] = pair[:, lane * 128 : (lane + 1) * 128]


def head_grads(dp, is_own, own, other, merging, after):
    side = SIDE
    half = own.shape[1]
    width = merging.shape[2]
    at = Layout(side, 2 * half, width)
    return call(
        partial(head_grads_kernel, side, dp, is_own),
        "head_grads",
        16,
        570000000,
        (own, other, merging),
        [spec(pl.ANY)] * 3,
        jax.ShapeDtypeStruct((width // 128 * half + 16 * width // 128, 128), BF16),
        spec(pltpu.VMEM),
        [
            pltpu.VMEM((2 * at.stacked, half), BF16),
            pltpu.VMEM((2, at.lanes * at.mid, half), BF16),
            pltpu.VMEM((2, at.lanes * 16, half), BF16),
            pltpu.VMEM(merging.shape, F32),
            pltpu.SemaphoreType.DMA((7,)),
        ],
        after,
    )


def add_tails(one, two):
    count = one.shape[0] // 16
    one = one.astype(F32).reshape(count, 16, 128)
    two = two.astype(F32).reshape(count, 16, 128)
    total = (one[:, :8] + one[:, 8:]) + (two[:, :8] + two[:, 8:])
    high = total.astype(BF16).astype(F32)
    return jnp.concatenate([high, total - high], axis=1).reshape(count * 16, 128).astype(BF16)


def sum_kernel(tail, keep, received, *outs):
    rows = keep.shape[0] - tail
    size = rows // len(outs)
    for num, out in enumerate(outs):
        part = slice(num * size, (num + 1) * size)
        out[:size, :] = (keep[part, :].astype(F32) + received[part, :].astype(F32)).astype(BF16)
    if tail:
        total = add_tails(keep[rows:, :], received[rows:, :])
        for out in outs:
            out[size:, :] = total


def summed(keep, received, parts, tail, after):
    vmem = spec(pltpu.VMEM)
    shape = jax.ShapeDtypeStruct(((keep.shape[0] - tail) // parts + tail, 128), BF16)
    return call(
        partial(sum_kernel, tail),
        "summed",
        4,
        1024,
        (keep, received),
        [vmem, vmem],
        (shape,) * parts,
        (vmem,) * parts,
        (),
        after,
    )


def pair_kernel(one, two, out):
    rows = out.shape[0] // 2
    out[:rows, :] = one[:rows, :]
    out[rows:, :] = two[:rows, :]


def paired(one, two, rows, after):
    vmem = spec(pltpu.VMEM)
    return call(
        pair_kernel,
        "paired",
        4,
        1024,
        (one, two),
        [vmem, vmem],
        jax.ShapeDtypeStruct((2 * rows, 128), BF16),
        vmem,
        (),
        after,
    )


def widen_trunk_kernel(dp, layer, half, kinds, *refs):
    sources = refs[: len(kinds)]
    out, done, held, wide, sems_in, sems_out = refs[-6:]
    done[...] = jnp.zeros(done.shape, F32)
    quarter = half // 2
    size = 9 * quarter
    jobs = []
    coming = []
    for source, (is_other, is_new) in zip(sources, kinds):
        core = own_core(dp) ^ int(is_other)
        first, second, third = block_bits(dp, core, LATE if layer else EARLY)
        first = first ^ int(is_new)
        for part in range(2):
            for lane in range(2):
                row = pl.multiple_of(((lane ^ second) * 2 + part) * size, size)
                coming.append((source.at[pl.ds(row, size)], held.at[len(jobs), lane]))
            jobs.append((core * half + (part ^ third) * quarter, first * half))
    made = copies(coming, sems_in)
    going = []
    for num, (row, column) in enumerate(jobs):
        for lane in range(2):
            made[2 * num + lane].wait()
            for offset in range(9):
                wide[num, offset, :, lane * 128 : (lane + 1) * 128] = held[
                    num, lane, offset * quarter : (offset + 1) * quarter, :
                ].astype(F32)
        one = pltpu.make_async_copy(
            wide.at[num],
            out.at[
                layer,
                :,
                pl.ds(pl.multiple_of(row, quarter), quarter),
                pl.ds(pl.multiple_of(column, half), half),
            ],
            sems_out.at[num],
        )
        one.start()
        going.append(one)
    for one in going:
        one.wait()


def widen_trunk(dp, layer, layers, half, sources, kinds, before=None, after=()):
    hbm = spec(pl.ANY)
    operands = list(sources) + ([before] if before is not None else [])
    count = 2 * len(kinds)
    return call(
        partial(widen_trunk_kernel, dp, layer, half, kinds),
        "widen_trunk",
        24,
        870000000,
        operands,
        [hbm] * len(operands),
        (
            jax.ShapeDtypeStruct((layers, 9, 2 * half, 2 * half), F32),
            jax.ShapeDtypeStruct((8, 128), F32),
        ),
        (hbm, spec(pltpu.VMEM)),
        [
            pltpu.VMEM((count, 2, 9 * half // 2, 128), BF16),
            pltpu.VMEM((count, 9, half // 2, half), F32),
            pltpu.SemaphoreType.DMA((2 * count,)),
            pltpu.SemaphoreType.DMA((count,)),
        ],
        after,
        {len(sources): 0} if before is not None else None,
    )


def widen_heads_kernel(dp, half, kinds, *refs):
    sources = refs[: len(kinds)]
    out, done, held, wide, sems_in, sems_out = refs[-6:]
    done[...] = jnp.zeros(done.shape, F32)
    quarter = half // 2
    size = held.shape[2]
    width = wide.shape[2]
    jobs = []
    coming = []
    for source, (is_other, is_new) in zip(sources, kinds):
        core = own_core(dp) ^ int(is_other)
        first, second, third = block_bits(dp, core, HEAD)
        for lane in range(2):
            for part in range(2):
                row = pl.multiple_of(((lane ^ second) * 2 + (part ^ third)) * size, size)
                coming.append((source.at[pl.ds(row, size)], held.at[len(jobs), part]))
            jobs.append((first ^ int(is_new), core * half, lane * width))
    made = copies(coming, sems_in)
    going = []
    for num, (tap, row, column) in enumerate(jobs):
        for part in range(2):
            made[2 * num + part].wait()
            for piece in range(width // 128):
                wide[
                    num, part * quarter : (part + 1) * quarter, piece * 128 : (piece + 1) * 128
                ] = held[num, part, piece * quarter : (piece + 1) * quarter, :].astype(F32)
        one = pltpu.make_async_copy(
            wide.at[num],
            out.at[tap, pl.ds(pl.multiple_of(row, half), half), pl.ds(column, width)],
            sems_out.at[num],
        )
        one.start()
        going.append(one)
    for one in going:
        one.wait()


def widen_heads(dp, half, width, sources, kinds, before=None, after=()):
    hbm = spec(pl.ANY)
    operands = list(sources) + ([before] if before is not None else [])
    count = 2 * len(kinds)
    return call(
        partial(widen_heads_kernel, dp, half, kinds),
        "widen_heads",
        40,
        1320000000,
        operands,
        [hbm] * len(operands),
        (
            jax.ShapeDtypeStruct((2, 2 * half, width), F32),
            jax.ShapeDtypeStruct((8, 128), F32),
        ),
        (hbm, spec(pltpu.VMEM)),
        [
            pltpu.VMEM((count, 2, width // 256 * half // 2, 128), BF16),
            pltpu.VMEM((count, half, width // 2), F32),
            pltpu.SemaphoreType.DMA((2 * count,)),
            pltpu.SemaphoreType.DMA((count,)),
        ],
        after,
        {len(sources): 0} if before is not None else None,
    )


def finish_kernel(
    dp, at, plan, own_feed, merged, received, own_sum, other_sum,
    merged_out, feed_out, scale_out, merging_out, held, sems,
):
    tail = pl.ds(at, held.shape[1])
    made = copies([(own_sum.at[tail], held.at[0]), (other_sum.at[tail], held.at[1])], sems)
    pipe = lax.axis_index("pipe")
    rows, half = own_feed.shape
    mid, width = merged.shape
    slot = plan[0, pipe]
    feed_out[slot] = own_feed[...]
    for num in range(half // 128):
        feed_out[1 - slot, :, num * 128 : (num + 1) * 128] = received[
            num * rows : (num + 1) * rows, :
        ].astype(F32)
    low_merged = merged[...]
    merged_out[pipe] = jnp.where(
        pipe == 0, low_merged[:, : width // 2], low_merged[:, width // 2 :]
    )
    first = half // 128 * rows
    for num in range(width // 256):
        merged_out[1 - pipe, :, num * 128 : (num + 1) * 128] = received[
            first + num * mid : first + (num + 1) * mid, :
        ]
    for one in made:
        one.wait()
    low = jnp.where(own_core(dp) == 0, held[0], held[1]).astype(F32)
    for num in range(width // 128):
        lanes = slice(num * 128, (num + 1) * 128)
        block = low[num * 16 : num * 16 + 8] + low[num * 16 + 8 : num * 16 + 16]
        for k in range(2):
            for s in range(3):
                merging_out[s, k : k + 1, lanes] = block[3 * k + s : 3 * k + s + 1]
        for k in range(2):
            column = num * 128 - k * 2 * half
            if 0 <= column < 2 * half:
                scale_out[k : k + 1, column : column + 128] = block[6:7]


def finish(dp, plan, own_feed, merged, received, own_sum, other_sum, after):
    rows, half = own_feed.shape
    mid, width = merged.shape
    vmem = spec(pltpu.VMEM)
    tail = 16 * width // 128
    return call(
        partial(finish_kernel, dp, own_sum.shape[0] - tail),
        "finish",
        8,
        510000000,
        (plan, own_feed, merged, received, own_sum, other_sum),
        [spec(pltpu.SMEM), vmem, vmem, vmem, spec(pl.ANY), spec(pl.ANY)],
        (
            jax.ShapeDtypeStruct((2, mid, width // 2), BF16),
            jax.ShapeDtypeStruct((2, rows, half), F32),
            jax.ShapeDtypeStruct((2, 2 * half), F32),
            jax.ShapeDtypeStruct((3, 2, width), F32),
        ),
        (vmem,) * 4,
        [pltpu.VMEM((2, tail, 128), BF16), pltpu.SemaphoreType.DMA((2,))],
        after,
    )


class Sum:
    def __init__(self, swap, piece, last, send, keep, tail=0):
        self.swap = partial(swap, piece)
        self.tail = tail
        self.steps = [("scatter", stage) for stage in range(0 if piece == HEAD else 1, 3)]
        self.steps += [("whole", stage) for stage in range(3, last + 1)]
        self.steps += [("gather", stage) for stage in (2, 1, 0)]
        self.at = 0
        self.keep = keep
        self.come = self.swap(self.steps[0][1], send)

    def advance(self, *after):
        kind = self.steps[self.at][0]
        self.at += 1
        following, stage = self.steps[self.at]
        if kind == "gather":
            self.keep = paired(self.keep, self.come, self.keep.shape[0] - self.tail, after)
            self.tail = 0
            send = self.keep
        else:
            parts = 2 if following == "scatter" else 1
            made = summed(self.keep, self.come, parts, self.tail, after)
            self.keep = made[0]
            send = made[-1]
            if following == "gather":
                self.final = self.keep
        self.come = self.swap(stage, send)
        return self.keep


def body(
    features,
    plan,
    trunk_weight,
    trunk_gain,
    trunk_shift,
    head_weight,
    norm_scale,
    merging_weight,
    merged_cotangent,
):
    dp = lax.axis_size("dp")
    devices = lax.axis_size("pipe") * dp
    layers = trunk_weight.shape[0]
    channels = features.shape[2]
    half = channels // 2
    width = head_weight.shape[2]
    last = dp.bit_length() - 2
    weights = trunk_weight.reshape(layers, 9 * channels, channels)
    merging = jnp.transpose(merging_weight, (1, 0, 2))
    tail = 16 * width // 128

    def swap(piece, stage, block):
        bits = stage_bits(dp, piece)[stage]
        route = [(i, i ^ (1 << bits[i & 1])) for i in range(devices)]
        return lax.ppermute(block, AXES, route)

    def swap_cores(block):
        return lax.ppermute(block, AXES, [(i, i ^ 1) for i in range(devices)])

    own, send, passed, grad2, slope, tap_grad, merged = section(
        dp,
        plan,
        features,
        weights,
        head_weight,
        merged_cotangent,
        trunk_gain,
        trunk_shift,
        norm_scale,
        merging,
    )
    other = swap_cores(send)
    near = swap(LATE, 0, passed)
    passed = far_factors(dp, other, SIDE, width, ())
    far = swap(LATE, 0, passed)
    head_send = head_grads(dp, False, own, other, merging, (passed,))
    head_keep = head_grads(dp, True, own, other, merging, (head_send, near))
    head = Sum(swap, HEAD, last, head_send, head_keep, tail)
    grad1 = back(1, grad2, weights, slope, None, (head_keep, far))
    other_grad1 = swap_cores(grad1)
    passed = first_factors(dp, own, other, grad1, other_grad1, SIDE, width, ())
    first_far = swap(EARLY, 0, passed)
    token = head.advance(passed)
    late_blocks = late_grads(dp, width, own, other, near, far, (token,))
    late = Sum(swap, LATE, last, *late_blocks)
    token = head.advance(late.keep)
    early_blocks = early_grads(
        dp, width, own, other, grad1, other_grad1, first_far, (token,)
    )
    early = Sum(swap, EARLY, last, *early_blocks)
    pieces = {"H": head, "L": late, "E": early}

    def advance(order, *tokens):
        for name in order:
            tokens = (pieces[name].advance(*tokens),)
        return tokens[0]

    token = advance("LHELHE" + "LHE" * (last - 3), early.keep)
    own_feed, sent = back(0, grad1, weights, tap_grad, merged, (token,))
    received = lax.ppermute(sent, "pipe", [(0, 1), (1, 0)])
    token = advance("LHELH", own_feed)
    other_head = swap_cores(head.keep)
    other_sum = swap_cores(head.final)
    token = advance("EL", token)
    other_late = swap_cores(late.keep)
    merged_maps, features_grad, scale_grad, merging_grad = finish(
        dp, plan, own_feed, merged, received, head.final, other_sum, (token,)
    )
    token = advance("E", merged_maps)
    other_early = swap_cores(early.keep)
    kept = ((False, False), (True, False))
    came = ((False, True), (True, True))
    head_out, done = widen_heads(dp, half, width, (head.keep, other_head), kept, None, (token,))
    trunk_out, done = widen_trunk(
        dp, 1, layers, half, (late.keep, other_late), kept, None, (done,)
    )
    trunk_out, done = widen_trunk(
        dp, 0, layers, half, (early.keep, other_early), kept, trunk_out, (done, head.come)
    )
    head_out, done = widen_heads(
        dp, half, width, (head.come, swap_cores(head.come)), came, head_out, (done, late.come)
    )
    trunk_out, done = widen_trunk(
        dp, 1, layers, half, (late.come, swap_cores(late.come)), came, trunk_out, (done, early.come)
    )
    other_new = swap_cores(early.come)
    trunk_out, done = widen_trunk(dp, 0, layers, half, (early.come,), came[:1], trunk_out, (done,))
    trunk_out, done = widen_trunk(dp, 0, layers, half, (other_new,), came[1:], trunk_out, (done,))
    return (
        merged_maps,
        features_grad,
        trunk_out.reshape(trunk_weight.shape),
        head_out,
        scale_grad,
        jnp.transpose(merging_grad, (1, 0, 2)),
    )


def solution(mesh):
    placed = (P("dp", None, None), P("dp", None), P(), P(), P(), P(), P(), P(), P("dp", None, None))
    return jax.shard_map(
        body,
        mesh=mesh,
        in_specs=placed,
        out_specs=(P("dp", None, "pipe"), P("dp", None, "pipe"), P(), P(), P(), P()),
        check_vma=False,
    )
```

time: 255 us -> 184 us (0.72)
  starting transfers between devices: 53.3 us -> 34.9 us
  other arithmetic: 17.8 us -> 0 us
  local copies, waits for them, and re-layouts: 16.9 us -> 0.97 us
  between operations: 14.4 us -> 1.19 us
  waiting for transfers between devices: 92.1 us -> 86.6 us
    ppermute x31 -> x32, starting transfers between devices: 53.3 us -> 34.9 us  [the longest x22 32.2 us: swap(): return lax.ppermute(block, AXES, route)]
    unnamed x31 -> x16, local copies, waits for them, and re-layouts: 13.6 us -> 0.97 us
    concatenate x9 -> x0, other arithmetic: 7.03 us -> none  [gather(): block = jnp.concatenate([block, swap_over(block, devices, stage)], axis=0)]
    ppermute x31 -> x32, waiting for transfers between devices: 92.1 us -> 86.6 us  [the longest x22 83.2 us: swap(): return lax.ppermute(block, AXES, route)]
    select_n x2 -> x0, other arithmetic: 3.29 us -> none  [in_order(): return jnp.where(is_first, jnp.stack([one, two]), jnp.stack([two, one]))]
    pallas_call x12 -> x33, Pallas kernels: 59.1 us -> 60.2 us  [call(): pl.pallas_call(run, out_shape=out_shape, in_specs=list(in_specs) + [spec(...]
  transfers between devices with their start and end apart: 32 -> 32, of which waited for: 17 -> 15; matrix products, arithmetic and copies ran while one was open for 11% -> 0% of each run, Pallas kernels for 14% -> 24%
where the time goes in v2:
time: 184 us
  waiting for transfers between devices  86.6 us (47%)
  Pallas kernels  60.2 us (33%)
  starting transfers between devices  34.9 us (19%)
    ppermute x22, waiting for transfers between devices, swap(): return lax.ppermute(block, AXES, route)  83.2 us
    pallas_call x33, Pallas kernels, call(): pl.pallas_call(run, out_shape=out_shape, in_specs=list(in_specs) + [spec(...  60.2 us
    ppermute x22, starting transfers between devices, swap(): return lax.ppermute(block, AXES, route)  32.2 us
  transfers between devices with their start and end apart: 32, of which 15 were waited for; matrix products, arithmetic and copies ran while one was open for 0% of the time, Pallas kernels for 24%

profile of v2, /device:TPU:0, one launch (start us, length us, event | category | flops | bytes accessed | tf_op | source)
XLA Modules:
  0.0 183.8 jit_solution(2315830475154769275)
XLA Ops:
  0.6 14.1 %section.1 = (bf16[2192,256]{1,0:T(8,128)(2,1)}, bf16[2192,256]{1,0:T(8,128)(2,1)}, bf16[672,256]{1,0:T(8,128)(2,1)}, bf16[672,256]{1,0:T(8,128)(2,1)}, f32[336,...) custom-call(s32[1,2]{1,0:T(1,128)} %refs_0_.3, bf16[2,336,512]{2,1,0:T(8,128)(2,1)} %refs_1_.1, ...), custom_call_target="tpu_custom_call" | custom-call | flops 4200000000 | bytes 1024 | tf_op jit(solution)/shard_map/section/pallas_call | solution.py:80
  15.3 2.6 %collective-permute-start.1 = (bf16[672,256]{1,0:T(8,128)(2,1)}, bf16[672,256]{1,0:T(8,128)(2,1)S(1)}, u32[]{:S(2)}, u32[]{:S(2)}) collective-permute-start(bf16[672,256]{1,0:T(8,128)(2,1)} %get-tuple-element.48), channel_id=1, source_target_pairs={{0,2},{1,17},{2,0},{3,19},{4,6},{5,21},{6,4},{7,23},{8,10},{9,25},... | collective-permute-start | bytes 1032200 | tf_op jit(solution)/shard_map/ppermute | solution.py:1133
  18.1 2.9 %collective-permute-start.2 = (bf16[672,256]{1,0:T(8,128)(2,1)S(1)}, bf16[672,256]{1,0:T(8,128)(2,1)S(1)}, u32[]{:S(2)}, u32[]{:S(2)}) collective-permute-start(bf16[672,256]{1,0:T(8,128)(2,1)S(1)} %far_factors.1.refs_3_), channel_id=1, source_target_pairs={{0,2},{1,17},{2,0},{3,19},{4,6},{5,21},{6,4},{7,23},{8,10},{9,25},... | collective-permute-start | bytes 1032200 | tf_op jit(solution)/shard_map/ppermute | solution.py:1133
  21.1 2.1 %head_grads.2.refs_3_ = bf16[3808,128]{1,0:T(8,128)(2,1)S(1)} custom-call(bf16[2192,256]{1,0:T(8,128)(2,1)S(1)} %copy-done, bf16[2192,256]{1,0:T(8,128)(2,1)S(1)} %collective-permute-done.refs_0_.refs_1_, f32[3,2,1792]{2,1,0:T(2,128)S(1)} %bitcast.5, bf16[672,256]{1,0:T(8,128)(2,1)S(1)} %far_factors.1.refs_3_), custom_call_target="tpu_custom_call" | custom-call | flops 570000000 | bytes 1024 | tf_op jit(solution)/shard_map/head_grads/pallas_call | solution.py:80
  23.2 1.5 collective-permute-start.5
  24.7 2.1 %head_grads.3.refs_3_.refs_0_ = bf16[3808,128]{1,0:T(8,128)(2,1)S(1)} custom-call(bf16[2192,256]{1,0:T(8,128)(2,1)S(1)} %copy-done, bf16[2192,256]{1,0:T(8,128)(2,1)S(1)} %collective-permute-done.refs_0_.refs_1_, f32[3,2,1792]{2,1,0:T(2,128)S(1)} %bitcast.6, bf16[3808,128]{1,0:T(8,128)(2,1)S(1)} %head_grads.2.refs_3_, ...), custom_call_target="tpu_custom_call" | custom-call | flops 570000000 | bytes 1024 | tf_op jit(solution)/shard_map/head_grads/pallas_call | solution.py:80
  27.0 3.4 %back.2.refs_2_.refs_0_ = bf16[672,256]{1,0:T(8,128)(2,1)S(1)} custom-call(bf16[672,256]{1,0:T(8,128)(2,1)S(1)} %copy-done.4, bf16[2,4608,512]{2,1,0:T(8,128)(2,1)} %bitcast.9, f32[336,512]{1,0:T(8,128)S(1)} %copy-done.3, bf16[3808,128]{1,0:T(8,128)(2,1)S(1)} %head_grads.3.refs_3_.refs_0_, bf16[672,256]{1,0:T(8,128)(2,1)S(1)} %collective-permute-done.2.refs_4_.refs_3_), custom_call_target="tpu_custom_call" | custom-call | flops 1500000000 | bytes 1024 | tf_op jit(solution)/shard_map/back/pallas_call | solution.py:80
  30.4 1.6 collective-permute-done.3.refs_3_
  32.1 1.8 first_factors.1.refs_2_
  33.9 2.2 %collective-permute-start.4 = (bf16[1344,256]{1,0:T(8,128)(2,1)S(1)}, bf16[1344,256]{1,0:T(8,128)(2,1)S(1)}, u32[]{:S(2)}, u32[]{:S(2)}) collective-permute-start(bf16[1344,256]{1,0:T(8,128)(2,1)S(1)} %first_factors.1.refs_2_), channel_id=1, source_target_pairs={{0,4},{1,3},{2,6},{3,1},{4,0},{5,7},{6,2},{7,5},{8,12},{9,11},{10,... | collective-permute-start | bytes 2064392 | tf_op jit(solution)/shard_map/ppermute | solution.py:1133
  36.1 1.2 collective-permute-done.5.refs_1_
  37.5 1.7 collective-permute-start.6
  39.2 4.3 %late_grads.1 = (bf16[2304,128]{1,0:T(8,128)(2,1)S(1)}, bf16[2304,128]{1,0:T(8,128)(2,1)S(1)}) custom-call(bf16[2192,256]{1,0:T(8,128)(2,1)S(1)} %copy-done, bf16[2192,256]{1,0:T(8,128)(2,1)S(1)} %collective-permute-done.refs_0_.refs_1_, bf16[672,256]{1,0:T(8,128)(2,1)S(1)} %collective-permute-done.1.refs_4_.refs_2_, ...), custom_call_target="tpu_custom_call" | custom-call | flops 1440000000 | bytes 1024 | tf_op jit(solution)/shard_map/late_grads/pallas_call | solution.py:80
  43.5 1.5 collective-permute-start.9
  45.0 7.2 %collective-permute-done.6.refs_1_ = bf16[2016,128]{1,0:T(8,128)(2,1)S(1)} collective-permute-done((bf16[2016,128]{1,0:T(8,128)(2,1)S(1)}, bf16[2016,128]{1,0:T(8,128)(2,1)S(1)}, u32[]{:S(2)}, u32[]{:S(2)}) %collective-permute-start.6) | collective-permute-done | bytes 516128 | tf_op jit(solution)/shard_map/ppermute | solution.py:1133
  52.4 4.0 %early_grads.1 = (bf16[2304,128]{1,0:T(8,128)(2,1)S(1)}, bf16[2304,128]{1,0:T(8,128)(2,1)S(1)}) custom-call(bf16[2192,256]{1,0:T(8,128)(2,1)S(1)} %copy-done, bf16[2192,256]{1,0:T(8,128)(2,1)S(1)} %collective-permute-done.refs_0_.refs_1_, bf16[672,256]{1,0:T(8,128)(2,1)S(1)} %back.2.refs_2_.refs_0_, bf16[672,256]{1,0:T(8,128)(2,1)S(1)} %collective-permute-done.3.refs_3_, ...), custom_call_target="tpu_custom_call" | custom-call | flops 1140000000 | bytes 1024 | tf_op jit(solution)/shard_map/early_grads/pallas_call | solution.py:80
  56.4 1.7 collective-permute-start.7
  58.1 1.6 collective-permute-start.8
  60.3 13.6 %collective-permute-done.8.refs_1_ = bf16[1120,128]{1,0:T(8,128)(2,1)S(1)} collective-permute-done((bf16[1120,128]{1,0:T(8,128)(2,1)S(1)}, bf16[1120,128]{1,0:T(8,128)(2,1)S(1)}, u32[]{:S(2)}, u32[]{:S(2)}) %collective-permute-start.8) | collective-permute-done | bytes 286752 | tf_op jit(solution)/shard_map/ppermute | solution.py:1133
  74.0 1.3 collective-permute-start.11
  75.4 1.6 collective-permute-start.10
  77.0 1.5 collective-permute-done.12.refs_1_
  78.6 1.3 collective-permute-start.15
  79.9 15.6 %collective-permute-done.11.refs_1_ = bf16[1120,128]{1,0:T(8,128)(2,1)S(1)} collective-permute-done((bf16[1120,128]{1,0:T(8,128)(2,1)S(1)}, bf16[1120,128]{1,0:T(8,128)(2,1)S(1)}, u32[]{:S(2)}, u32[]{:S(2)}) %collective-permute-start.11) | collective-permute-done | bytes 286752 | tf_op jit(solution)/shard_map/ppermute | solution.py:1133
  95.7 2.0 %collective-permute-start.17 = (bf16[1152,128]{1,0:T(8,128)(2,1)S(1)}, bf16[1152,128]{1,0:T(8,128)(2,1)S(1)}, u32[]{:S(2)}, u32[]{:S(2)}) collective-permute-start(bf16[1152,128]{1,0:T(8,128)(2,1)S(1)} %summed.17.refs_4_.refs_0_), channel_id=1, source_target_pairs={{0,8},{1,9},{2,10},{3,11},{4,12},{5,13},{6,14},{7,15},{8,0},{9,1},... | collective-permute-start | bytes 884744 | tf_op jit(solution)/shard_map/ppermute | solution.py:1133
  97.7 3.4 %back.3 = (f32[336,256]{1,0:T(8,128)S(1)}, bf16[1120,128]{1,0:T(8,128)(2,1)S(1)}) custom-call(bf16[672,256]{1,0:T(8,128)(2,1)S(1)} %back.2.refs_2_.refs_0_, bf16[2,4608,512]{2,1,0:T(8,128)(2,1)} %bitcast.10, f32[336,512]{1,0:T(8,128)S(1)} %copy-done.2, bf16[64,1792]{1,0:T(8,128)(2,1)S(1)} %copy-done.1, bf16[1152,128]{1,0:T(8,128)(2,1)S(1)} %summed.17.refs_4_.refs_0_), custom_call_target="tpu_custom_call" | custom-call | flops 1500000000 | bytes 1024 | tf_op jit(solution)/shard_map/back/pallas_call | solution.py:80
  101.3 7.0 %collective-permute-done.18.refs_1_ = bf16[1120,128]{1,0:T(8,128)(2,1)S(1)} collective-permute-done((bf16[1120,128]{1,0:T(8,128)(2,1)S(1)}, bf16[1120,128]{1,0:T(8,128)(2,1)S(1)}, u32[]{:S(2)}, u32[]{:S(2)}) %collective-permute-start.18) | collective-permute-done | bytes 286752 | tf_op jit(solution)/shard_map/ppermute | solution.py:1133
  108.9 1.2 collective-permute-start.20
  110.2 5.4 %collective-permute-done.16.refs_1_ = bf16[1152,128]{1,0:T(8,128)(2,1)S(1)} collective-permute-done((bf16[1152,128]{1,0:T(8,128)(2,1)S(1)}, bf16[1152,128]{1,0:T(8,128)(2,1)S(1)}, u32[]{:S(2)}, u32[]{:S(2)}) %collective-permute-start.16) | collective-permute-done | bytes 294944 | tf_op jit(solution)/shard_map/ppermute | solution.py:1133
  115.6 1.2 collective-permute-start.19
  116.8 4.2 %collective-permute-done.21.refs_1_ = bf16[1792,128]{1,0:T(8,128)(2,1)S(1)} collective-permute-done((bf16[1792,128]{1,0:T(8,128)(2,1)S(1)}, bf16[1792,128]{1,0:T(8,128)(2,1)S(1)}, u32[]{:S(2)}, u32[]{:S(2)}) %collective-permute-start.21) | collective-permute-done | bytes 458784 | tf_op jit(solution)/shard_map/ppermute | solution.py:1133
  121.2 1.2 collective-permute-start.22
  122.4 1.1 collective-permute-start.13
  123.5 5.5 %collective-permute-done.19.refs_1_ = bf16[2304,128]{1,0:T(8,128)(2,1)S(1)} collective-permute-done((bf16[2304,128]{1,0:T(8,128)(2,1)S(1)}, bf16[2304,128]{1,0:T(8,128)(2,1)S(1)}, u32[]{:S(2)}, u32[]{:S(2)}) %collective-permute-start.19) | collective-permute-done | bytes 589856 | tf_op jit(solution)/shard_map/ppermute | solution.py:1133
  129.0 4.4 %collective-permute-start.25 = (bf16[4608,128]{1,0:T(8,128)(2,1)S(1)}, bf16[4608,128]{1,0:T(8,128)(2,1)S(1)}, u32[]{:S(2)}, u32[]{:S(2)}) collective-permute-start(bf16[4608,128]{1,0:T(8,128)(2,1)S(1)} %paired.10.refs_6_.refs_0_), channel_id=1, source_target_pairs={{0,2},{1,17},{2,0},{3,19},{4,6},{5,21},{6,4},{7,23},{8,10},{9,25},... | collective-permute-start | bytes 3538952 | tf_op jit(solution)/shard_map/ppermute | solution.py:1133
  133.4 1.7 collective-permute-done.13.refs_3_
  135.1 1.7 finish.1
  136.9 0.9 copy-done.5
  138.0 1.1 collective-permute-start.30
  139.5 17.5 %collective-permute-done.25.refs_4_.refs_0_ = bf16[4608,128]{1,0:T(8,128)(2,1)S(1)} collective-permute-done((bf16[4608,128]{1,0:T(8,128)(2,1)S(1)}, bf16[4608,128]{1,0:T(8,128)(2,1)S(1)}, u32[]{:S(2)}, u32[]{:S(2)}) %collective-permute-start.25) | collective-permute-done | bytes 1179680 | tf_op jit(solution)/shard_map/ppermute | solution.py:1133
  157.6 4.4 %collective-permute-done.23.refs_4_.refs_0_ = bf16[4608,128]{1,0:T(8,128)(2,1)S(1)} collective-permute-done((bf16[4608,128]{1,0:T(8,128)(2,1)S(1)}, bf16[4608,128]{1,0:T(8,128)(2,1)S(1)}, u32[]{:S(2)}, u32[]{:S(2)}) %collective-permute-start.23) | collective-permute-done | bytes 1179680 | tf_op jit(solution)/shard_map/ppermute | solution.py:1133
  161.9 4.4 %widen_heads.2 = (f32[2,512,1792]{2,1,0:T(8,128)}, f32[8,128]{1,0:T(8,128)S(1)}) custom-call(bf16[3584,128]{1,0:T(8,128)(2,1)S(1)} %paired.8.refs_2_.refs_0_, bf16[3584,128]{1,0:T(8,128)(2,1)S(1)} %collective-permute-done.29.refs_1_, bf16[4608,128]{1,0:T(8,128)(2,1)S(1)} %paired.11.refs_2_.refs_0_), custom_call_target="tpu_custom_call" | custom-call | flops 1320000000 | bytes 1024 | tf_op jit(solution)/shard_map/widen_heads/pallas_call | solution.py:80
  166.3 2.9 %widen_trunk.5 = (f32[2,9,512,512]{3,2,1,0:T(8,128)}, f32[8,128]{1,0:T(8,128)S(1)}) custom-call(bf16[4608,128]{1,0:T(8,128)(2,1)S(1)} %paired.10.refs_6_.refs_0_, bf16[4608,128]{1,0:T(8,128)(2,1)S(1)} %collective-permute-done.28.refs_1_, f32[8,128]{1,0:T(8,128)S(1)} %get-tuple-element.67.refs_2_), custom_call_target="tpu_custom_call" | custom-call | flops 870000000 | bytes 1024 | tf_op jit(solution)/shard_map/widen_trunk/pallas_call | solution.py:80
  169.2 2.9 %widen_trunk.6 = (f32[2,9,512,512]{3,2,1,0:T(8,128)}, f32[8,128]{1,0:T(8,128)S(1)}) custom-call(bf16[4608,128]{1,0:T(8,128)(2,1)S(1)} %paired.11.refs_2_.refs_0_, bf16[4608,128]{1,0:T(8,128)(2,1)S(1)} %collective-permute-done.27.refs_1_, f32[2,9,512,512]{3,2,1,0:T(8,128)} %get-tuple-element.68.refs_2_, ...), custom_call_target="tpu_custom_call", output_to_operand_aliasing={{0}: (2, {})} | custom-call | flops 870000000 | bytes 1024 | tf_op jit(solution)/shard_map/widen_trunk/pallas_call | solution.py:80
  172.1 4.4 %widen_heads.3 = (f32[2,512,1792]{2,1,0:T(8,128)}, f32[8,128]{1,0:T(8,128)S(1)}) custom-call(bf16[3584,128]{1,0:T(8,128)(2,1)S(1)} %collective-permute-done.30.refs_4_.refs_0_, bf16[3584,128]{1,0:T(8,128)(2,1)S(1)} %collective-permute-done.31.refs_1_, f32[2,512,1792]{2,1,0:T(8,128)} %get-tuple-element.71.refs_2_, ...), custom_call_target="tpu_custom_call", output_to_operand_aliasing={{0}: (2, {})} | custom-call | flops 1320000000 | bytes 1024 | tf_op jit(solution)/shard_map/widen_heads/pallas_call | solution.py:80
  176.5 2.9 %widen_trunk.7 = (f32[2,9,512,512]{3,2,1,0:T(8,128)}, f32[8,128]{1,0:T(8,128)S(1)}) custom-call(bf16[4608,128]{1,0:T(8,128)(2,1)S(1)} %collective-permute-done.25.refs_4_.refs_0_, bf16[4608,128]{1,0:T(8,128)(2,1)S(1)} %collective-permute-done.26.refs_1_, f32[2,9,512,512]{3,2,1,0:T(8,128)} %get-tuple-element.70.refs_2_, ...), custom_call_target="tpu_custom_call", output_to_operand_aliasing={{0}: (2, {})} | custom-call | flops 870000000 | bytes 1024 | tf_op jit(solution)/shard_map/widen_trunk/pallas_call | solution.py:80
  179.4 1.8 widen_trunk.8
  181.2 2.4 %widen_trunk.9 = (f32[2,9,512,512]{3,2,1,0:T(8,128)}, f32[8,128]{1,0:T(8,128)}) custom-call(bf16[4608,128]{1,0:T(8,128)(2,1)S(1)} %collective-permute-done.24.refs_0_, f32[2,9,512,512]{3,2,1,0:T(8,128)} %get-tuple-element.76.refs_1_, f32[8,128]{1,0:T(8,128)S(1)} %get-tuple-element.77.refs_2_), custom_call_target="tpu_custom_call", output_to_operand_aliasing={{0}: (1, {})} | custom-call | flops 870000000 | bytes 1024 | tf_op jit(solution)/shard_map/widen_trunk/pallas_call | solution.py:80
  (65 shorter events, 4.8 us)
Async XLA Ops:
  14.8 6.3 %copy-start = (bf16[2192,256]{1,0:T(8,128)(2,1)S(1)}, bf16[2192,256]{1,0:T(8,128)(2,1)}, u32[]{:S(2)}) copy-start(bf16[2192,256]{1,0:T(8,128)(2,1)} %get-tuple-element.46.refs_0_) | copy-start | bytes 3366916
  14.8 6.3 %copy-start.6 = (f32[2,3,1792]{2,0,1:T(2,128)S(1)}, f32[2,3,1792]{2,0,1:T(2,128)}, u32[]{:S(2)}) copy-start(f32[2,3,1792]{2,0,1:T(2,128)} %param.16) | copy-start | bytes 129028
  14.8 3.1 %collective-permute-start = (bf16[2192,256]{1,0:T(8,128)(2,1)}, bf16[2192,256]{1,0:T(8,128)(2,1)S(1)}, u32[]{:S(2)}, u32[]{:S(2)}) collective-permute-start(bf16[2192,256]{1,0:T(8,128)(2,1)} %get-tuple-element.47), channel_id=1, source_target_pairs={{0,1},{1,0},{2,3},{3,2},{4,5},{5,4},{6,7},{7,6},{8,9},{9,8},{10,11... | collective-permute-start | bytes 3366920 | tf_op jit(solution)/shard_map/ppermute | solution.py:1136
  15.3 9.5 %collective-permute-start.1 = (bf16[672,256]{1,0:T(8,128)(2,1)}, bf16[672,256]{1,0:T(8,128)(2,1)S(1)}, u32[]{:S(2)}, u32[]{:S(2)}) collective-permute-start(bf16[672,256]{1,0:T(8,128)(2,1)} %get-tuple-element.48), channel_id=1, source_target_pairs={{0,2},{1,17},{2,0},{3,19},{4,6},{5,21},{6,4},{7,23},{8,10},{9,25},... | collective-permute-start | bytes 1032200 | tf_op jit(solution)/shard_map/ppermute | solution.py:1133
  18.1 8.8 %collective-permute-start.2 = (bf16[672,256]{1,0:T(8,128)(2,1)S(1)}, bf16[672,256]{1,0:T(8,128)(2,1)S(1)}, u32[]{:S(2)}, u32[]{:S(2)}) collective-permute-start(bf16[672,256]{1,0:T(8,128)(2,1)S(1)} %far_factors.1.refs_3_), channel_id=1, source_target_pairs={{0,2},{1,17},{2,0},{3,19},{4,6},{5,21},{6,4},{7,23},{8,10},{9,25},... | collective-permute-start | bytes 1032200 | tf_op jit(solution)/shard_map/ppermute | solution.py:1133
  23.2 3.8 %copy-start.3 = (f32[336,512]{1,0:T(8,128)S(1)}, f32[336,512]{1,0:T(8,128)}, u32[]{:S(2)}) copy-start(f32[336,512]{1,0:T(8,128)} %get-tuple-element.45.refs_2_) | copy-start | bytes 2064388
  23.2 3.8 %copy-start.4 = (bf16[672,256]{1,0:T(8,128)(2,1)S(1)}, bf16[672,256]{1,0:T(8,128)(2,1)}, u32[]{:S(2)}) copy-start(bf16[672,256]{1,0:T(8,128)(2,1)} %get-tuple-element.44.refs_0_) | copy-start | bytes 1032196
  23.2 14.1 %collective-permute-start.5 = (bf16[3808,128]{1,0:T(8,128)(2,1)S(1)}, bf16[3808,128]{1,0:T(8,128)(2,1)S(1)}, u32[]{:S(2)}, u32[]{:S(2)}) collective-permute-start(bf16[3808,128]{1,0:T(8,128)(2,1)S(1)} %head_grads.2.refs_3_), channel_id=1, source_target_pairs={{0,16},{1,5},{2,18},{3,7},{4,20},{5,1},{6,22},{7,3},{8,24},{9,13},... | collective-permute-start | bytes 2924552 | tf_op jit(solution)/shard_map/ppermute | solution.py:1133
  30.4 1.7 collective-permute-start.3
  33.9 18.5 %collective-permute-start.4 = (bf16[1344,256]{1,0:T(8,128)(2,1)S(1)}, bf16[1344,256]{1,0:T(8,128)(2,1)S(1)}, u32[]{:S(2)}, u32[]{:S(2)}) collective-permute-start(bf16[1344,256]{1,0:T(8,128)(2,1)S(1)} %first_factors.1.refs_2_), channel_id=1, source_target_pairs={{0,4},{1,3},{2,6},{3,1},{4,0},{5,7},{6,2},{7,5},{8,12},{9,11},{10,... | collective-permute-start | bytes 2064392 | tf_op jit(solution)/shard_map/ppermute | solution.py:1133
  37.5 14.8 %collective-permute-start.6 = (bf16[2016,128]{1,0:T(8,128)(2,1)S(1)}, bf16[2016,128]{1,0:T(8,128)(2,1)S(1)}, u32[]{:S(2)}, u32[]{:S(2)}) collective-permute-start(bf16[2016,128]{1,0:T(8,128)(2,1)S(1)} %get-tuple-element.52), channel_id=1, source_target_pairs={{0,2},{1,17},{2,0},{3,19},{4,6},{5,21},{6,4},{7,23},{8,10},{9,25},... | collective-permute-start | bytes 1548296 | tf_op jit(solution)/shard_map/ppermute | solution.py:1133
  43.5 16.2 %collective-permute-start.9 = (bf16[2304,128]{1,0:T(8,128)(2,1)S(1)}, bf16[2304,128]{1,0:T(8,128)(2,1)S(1)}, u32[]{:S(2)}, u32[]{:S(2)}) collective-permute-start(bf16[2304,128]{1,0:T(8,128)(2,1)S(1)} %get-tuple-element.58), channel_id=1, source_target_pairs={{0,16},{1,3},{2,18},{3,1},{4,20},{5,7},{6,22},{7,5},{8,24},{9,11},... | collective-permute-start | bytes 1769480 | tf_op jit(solution)/shard_map/ppermute | solution.py:1133
  56.4 18.9 %collective-permute-start.7 = (bf16[2304,128]{1,0:T(8,128)(2,1)S(1)}, bf16[2304,128]{1,0:T(8,128)(2,1)S(1)}, u32[]{:S(2)}, u32[]{:S(2)}) collective-permute-start(bf16[2304,128]{1,0:T(8,128)(2,1)S(1)} %get-tuple-element.56), channel_id=1, source_target_pairs={{0,2},{1,17},{2,0},{3,19},{4,6},{5,21},{6,4},{7,23},{8,10},{9,25},... | collective-permute-start | bytes 1769480 | tf_op jit(solution)/shard_map/ppermute | solution.py:1133
  58.1 15.8 %collective-permute-start.8 = (bf16[1120,128]{1,0:T(8,128)(2,1)S(1)}, bf16[1120,128]{1,0:T(8,128)(2,1)S(1)}, u32[]{:S(2)}, u32[]{:S(2)}) collective-permute-start(bf16[1120,128]{1,0:T(8,128)(2,1)S(1)} %get-tuple-element.57), channel_id=1, source_target_pairs={{0,4},{1,3},{2,6},{3,1},{4,0},{5,7},{6,2},{7,5},{8,12},{9,11},{10,... | collective-permute-start | bytes 860168 | tf_op jit(solution)/shard_map/ppermute | solution.py:1133
  59.8 18.8 %collective-permute-start.12 = (bf16[1152,128]{1,0:T(8,128)(2,1)S(1)}, bf16[1152,128]{1,0:T(8,128)(2,1)S(1)}, u32[]{:S(2)}, u32[]{:S(2)}) collective-permute-start(bf16[1152,128]{1,0:T(8,128)(2,1)S(1)} %get-tuple-element.62), channel_id=1, source_target_pairs={{0,4},{1,5},{2,6},{3,7},{4,0},{5,1},{6,2},{7,3},{8,12},{9,13},{10,... | collective-permute-start | bytes 884744 | tf_op jit(solution)/shard_map/ppermute | solution.py:1133
  74.0 21.5 %collective-permute-start.11 = (bf16[1120,128]{1,0:T(8,128)(2,1)S(1)}, bf16[1120,128]{1,0:T(8,128)(2,1)S(1)}, u32[]{:S(2)}, u32[]{:S(2)}) collective-permute-start(bf16[1120,128]{1,0:T(8,128)(2,1)S(1)} %summed.13.refs_2_.refs_0_), channel_id=1, source_target_pairs={{0,8},{1,9},{2,10},{3,11},{4,12},{5,13},{6,14},{7,15},{8,0},{9,1},... | collective-permute-start | bytes 860168 | tf_op jit(solution)/shard_map/ppermute | solution.py:1133
  75.4 20.2 %collective-permute-start.10 = (bf16[1152,128]{1,0:T(8,128)(2,1)S(1)}, bf16[1152,128]{1,0:T(8,128)(2,1)S(1)}, u32[]{:S(2)}, u32[]{:S(2)}) collective-permute-start(bf16[1152,128]{1,0:T(8,128)(2,1)S(1)} %get-tuple-element.61), channel_id=1, source_target_pairs={{0,16},{1,5},{2,18},{3,7},{4,20},{5,1},{6,22},{7,3},{8,24},{9,13},... | collective-permute-start | bytes 884744 | tf_op jit(solution)/shard_map/ppermute | solution.py:1133
  78.6 19.1 %copy-start.1 = (bf16[64,1792]{1,0:T(8,128)(2,1)S(1)}, bf16[64,1792]{1,0:T(8,128)(2,1)}, u32[]{:S(2)}) copy-start(bf16[64,1792]{1,0:T(8,128)(2,1)} %get-tuple-element.50.refs_3_.refs_2_) | copy-start | bytes 688132
  78.6 19.1 %copy-start.2 = (f32[336,512]{1,0:T(8,128)S(1)}, f32[336,512]{1,0:T(8,128)}, u32[]{:S(2)}) copy-start(f32[336,512]{1,0:T(8,128)} %get-tuple-element.49.refs_2_) | copy-start | bytes 2064388
  78.6 22.5 %collective-permute-start.15 = (bf16[1152,128]{1,0:T(8,128)(2,1)S(1)}, bf16[1152,128]{1,0:T(8,128)(2,1)S(1)}, u32[]{:S(2)}, u32[]{:S(2)}) collective-permute-start(bf16[1152,128]{1,0:T(8,128)(2,1)S(1)} %summed.15.refs_2_.refs_0_), channel_id=1, source_target_pairs={{0,8},{1,9},{2,10},{3,11},{4,12},{5,13},{6,14},{7,15},{8,0},{9,1},... | collective-permute-start | bytes 884744 | tf_op jit(solution)/shard_map/ppermute | solution.py:1133
  95.6 12.7 %collective-permute-start.18 = (bf16[1120,128]{1,0:T(8,128)(2,1)S(1)}, bf16[1120,128]{1,0:T(8,128)(2,1)S(1)}, u32[]{:S(2)}, u32[]{:S(2)}) collective-permute-start(bf16[1120,128]{1,0:T(8,128)(2,1)S(1)} %summed.16.refs_2_.refs_0_.refs_4_), channel_id=1, source_target_pairs={{0,4},{1,3},{2,6},{3,1},{4,0},{5,7},{6,2},{7,5},{8,12},{9,11},{10,... | collective-permute-start | bytes 860168 | tf_op jit(solution)/shard_map/ppermute | solution.py:1133
  95.7 13.1 %collective-permute-start.17 = (bf16[1152,128]{1,0:T(8,128)(2,1)S(1)}, bf16[1152,128]{1,0:T(8,128)(2,1)S(1)}, u32[]{:S(2)}, u32[]{:S(2)}) collective-permute-start(bf16[1152,128]{1,0:T(8,128)(2,1)S(1)} %summed.17.refs_4_.refs_0_), channel_id=1, source_target_pairs={{0,8},{1,9},{2,10},{3,11},{4,12},{5,13},{6,14},{7,15},{8,0},{9,1},... | collective-permute-start | bytes 884744 | tf_op jit(solution)/shard_map/ppermute | solution.py:1133
  108.3 12.8 %collective-permute-start.21 = (bf16[1792,128]{1,0:T(8,128)(2,1)S(1)}, bf16[1792,128]{1,0:T(8,128)(2,1)S(1)}, u32[]{:S(2)}, u32[]{:S(2)}) collective-permute-start(bf16[1792,128]{1,0:T(8,128)(2,1)S(1)} %paired.6.refs_2_.refs_0_), channel_id=1, source_target_pairs={{0,2},{1,17},{2,0},{3,19},{4,6},{5,21},{6,4},{7,23},{8,10},{9,25},... | collective-permute-start | bytes 1376264 | tf_op jit(solution)/shard_map/ppermute | solution.py:1133
  108.9 6.7 %collective-permute-start.16 = (bf16[1152,128]{1,0:T(8,128)(2,1)S(1)}, bf16[1152,128]{1,0:T(8,128)(2,1)S(1)}, u32[]{:S(2)}, u32[]{:S(2)}) collective-permute-start(bf16[1152,128]{1,0:T(8,128)(2,1)S(1)} %summed.18.refs_2_.refs_0_), channel_id=1, source_target_pairs={{0,4},{1,5},{2,6},{3,7},{4,0},{5,1},{6,2},{7,3},{8,12},{9,13},{10,... | collective-permute-start | bytes 884744 | tf_op jit(solution)/shard_map/ppermute | solution.py:1133
  108.9 12.2 %collective-permute-start.20 = (bf16[1152,128]{1,0:T(8,128)(2,1)S(1)}, bf16[1152,128]{1,0:T(8,128)(2,1)S(1)}, u32[]{:S(2)}, u32[]{:S(2)}) collective-permute-start(bf16[1152,128]{1,0:T(8,128)(2,1)S(1)} %summed.19.refs_2_.refs_0_), channel_id=1, source_target_pairs={{0,16},{1,5},{2,18},{3,7},{4,20},{5,1},{6,22},{7,3},{8,24},{9,13},... | collective-permute-start | bytes 884744 | tf_op jit(solution)/shard_map/ppermute | solution.py:1133
  115.6 13.3 %collective-permute-start.19 = (bf16[2304,128]{1,0:T(8,128)(2,1)S(1)}, bf16[2304,128]{1,0:T(8,128)(2,1)S(1)}, u32[]{:S(2)}, u32[]{:S(2)}) collective-permute-start(bf16[2304,128]{1,0:T(8,128)(2,1)S(1)} %paired.7.refs_2_.refs_0_), channel_id=1, source_target_pairs={{0,16},{1,3},{2,18},{3,1},{4,20},{5,7},{6,22},{7,5},{8,24},{9,11},... | collective-permute-start | bytes 1769480 | tf_op jit(solution)/shard_map/ppermute | solution.py:1133
  121.2 15.7 %collective-permute-start.22 = (bf16[2304,128]{1,0:T(8,128)(2,1)S(1)}, bf16[2304,128]{1,0:T(8,128)(2,1)S(1)}, u32[]{:S(2)}, u32[]{:S(2)}) collective-permute-start(bf16[2304,128]{1,0:T(8,128)(2,1)S(1)} %paired.9.refs_2_.refs_0_), channel_id=1, source_target_pairs={{0,2},{1,17},{2,0},{3,19},{4,6},{5,21},{6,4},{7,23},{8,10},{9,25},... | collective-permute-start | bytes 1769480 | tf_op jit(solution)/shard_map/ppermute | solution.py:1133
  122.4 11.0 %collective-permute-start.14 = (bf16[1120,128]{1,0:T(8,128)(2,1)S(1)}, bf16[1120,128]{1,0:T(8,128)(2,1)S(1)}, u32[]{:S(2)}, u32[]{:S(2)}) collective-permute-start(bf16[1120,128]{1,0:T(8,128)(2,1)S(1)} %summed.16.refs_2_.refs_0_.refs_4_), channel_id=1, source_target_pairs={{0,1},{1,0},{2,3},{3,2},{4,5},{5,4},{6,7},{7,6},{8,9},{9,8},{10,11... | collective-permute-start | bytes 860168 | tf_op jit(solution)/shard_map/ppermute | solution.py:1136
  122.4 12.7 %copy-start.7 = (s32[1,2]{1,0:T(1,128)S(1)}, s32[1,2]{1,0:T(1,128)}, u32[]{:S(2)}) copy-start(s32[1,2]{1,0:T(1,128)} %refs_0_.3) | copy-start | bytes 28
  122.4 12.7 %collective-permute-start.13 = (bf16[1120,128]{1,0:T(8,128)(2,1)S(1)}, bf16[1120,128]{1,0:T(8,128)(2,1)S(1)}, u32[]{:S(2)}, u32[]{:S(2)}) collective-permute-start(bf16[1120,128]{1,0:T(8,128)(2,1)S(1)} %get-tuple-element.64), channel_id=1, source_target_pairs={{0,16},{16,0},{1,17},{17,1},{2,18},{18,2},{3,19},{19,3},{4,20},{20... | collective-permute-start | bytes 860168 | tf_op jit(solution)/shard_map/ppermute | solution.py:1178
  129.0 28.0 %collective-permute-start.25 = (bf16[4608,128]{1,0:T(8,128)(2,1)S(1)}, bf16[4608,128]{1,0:T(8,128)(2,1)S(1)}, u32[]{:S(2)}, u32[]{:S(2)}) collective-permute-start(bf16[4608,128]{1,0:T(8,128)(2,1)S(1)} %paired.10.refs_6_.refs_0_), channel_id=1, source_target_pairs={{0,2},{1,17},{2,0},{3,19},{4,6},{5,21},{6,4},{7,23},{8,10},{9,25},... | collective-permute-start | bytes 3538952 | tf_op jit(solution)/shard_map/ppermute | solution.py:1133
  133.4 5.6 %collective-permute-start.29 = (bf16[3584,128]{1,0:T(8,128)(2,1)S(1)}, bf16[3584,128]{1,0:T(8,128)(2,1)S(1)}, u32[]{:S(2)}, u32[]{:S(2)}) collective-permute-start(bf16[3584,128]{1,0:T(8,128)(2,1)S(1)} %paired.8.refs_2_.refs_0_), channel_id=1, source_target_pairs={{0,1},{1,0},{2,3},{3,2},{4,5},{5,4},{6,7},{7,6},{8,9},{9,8},{10,11... | collective-permute-start | bytes 2752520 | tf_op jit(solution)/shard_map/ppermute | solution.py:1136
  136.9 0.9 copy-start.5
  137.9 24.1 %collective-permute-start.23 = (bf16[4608,128]{1,0:T(8,128)(2,1)S(1)}, bf16[4608,128]{1,0:T(8,128)(2,1)S(1)}, u32[]{:S(2)}, u32[]{:S(2)}) collective-permute-start(bf16[4608,128]{1,0:T(8,128)(2,1)S(1)} %paired.11.refs_2_.refs_0_), channel_id=1, source_target_pairs={{0,4},{1,3},{2,6},{3,1},{4,0},{5,7},{6,2},{7,5},{8,12},{9,11},{10,... | collective-permute-start | bytes 3538952 | tf_op jit(solution)/shard_map/ppermute | solution.py:1133
  138.0 19.1 %collective-permute-start.30 = (bf16[3584,128]{1,0:T(8,128)(2,1)S(1)}, bf16[3584,128]{1,0:T(8,128)(2,1)S(1)}, u32[]{:S(2)}, u32[]{:S(2)}) collective-permute-start(bf16[3584,128]{1,0:T(8,128)(2,1)S(1)} %paired.8.refs_2_.refs_0_), channel_id=1, source_target_pairs={{0,16},{1,5},{2,18},{3,7},{4,20},{5,1},{6,22},{7,3},{8,24},{9,13},... | collective-permute-start | bytes 2752520 | tf_op jit(solution)/shard_map/ppermute | solution.py:1133
  139.0 27.3 %collective-permute-start.28 = (bf16[4608,128]{1,0:T(8,128)(2,1)S(1)}, bf16[4608,128]{1,0:T(8,128)(2,1)S(1)}, u32[]{:S(2)}, u32[]{:S(2)}) collective-permute-start(bf16[4608,128]{1,0:T(8,128)(2,1)S(1)} %paired.10.refs_6_.refs_0_), channel_id=1, source_target_pairs={{0,1},{1,0},{2,3},{3,2},{4,5},{5,4},{6,7},{7,6},{8,9},{9,8},{10,11... | collective-permute-start | bytes 3538952 | tf_op jit(solution)/shard_map/ppermute | solution.py:1136
  139.0 30.2 %collective-permute-start.27 = (bf16[4608,128]{1,0:T(8,128)(2,1)S(1)}, bf16[4608,128]{1,0:T(8,128)(2,1)S(1)}, u32[]{:S(2)}, u32[]{:S(2)}) collective-permute-start(bf16[4608,128]{1,0:T(8,128)(2,1)S(1)} %paired.11.refs_2_.refs_0_), channel_id=1, source_target_pairs={{0,1},{1,0},{2,3},{3,2},{4,5},{5,4},{6,7},{7,6},{8,9},{9,8},{10,11... | collective-permute-start | bytes 3538952 | tf_op jit(solution)/shard_map/ppermute | solution.py:1136
  157.1 19.5 %collective-permute-start.26 = (bf16[4608,128]{1,0:T(8,128)(2,1)S(1)}, bf16[4608,128]{1,0:T(8,128)(2,1)S(1)}, u32[]{:S(2)}, u32[]{:S(2)}) collective-permute-start(bf16[4608,128]{1,0:T(8,128)(2,1)S(1)} %collective-permute-done.25.refs_4_.refs_0_), channel_id=1, source_target_pairs={{0,1},{1,0},{2,3},{3,2},{4,5},{5,4},{6,7},{7,6},{8,9},{9,8},{10,11... | collective-permute-start | bytes 3538952 | tf_op jit(solution)/shard_map/ppermute | solution.py:1136
  157.1 15.0 %collective-permute-start.31 = (bf16[3584,128]{1,0:T(8,128)(2,1)S(1)}, bf16[3584,128]{1,0:T(8,128)(2,1)S(1)}, u32[]{:S(2)}, u32[]{:S(2)}) collective-permute-start(bf16[3584,128]{1,0:T(8,128)(2,1)S(1)} %collective-permute-done.30.refs_4_.refs_0_), channel_id=1, source_target_pairs={{0,1},{1,0},{2,3},{3,2},{4,5},{5,4},{6,7},{7,6},{8,9},{9,8},{10,11... | collective-permute-start | bytes 2752520 | tf_op jit(solution)/shard_map/ppermute | solution.py:1136
  161.9 19.3 %collective-permute-start.24 = (bf16[4608,128]{1,0:T(8,128)(2,1)S(1)}, bf16[4608,128]{1,0:T(8,128)(2,1)S(1)}, u32[]{:S(2)}, u32[]{:S(2)}) collective-permute-start(bf16[4608,128]{1,0:T(8,128)(2,1)S(1)} %collective-permute-done.23.refs_4_.refs_0_), channel_id=1, source_target_pairs={{0,1},{1,0},{2,3},{3,2},{4,5},{5,4},{6,7},{7,6},{8,9},{9,8},{10,11... | collective-permute-start | bytes 3538952 | tf_op jit(solution)/shard_map/ppermute | solution.py:1136

commit v3 on v2

--- a/solution.py
+++ b/solution.py
@@ -28,9 +28,9 @@
     if piece == HEAD:
         stages = [(two, three), (one, two), (three, one), (four, four)]
     elif piece == LATE:
-        stages = [(one, two), (two, one), (three, three), (four, four)]
+        stages = [(two, three), (one, two), (three, one), (four, four)]
     else:
-        stages = [(three, one), (one, two), (two, three), (four, four)]
+        stages = [(one, three), (two, one), (three, two), (four, four)]
     return stages + [(bit, bit) for bit in range(4, size)]
 
 
@@ -59,8 +59,7 @@
         self.grad = (0, self.span)
         self.normed = self.span + rows
         self.cot = self.normed + 2 * self.stacked
-        self.small = self.cot + self.lanes * self.mid
-        self.feed = self.small + 16 * self.lanes
+        self.feed = self.cot + self.lanes * self.mid
         self.total = self.feed + rows
 
 
@@ -68,26 +67,31 @@
     return pl.BlockSpec(memory_space=memory)
 
 
-def call(
-    kernel, name, mib, cost, operands, in_specs, out_shape, out_specs, scratch=(), after=(), aliases=None
-):
+def call(kernel, name, mib, cost, operands, in_specs, out_shape, out_specs, scratch=(), after=(), aliases=None):
     count = len(operands)
     extra = len(after)
+    several = isinstance(out_shape, tuple)
+    shapes = out_shape if several else (out_shape,)
+    specs = out_specs if several else (out_specs,)
 
     def run(*refs):
-        kernel(*refs[:count], *refs[count + extra :])
-
-    return pl.pallas_call(
+        results = refs[count + extra :]
+        mark = results[len(shapes)]
+        kernel(*refs[:count], *results[: len(shapes)], *results[len(shapes) + 1 :])
+        mark[...] = jnp.zeros(mark.shape, F32)
+
+    *made, mark = pl.pallas_call(
         run,
-        out_shape=out_shape,
+        out_shape=(*shapes, jax.ShapeDtypeStruct((8, 128), F32)),
         in_specs=list(in_specs) + [spec(pl.ANY)] * extra,
-        out_specs=out_specs,
+        out_specs=(*specs, spec(pltpu.VMEM)),
         scratch_shapes=list(scratch),
         input_output_aliases=aliases or {},
         compiler_params=pltpu.CompilerParams(vmem_limit_bytes=mib * MIB),
         cost_estimate=pl.CostEstimate(flops=cost, bytes_accessed=1024, transcendentals=0),
         name=name,
     )(*operands, *after)
+    return (tuple(made) if several else made[0]), mark
 
 
 def grids(side):
@@ -119,44 +123,64 @@
     return first, last
 
 
-def column_shifts(value, side, target):
+def column_shifts(value, side, low, high):
     first, last = edge_masks(side)
     rows = value.shape[0]
-    target[0] = jnp.where(first, 0.0, pltpu.roll(value, 1, 0))
-    target[1] = value
-    target[2] = jnp.where(last, 0.0, pltpu.roll(value, rows - 1, 0))
-
-
-def row_shift(shifted, b, a, side):
-    parts = []
-    width = shifted.shape[2]
+    fine = side * side
+    for b, one in enumerate(
+        (
+            jnp.where(first, 0.0, pltpu.roll(value, 1, 0)),
+            value,
+            jnp.where(last, 0.0, pltpu.roll(value, rows - 1, 0)),
+        )
+    ):
+        low[b] = one[:fine].astype(BF16)
+        high[b] = one[fine:]
+
+
+def put_row_shift(target, row_start, lane_start, low, high, b, a, side):
+    width = low.shape[2]
+    lanes = slice(lane_start, lane_start + width)
+    fine = side * side
     for start, extent in grids(side):
         count = extent * extent
+        row = row_start + start
+        if start == 0:
+            blank = jnp.zeros((extent, width), BF16)
+            if a == 1:
+                target[row : row + count, lanes] = low[b]
+            elif a == 0:
+                target[row : row + extent, lanes] = blank
+                target[row + extent : row + count, lanes] = low[b, : count - extent, :]
+            else:
+                target[row : row + count - extent, lanes] = low[b, extent:, :]
+                target[row + count - extent : row + count, lanes] = blank
+            continue
+        start -= fine
         if a == 1:
-            part = shifted[b, start : start + count, :]
+            part = high[b, start : start + count, :]
         elif extent % 8 == 0:
             blank = jnp.zeros((extent, width), F32)
             if a == 0:
-                part = jnp.concatenate([blank, shifted[b, start : start + count - extent, :]], axis=0)
+                part = jnp.concatenate([blank, high[b, start : start + count - extent, :]], axis=0)
             else:
-                part = jnp.concatenate([shifted[b, start + extent : start + count, :], blank], axis=0)
+                part = jnp.concatenate([high[b, start + extent : start + count, :], blank], axis=0)
         else:
-            whole = shifted[b, start : start + count, :]
-            row = iota((count, 1), 0)
+            whole = high[b, start : start + count, :]
+            at = iota((count, 1), 0)
             if a == 0:
-                part = jnp.where(row < extent, 0.0, pltpu.roll(whole, extent, 0))
+                part = jnp.where(at < extent, 0.0, pltpu.roll(whole, extent, 0))
             else:
-                part = jnp.where(row >= count - extent, 0.0, pltpu.roll(whole, count - extent, 0))
-        parts.append(part.astype(BF16))
-    return parts
-
-
-def put_row_shift(target, row_start, lane_start, shifted, b, a, side):
-    width = shifted.shape[2]
-    for (start, extent), part in zip(grids(side), row_shift(shifted, b, a, side)):
-        target[
-            row_start + start : row_start + start + extent * extent, lane_start : lane_start + width
-        ] = part
+                part = jnp.where(at >= count - extent, 0.0, pltpu.roll(whole, count - extent, 0))
+        target[row : row + count, lanes] = part.astype(BF16)
+
+
+def shift_scratch(side, width):
+    fine = side * side
+    return [
+        pltpu.VMEM((3, fine, width), BF16),
+        pltpu.VMEM((3, rows_of(side) - fine, width), F32),
+    ]
 
 
 def dot(left, right):
@@ -168,7 +192,8 @@
 
 
 def block_of(index, extent):
-    return (index // extent // 2) * (extent // 2) + (index % extent) // 2
+    bits = extent.bit_length() - 1
+    return ((index >> (bits + 1)) << (bits - 1)) + ((index & (extent - 1)) >> 1)
 
 
 def pool_matrix(extent, value):
@@ -217,6 +242,17 @@
     for one in made:
         one.start()
     return made
+
+
+def tap_norm(tap):
+    return lax.rsqrt(jnp.mean(tap * tap, axis=-1, keepdims=True) + EPSILON)
+
+
+def tap_backward(tap, r, scale_row, back, wide, mid):
+    back = jnp.concatenate([spread(wide, 0.25 * back[:mid]), back[mid:]], axis=0)
+    upstream = back * scale_row
+    grad = r * (upstream - tap * (r * r) * jnp.mean(upstream * tap, axis=-1, keepdims=True))
+    return grad, jnp.sum(back * tap * r, axis=0, keepdims=True)
 
 
 def section_kernel(
@@ -236,8 +272,8 @@
     pass_out,
     grad_out,
     slope_out,
-    tap_grad_out,
-    merged_out,
+    normed_out,
+    scale_out,
     feed,
     weights,
     heads,
@@ -246,7 +282,8 @@
     shift,
     scale,
     merging,
-    shifted,
+    low_shifted,
+    high_shifted,
     patch,
     sems,
 ):
@@ -254,7 +291,7 @@
     fine = side * side
     channels = feed.shape[1]
     half = channels // 2
-    width = heads.shape[2]
+    width = heads.shape[1]
     at = Layout(side, channels, width)
     mid = at.mid
     pipe = lax.axis_index("pipe")
@@ -269,19 +306,18 @@
             )
             for num in range(6)
         ]
-        + [(cotangent.at[pipe], cot_ref)]
-        + [(head_weight.at[num], heads.at[num]) for num in range(2)]
+        + [(cotangent.at[pipe], cot_ref), (head_weight.at[1], heads)]
         + [(gain_in, gain), (shift_in, shift), (scale_in, scale), (merging_in, merging)],
         sems,
     )
     made[0].wait()
 
     def conv(value, layer):
-        column_shifts(value, side, shifted)
+        column_shifts(value, side, low_shifted, high_shifted)
         total = jnp.zeros((rows, channels), F32)
         for a in range(3):
             for b in range(3):
-                put_row_shift(patch, 0, b * channels, shifted, b, a, side)
+                put_row_shift(patch, 0, b * channels, low_shifted, high_shifted, b, a, side)
             made[1 + 3 * layer + a].wait()
             total = total + dot(patch[...], weights[3 * layer + a])
         return total
@@ -297,7 +333,7 @@
     feed_value = low_feed.astype(F32)
     put_halves(at.feed, low_feed)
     first_pre = conv(feed_value, 0)
-    for num in range(10, 14):
+    for num in range(9, 13):
         made[num].wait()
     act1, slope1 = gelu_and_slope(gain[0:1, :] * first_pre + shift[0:1, :])
     slope_out[...] = slope1 * gain[0:1, :]
@@ -307,52 +343,27 @@
     trunk_out, slope2 = gelu_and_slope(z2)
     taps = [feed_value, trunk_out.astype(BF16).astype(F32)]
 
-    made[7].wait()
-    cot_low = cot_ref[...]
-    cot = cot_low.astype(F32)
-    coarse_cot = dot(pool_matrix(side // 2, 1.0), cot_low)
     pool = pool_matrix(side, 0.25)
-    wide = spread_matrix(side)
-    merged = jnp.zeros((mid, width), F32)
-    coarse_merged = jnp.zeros((at.stacked - 2 * mid, width), F32)
-    small = []
-    scale_rows = []
     for k in range(2):
         tap = taps[k]
-        scale_row = scale[k : k + 1, :]
-        r = lax.rsqrt(jnp.mean(tap * tap, axis=-1, keepdims=True) + EPSILON)
-        normed = (tap * r * scale_row).astype(BF16)
+        r = tap_norm(tap)
+        normed = (tap * r * scale[k : k + 1, :]).astype(BF16)
         pooled = dot(pool, normed[:fine]).astype(BF16)
         rows_k = jnp.concatenate([pooled, normed[fine:]], axis=0)
         put_halves(at.normed + k * at.stacked, rows_k)
-        made[8 + k].wait()
-        product = dot(rows_k, heads[k])
-        weights_k = [merging[s, k : k + 1, :] for s in range(3)]
-        merged = merged + weights_k[0] * product[:mid] + weights_k[1] * product[mid : 2 * mid]
-        coarse_merged = coarse_merged + weights_k[2] * product[2 * mid :]
-        small.append(jnp.sum(cot * product[:mid], axis=0, keepdims=True))
-        small.append(jnp.sum(cot * product[mid : 2 * mid], axis=0, keepdims=True))
-        small.append(jnp.sum(coarse_cot * product[2 * mid :], axis=0, keepdims=True))
-        grads = head_cotangents(cot, coarse_cot, weights_k)
-        back = dot_last(grads, heads[k])
-        back = jnp.concatenate([spread(wide, 0.25 * back[:mid]), back[mid:]], axis=0)
-        upstream = back * scale_row
-        tap_grad = r * (
-            upstream - tap * (r * r) * jnp.mean(upstream * tap, axis=-1, keepdims=True)
-        )
-        scale_rows.append(jnp.sum(back * tap * r, axis=0, keepdims=True))
-        if k == 0:
-            tap_grad_out[...] = tap_grad
-    small.append(
-        jnp.concatenate(scale_rows + [jnp.zeros((1, width - 2 * channels), F32)], axis=1)
-    )
-    small.append(jnp.zeros((1, width), F32))
-    small = jnp.concatenate(small, axis=0)
-    merged = merged + spread(spread_matrix(side // 2), coarse_merged)
-    merged_out[...] = merged.astype(BF16)
+        normed_out[k] = rows_k
+    made[7].wait()
+    cot_low = cot_ref[...]
+    coarse_cot = dot(pool_matrix(side // 2, 1.0), cot_low)
+    grads = head_cotangents(
+        cot_low.astype(F32), coarse_cot, [merging[s, 1:2, :] for s in range(3)]
+    )
+    made[8].wait()
+    tap_grad, scale_row = tap_backward(
+        tap, r, scale[1:2, :], dot_last(grads, heads[...]), spread_matrix(side), mid
+    )
+    scale_out[...] = jnp.broadcast_to(scale_row, scale_out.shape)
     grad2 = (tap_grad.astype(BF16).astype(F32) * slope2 * gain[1:2, :]).astype(BF16)
-    high = small.astype(BF16)
-    both = jnp.concatenate([high.astype(F32), small - high.astype(F32)], axis=0).astype(BF16)
     for num in range(2):
         grad_out[num * rows : (num + 1) * rows, :] = grad2[:, num * half : (num + 1) * half]
     for target in (own_out, send_out):
@@ -361,7 +372,6 @@
         for num in range(at.lanes):
             lanes = slice(num * half, (num + 1) * half)
             target[at.cot + num * mid : at.cot + (num + 1) * mid, :] = cot_low[:, lanes]
-            target[at.small + num * 16 : at.small + (num + 1) * 16, :] = both[:, lanes]
     pass_out[...] = own_out[pl.ds(pl.multiple_of((1 - pick) * at.skip, 16), at.span), :]
 
 
@@ -378,67 +388,71 @@
         partial(section_kernel, side, dp),
         "section",
         60,
-        4200000000,
+        1150000000,
         (plan, features, trunk_weight, head_weight, cotangent, gain, shift, scale, merging),
-        [spec(pltpu.SMEM)] + [spec(pl.ANY)] * 8,
+        [spec(pltpu.SMEM)] + [spec(pltpu.HBM)] * 8,
         (
             jax.ShapeDtypeStruct((at.total, half), BF16),
             jax.ShapeDtypeStruct((at.total, half), BF16),
             jax.ShapeDtypeStruct((at.span, half), BF16),
             jax.ShapeDtypeStruct((2 * rows, half), BF16),
             jax.ShapeDtypeStruct((rows, channels), F32),
-            jax.ShapeDtypeStruct((rows, channels), F32),
-            jax.ShapeDtypeStruct((mid, width), BF16),
+            jax.ShapeDtypeStruct((2, at.stacked, channels), BF16),
+            jax.ShapeDtypeStruct((8, channels), F32),
         ),
         (vmem,) * 7,
         [
             pltpu.VMEM((rows, channels), BF16),
             pltpu.VMEM((6, 3 * channels, channels), BF16),
-            pltpu.VMEM((2, channels, width), BF16),
+            pltpu.VMEM((channels, width), BF16),
             pltpu.VMEM((mid, width), BF16),
             pltpu.VMEM(gain.shape, F32),
             pltpu.VMEM(shift.shape, F32),
             pltpu.VMEM(scale.shape, F32),
             pltpu.VMEM(merging.shape, F32),
-            pltpu.VMEM((3, rows, channels), F32),
+            *shift_scratch(side, channels),
             pltpu.VMEM((rows, 3 * channels), BF16),
-            pltpu.SemaphoreType.DMA((14,)),
+            pltpu.SemaphoreType.DMA((13,)),
         ],
     )
 
 
-def back_kernel(side, layer, grad, trunk_weight, factor, *rest):
-    if layer == 0:
-        merged, own_out, send_out, weights, shifted, patch, sems = rest
-    else:
-        grad_out, weights, shifted, patch, sems = rest
+def back_kernel(side, layer, grad_in, trunk_weight, factor_in, *rest):
+    grad, factor, weights, low_shifted, high_shifted, patch, sems = rest[-7:]
     channels = trunk_weight.shape[2]
     half = channels // 2
     rows = rows_of(side)
     made = copies(
-        [
-            (trunk_weight.at[layer, pl.ds(num * 3 * channels, 3 * channels)], weights.at[num])
-            for num in range(3)
-        ],
+        [(grad_in, grad)]
+        + [
+            (trunk_weight.at[layer, pl.ds(num * channels, channels)], weights.at[num])
+            for num in range(9)
+        ]
+        + [(factor_in, factor)],
         sems,
     )
+    made[0].wait()
     value = jnp.concatenate([grad[:rows, :], grad[rows:, :]], axis=1).astype(F32)
-    column_shifts(value, side, shifted)
+    column_shifts(value, side, low_shifted, high_shifted)
     total = jnp.zeros((rows, channels), F32)
     for a in range(3):
         for b in range(3):
-            put_row_shift(patch, 0, b * channels, shifted, 2 - b, 2 - a, side)
-        made[a].wait()
+            put_row_shift(
+                patch, 0, b * channels, low_shifted, high_shifted, 2 - b, 2 - a, side
+            )
         for b in range(3):
+            made[1 + 3 * a + b].wait()
             total = total + dot_last(
-                patch[:, b * channels : (b + 1) * channels],
-                weights[a, b * channels : (b + 1) * channels, :],
+                patch[:, b * channels : (b + 1) * channels], weights[3 * a + b]
             )
+    made[10].wait()
     if layer == 1:
+        (grad_out,) = rest[:-7]
         low = (total * factor[...]).astype(BF16)
         grad_out[:rows, :] = low[:, :half]
         grad_out[rows:, :] = low[:, half:]
         return
+    merged, own_out, send_out = rest[:-7]
     pipe = lax.axis_index("pipe")
     total = total + factor[...]
     left, right = total[:, :half], total[:, half:]
@@ -464,7 +478,8 @@
     channels = trunk_weight.shape[2]
     half = channels // 2
     vmem = spec(pltpu.VMEM)
-    in_specs = [vmem, spec(pl.ANY), vmem]
+    hbm = spec(pl.ANY)
+    in_specs = [hbm, spec(pltpu.HBM), hbm]
     operands = [grad, trunk_weight, factor]
     if layer == 0:
         in_specs.append(vmem)
@@ -480,50 +495,35 @@
     return call(
         partial(back_kernel, side, layer),
         "back",
-        46,
-        1500000000,
+        60 if layer else 46,
+        350000000,
         operands,
         in_specs,
         out_shape,
         out_specs,
         [
-            pltpu.VMEM((3, 3 * channels, channels), BF16),
-            pltpu.VMEM((3, rows, channels), F32),
+            pltpu.VMEM((2 * rows, half), BF16),
+            pltpu.VMEM((rows, channels), F32),
+            pltpu.VMEM((9, channels, channels), BF16),
+            *shift_scratch(side, channels),
             pltpu.VMEM((rows, 3 * channels), BF16),
-            pltpu.SemaphoreType.DMA((3,)),
+            pltpu.SemaphoreType.DMA((11,)),
         ],
         after,
     )
 
 
-def through(pairs, held, sems):
-    coming = [
-        pltpu.make_async_copy(source, slot, sems.at[num])
-        for num, (source, slot, target) in enumerate(pairs)
-    ]
-    going = [
-        pltpu.make_async_copy(slot, target, sems.at[len(pairs) + num])
-        for num, (source, slot, target) in enumerate(pairs)
-    ]
-    for one in coming:
-        one.start()
-    for one, two in zip(coming, going):
-        one.wait()
-        two.start()
-    for two in going:
-        two.wait()
-
-
 def move_kernel(moves, *refs):
-    sources, out, held, sems = refs[:-3], refs[-3], refs[-2], refs[-1]
-    through(
+    sources, out, sems = refs[:-2], refs[-2], refs[-1]
+    made = copies(
         [
-            (sources[num].at[first()], held.at[pl.ds(place, count)], out.at[pl.ds(place, count)])
+            (sources[num].at[first()], out.at[pl.ds(place, count)])
             for num, first, place, count in moves
         ],
-        held,
         sems,
     )
+    for one in made:
+        one.wait()
 
 
 def far_factors(dp, other, side, width, after):
@@ -538,12 +538,12 @@
         partial(move_kernel, [(0, rows, 0, at.span)]),
         "far_factors",
         4,
-        120000000,
+        30000000,
         (other,),
         [spec(pl.ANY)],
         jax.ShapeDtypeStruct((at.span, half), BF16),
-        spec(pl.ANY),
-        [pltpu.VMEM((at.span, half), BF16), pltpu.SemaphoreType.DMA((2,))],
+        spec(pltpu.VMEM),
+        [pltpu.SemaphoreType.DMA((1,))],
         after,
     )
 
@@ -569,28 +569,28 @@
         ),
         "first_factors",
         4,
-        540000000,
+        90000000,
         (own, other, own_grad, other_grad),
         [spec(pl.ANY)] * 4,
         jax.ShapeDtypeStruct((4 * at.rows, half), BF16),
-        spec(pl.ANY),
-        [pltpu.VMEM((4 * at.rows, half), BF16), pltpu.SemaphoreType.DMA((8,))],
+        spec(pltpu.VMEM),
+        [pltpu.SemaphoreType.DMA((4,))],
         after,
     )
 
 
-def put_trunk_blocks(dp, piece, send, keep, xs, gs, shifted, patch, side, wait_x, wait_g):
+def put_trunk_blocks(dp, piece, send, keep, xs, gs, low, high, patch, side, wait_x, wait_g):
     rows = rows_of(side)
     half = xs.shape[1]
     quarter = half // 2
     _, second, third = block_bits(dp, own_core(dp), piece)
     for image in range(4):
         wait_g(image)
-        column_shifts(gs[image * rows : (image + 1) * rows, :].astype(F32), side, shifted)
+        column_shifts(gs[image * rows : (image + 1) * rows, :].astype(F32), side, low, high)
         for a in range(3):
             for b in range(3):
                 put_row_shift(
-                    patch, image * rows, (3 * a + b) * half, shifted, 2 - b, 2 - a, side
+                    patch, image * rows, (3 * a + b) * half, low, high, 2 - b, 2 - a, side
                 )
     for image in range(4):
         wait_x(image)
@@ -610,7 +610,7 @@
 
 
 def late_grads_kernel(
-    side, dp, width, own, other, near, far, send, keep, xs, gs, shifted, patch, sems
+    side, dp, width, own, other, near, far, send, keep, xs, gs, low, high, patch, sems
 ):
     half = xs.shape[1]
     at = Layout(side, 2 * half, width)
@@ -636,7 +636,8 @@
         keep,
         xs,
         gs,
-        shifted,
+        low,
+        high,
         patch,
         side,
         lambda image: made[2 * image + 1].wait(),
@@ -650,10 +651,7 @@
 
 
 def trunk_scratch(rows, half):
-    return [
-        pltpu.VMEM((3, rows, half), F32),
-        pltpu.VMEM((4 * rows, 9 * half), BF16),
-    ]
+    return shift_scratch(SIDE, half) + [pltpu.VMEM((4 * rows, 9 * half), BF16)]
 
 
 def late_grads(dp, width, own, other, near, far, after):
@@ -666,7 +664,7 @@
         partial(late_grads_kernel, side, dp, width),
         "late_grads",
         28,
-        1440000000,
+        430000000,
         (own, other, near, far),
         [spec(pl.ANY)] * 4,
         (shape, shape),
@@ -682,7 +680,7 @@
 
 
 def early_grads_kernel(
-    side, dp, width, own, other, own_g, other_g, far, send, keep, xs, gs, shifted, patch, sems
+    side, dp, width, own, other, own_g, other_g, far, send, keep, xs, gs, low, high, patch, sems
 ):
     half = xs.shape[1]
     at = Layout(side, 2 * half, width)
@@ -707,7 +705,8 @@
         keep,
         xs,
         gs,
-        shifted,
+        low,
+        high,
         patch,
         side,
         lambda image: made[3 + image].wait() if image < 3 else None,
@@ -725,7 +724,7 @@
         partial(early_grads_kernel, side, dp, width),
         "early_grads",
         28,
-        1140000000,
+        370000000,
         (own, other, own_g, other_g, far),
         [spec(pl.ANY)] * 5,
         (shape, shape),
@@ -741,82 +740,160 @@
 
 
 def head_grads_kernel(
-    side, dp, is_own, own, other, merging_in, out, ns, cots, smalls, merging, sems
+    side,
+    dp,
+    plan,
+    features,
+    head_weight,
+    normed_in,
+    scale_in,
+    last_scale_in,
+    own,
+    other,
+    merging_in,
+    send,
+    keep,
+    merged_out,
+    tap_grad_out,
+    feed,
+    heads,
+    normed,
+    scale,
+    last_scale,
+    ns,
+    cots,
+    merging,
+    sems,
 ):
-    half = ns.shape[1]
+    half = ns.shape[2]
     width = merging.shape[2]
     at = Layout(side, 2 * half, width)
     mid = at.mid
+    quarter = half // 2
     pick, second, third = block_bits(dp, own_core(dp), HEAD)
-    tap = pick if is_own else 1 - pick
-    first = pl.multiple_of(at.normed + tap * at.stacked, 16)
     pairs = [(merging_in, merging)]
     for num, source in enumerate((own, other)):
         pairs += [
             (source.at[pl.ds(at.cot, at.lanes * mid)], cots.at[num]),
-            (source.at[pl.ds(first, at.stacked)], ns.at[pl.ds(num * at.stacked, at.stacked)]),
-            (source.at[pl.ds(at.small, at.lanes * 16)], smalls.at[num]),
+            (source.at[pl.ds(at.normed, 2 * at.stacked)], ns.at[num]),
         ]
+    pairs += [(normed_in, normed), (head_weight.at[0], heads.at[0])]
+    pairs += [(features.at[plan[0, lax.axis_index("pipe")]], feed), (scale_in, scale)]
+    pairs += [(last_scale_in, last_scale), (head_weight.at[1], heads.at[1])]
     made = copies(pairs, sems)
-    made[0].wait()
-    weights = [merging[s, pl.ds(tap, 1), :] for s in range(3)]
     sums = pool_matrix(side // 2, 1.0)
-    grads = []
+    cotangents = []
     for image in range(2):
-        made[1 + 3 * image].wait()
+        made[1 + 2 * image].wait()
         cot_low = jnp.concatenate(
             [cots[image, num * mid : (num + 1) * mid, :] for num in range(at.lanes)], axis=1
         )
-        grads.append(head_cotangents(cot_low.astype(F32), dot(sums, cot_low), weights))
-    made[2].wait()
+        cotangents.append((cot_low.astype(F32), dot(sums, cot_low)))
+    for one in (made[0], made[2], made[4]):
+        one.wait()
+    for target, tap in ((send, 1 - pick), (keep, pick)):
+        weights = [merging[s, pl.ds(tap, 1), :] for s in range(3)]
+        grads = [head_cotangents(cot, coarse, weights) for cot, coarse in cotangents]
+        first = pl.multiple_of(tap * at.stacked, 16)
+        both = [ns[image, pl.ds(first, at.stacked), :] for image in range(2)]
+        product = dot(
+            jnp.concatenate(both, axis=0).T, jnp.concatenate(grads, axis=0)
+        ).astype(BF16)
+        for lane in range(2):
+            for num in range(width // 256):
+                column = lane * (width // 2) + num * 128
+                for part in range(2):
+                    row = ((lane ^ second) * 2 + (part ^ third)) * (width // 256) + num
+                    target[pl.ds(pl.multiple_of(row * quarter, quarter), quarter), :] = product[
+                        part * quarter : (part + 1) * quarter, column : column + 128
+                    ]
+    cot, coarse_cot = cotangents[0]
+    merged = jnp.zeros((mid, width), F32)
+    coarse_merged = jnp.zeros((at.stacked - 2 * mid, width), F32)
+    small = []
     made[5].wait()
-    product = dot(ns[...].T, jnp.concatenate(grads, axis=0)).astype(BF16)
-    quarter = half // 2
-    for lane in range(2):
-        for num in range(width // 256):
-            column = lane * (width // 2) + num * 128
-            for part in range(2):
-                row = pl.multiple_of(
-                    (((lane ^ second) * 2 + (part ^ third)) * (width // 256) + num) * quarter,
-                    quarter,
-                )
-                out[pl.ds(row, quarter), :] = product[
-                    part * quarter : (part + 1) * quarter, column : column + 128
-                ]
-    made[3].wait()
-    made[6].wait()
-    total = smalls[0].astype(F32) + smalls[1].astype(F32)
+    for k in range(2):
+        made[6 if k == 0 else 10].wait()
+        weights = [merging[s, k : k + 1, :] for s in range(3)]
+        product = dot(normed[k], heads[k])
+        merged = merged + weights[0] * product[:mid] + weights[1] * product[mid : 2 * mid]
+        coarse_merged = coarse_merged + weights[2] * product[2 * mid :]
+        small.append(jnp.sum(cot * product[:mid], axis=0, keepdims=True))
+        small.append(jnp.sum(cot * product[mid : 2 * mid], axis=0, keepdims=True))
+        small.append(jnp.sum(coarse_cot * product[2 * mid :], axis=0, keepdims=True))
+        if k == 0:
+            for one in made[7:10]:
+                one.wait()
+            tap = feed[...].astype(F32)
+            back = dot_last(head_cotangents(cot, coarse_cot, weights), heads[0])
+            tap_grad_out[...], scale_row = tap_backward(
+                tap, tap_norm(tap), scale[0:1, :], back, spread_matrix(side), mid
+            )
+    merged = merged + spread(spread_matrix(side // 2), coarse_merged)
+    merged_out[...] = merged.astype(BF16)
+    small.append(
+        jnp.concatenate(
+            [scale_row, last_scale[0:1, :], jnp.zeros((1, width - 4 * half), F32)], axis=1
+        )
+    )
+    small.append(jnp.zeros((1, width), F32))
+    pair = split_pair(jnp.concatenate(small, axis=0))
     first = width // 128 * half
-    for num in range(at.lanes):
-        pair = split_pair(total[num * 16 : num * 16 + 8] + total[num * 16 + 8 : num * 16 + 16])
-        for lane in range(half // 128):
-            row = first + (num * (half // 128) + lane) * 16
-            out[row : row + 16, :] = pair[:, lane * 128 : (lane + 1) * 128]
-
-
-def head_grads(dp, is_own, own, other, merging, after):
+    for num in range(width // 128):
+        for target in (send, keep):
+            target[first + num * 16 : first + (num + 1) * 16, :] = pair[
+                :, num * 128 : (num + 1) * 128
+            ]
+
+
+def head_grads(
+    dp, plan, features, head_weight, normed, scale, last_scale, own, other, merging, after
+):
     side = SIDE
+    rows = rows_of(side)
     half = own.shape[1]
     width = merging.shape[2]
     at = Layout(side, 2 * half, width)
+    shape = jax.ShapeDtypeStruct((width // 128 * half + 16 * width // 128, 128), BF16)
+    vmem = spec(pltpu.VMEM)
     return call(
-        partial(head_grads_kernel, side, dp, is_own),
+        partial(head_grads_kernel, side, dp),
         "head_grads",
-        16,
-        570000000,
-        (own, other, merging),
-        [spec(pl.ANY)] * 3,
-        jax.ShapeDtypeStruct((width // 128 * half + 16 * width // 128, 128), BF16),
-        spec(pltpu.VMEM),
+        40,
+        610000000,
+        (plan, features, head_weight, normed, scale, last_scale, own, other, merging),
+        [spec(pltpu.SMEM), spec(pltpu.HBM), spec(pltpu.HBM), spec(pl.ANY), spec(pltpu.HBM)]
+        + [spec(pl.ANY)] * 3
+        + [spec(pltpu.HBM)],
+        (
+            shape,
+            shape,
+            jax.ShapeDtypeStruct((at.mid, width), BF16),
+            jax.ShapeDtypeStruct((rows, 2 * half), F32),
+        ),
+        (vmem,) * 4,
         [
-            pltpu.VMEM((2 * at.stacked, half), BF16),
+            pltpu.VMEM((rows, 2 * half), BF16),
+            pltpu.VMEM((2, 2 * half, width), BF16),
+            pltpu.VMEM((2, at.stacked, 2 * half), BF16),
+            pltpu.VMEM(scale.shape, F32),
+            pltpu.VMEM(last_scale.shape, F32),
+            pltpu.VMEM((2, 2 * at.stacked, half), BF16),
             pltpu.VMEM((2, at.lanes * at.mid, half), BF16),
-            pltpu.VMEM((2, at.lanes * 16, half), BF16),
             pltpu.VMEM(merging.shape, F32),
-            pltpu.SemaphoreType.DMA((7,)),
+            pltpu.SemaphoreType.DMA((11,)),
         ],
         after,
     )
+
+
+def held_back(array, after):
+    def kernel(*refs):
+        pass
+
+    hbm = spec(pl.ANY)
+    shape = jax.ShapeDtypeStruct(array.shape, array.dtype)
+    return call(kernel, "held_back", 4, 1024, (array,), [hbm], shape, hbm, (), after, {0: 0})
 
 
 def add_tails(one, two):
@@ -847,7 +924,7 @@
         partial(sum_kernel, tail),
         "summed",
         4,
-        1024,
+        10000000,
         (keep, received),
         [vmem, vmem],
         (shape,) * parts,
@@ -869,7 +946,7 @@
         pair_kernel,
         "paired",
         4,
-        1024,
+        10000000,
         (one, two),
         [vmem, vmem],
         jax.ShapeDtypeStruct((2 * rows, 128), BF16),
@@ -881,8 +958,7 @@
 
 def widen_trunk_kernel(dp, layer, half, kinds, *refs):
     sources = refs[: len(kinds)]
-    out, done, held, wide, sems_in, sems_out = refs[-6:]
-    done[...] = jnp.zeros(done.shape, F32)
+    out, held, wide, sems_in, sems_out = refs[-5:]
     quarter = half // 2
     size = 9 * quarter
     jobs = []
@@ -929,14 +1005,11 @@
         partial(widen_trunk_kernel, dp, layer, half, kinds),
         "widen_trunk",
         24,
-        870000000,
+        290000000,
         operands,
         [hbm] * len(operands),
-        (
-            jax.ShapeDtypeStruct((layers, 9, 2 * half, 2 * half), F32),
-            jax.ShapeDtypeStruct((8, 128), F32),
-        ),
-        (hbm, spec(pltpu.VMEM)),
+        jax.ShapeDtypeStruct((layers, 9, 2 * half, 2 * half), F32),
+        hbm,
         [
             pltpu.VMEM((count, 2, 9 * half // 2, 128), BF16),
             pltpu.VMEM((count, 9, half // 2, half), F32),
@@ -950,8 +1023,7 @@
 
 def widen_heads_kernel(dp, half, kinds, *refs):
     sources = refs[: len(kinds)]
-    out, done, held, wide, sems_in, sems_out = refs[-6:]
-    done[...] = jnp.zeros(done.shape, F32)
+    out, held, wide, sems_in, sems_out = refs[-5:]
     quarter = half // 2
     size = held.shape[2]
     width = wide.shape[2]
@@ -993,14 +1065,11 @@
         partial(widen_heads_kernel, dp, half, kinds),
         "widen_heads",
         40,
-        1320000000,
+        440000000,
         operands,
         [hbm] * len(operands),
-        (
-            jax.ShapeDtypeStruct((2, 2 * half, width), F32),
-            jax.ShapeDtypeStruct((8, 128), F32),
-        ),
-        (hbm, spec(pltpu.VMEM)),
+        jax.ShapeDtypeStruct((2, 2 * half, width), F32),
+        hbm,
         [
             pltpu.VMEM((count, 2, width // 256 * half // 2, 128), BF16),
             pltpu.VMEM((count, half, width // 2), F32),
@@ -1013,66 +1082,135 @@
 
 
 def finish_kernel(
-    dp, at, plan, own_feed, merged, received, own_sum, other_sum,
-    merged_out, feed_out, scale_out, merging_out, held, sems,
+    dp, tail, plan, own_feed, merged, received, own_sum, other_sum,
+    merged_out, feed_out, scale_out, merging_out,
+    feeds, maps, ours, theirs, scales, weights, sems,
 ):
-    tail = pl.ds(at, held.shape[1])
-    made = copies([(own_sum.at[tail], held.at[0]), (other_sum.at[tail], held.at[1])], sems)
-    pipe = lax.axis_index("pipe")
     rows, half = own_feed.shape
     mid, width = merged.shape
+    first = own_sum.shape[0] - tail
+    pipe = lax.axis_index("pipe")
     slot = plan[0, pipe]
-    feed_out[slot] = own_feed[...]
+    made = copies(
+        [
+            (own_feed, feed_out.at[slot]),
+            (own_sum.at[pl.ds(first, tail)], ours),
+            (other_sum.at[pl.ds(first, tail)], theirs),
+        ],
+        sems,
+    )
     for num in range(half // 128):
-        feed_out[1 - slot, :, num * 128 : (num + 1) * 128] = received[
+        feeds[:, num * 128 : (num + 1) * 128] = received[
             num * rows : (num + 1) * rows, :
         ].astype(F32)
     low_merged = merged[...]
-    merged_out[pipe] = jnp.where(
-        pipe == 0, low_merged[:, : width // 2], low_merged[:, width // 2 :]
-    )
+    maps[0] = jnp.where(pipe == 0, low_merged[:, : width // 2], low_merged[:, width // 2 :])
     first = half // 128 * rows
     for num in range(width // 256):
-        merged_out[1 - pipe, :, num * 128 : (num + 1) * 128] = received[
+        maps[1, :, num * 128 : (num + 1) * 128] = received[
             first + num * mid : first + (num + 1) * mid, :
         ]
-    for one in made:
-        one.wait()
-    low = jnp.where(own_core(dp) == 0, held[0], held[1]).astype(F32)
+    going = [
+        pltpu.make_async_copy(feeds, feed_out.at[1 - slot], sems.at[3]),
+        pltpu.make_async_copy(maps.at[0], merged_out.at[pipe], sems.at[4]),
+        pltpu.make_async_copy(maps.at[1], merged_out.at[1 - pipe], sems.at[5]),
+    ]
+    for one in going:
+        one.start()
+    made[1].wait()
+    made[2].wait()
+    total = ours[...].astype(F32) + theirs[...].astype(F32)
     for num in range(width // 128):
         lanes = slice(num * 128, (num + 1) * 128)
-        block = low[num * 16 : num * 16 + 8] + low[num * 16 + 8 : num * 16 + 16]
+        block = total[num * 16 : num * 16 + 8] + total[num * 16 + 8 : num * 16 + 16]
         for k in range(2):
             for s in range(3):
-                merging_out[s, k : k + 1, lanes] = block[3 * k + s : 3 * k + s + 1]
-        for k in range(2):
+                weights[s, k : k + 1, lanes] = block[3 * k + s : 3 * k + s + 1]
             column = num * 128 - k * 2 * half
             if 0 <= column < 2 * half:
-                scale_out[k : k + 1, column : column + 128] = block[6:7]
+                scales[k : k + 1, column : column + 128] = block[6:7]
+    going += [
+        pltpu.make_async_copy(scales, scale_out, sems.at[6]),
+        pltpu.make_async_copy(weights, merging_out, sems.at[7]),
+    ]
+    for one in going[3:]:
+        one.start()
+    for one in going + made[:1]:
+        one.wait()
 
 
 def finish(dp, plan, own_feed, merged, received, own_sum, other_sum, after):
     rows, half = own_feed.shape
     mid, width = merged.shape
     vmem = spec(pltpu.VMEM)
+    hbm = spec(pl.ANY)
     tail = 16 * width // 128
     return call(
-        partial(finish_kernel, dp, own_sum.shape[0] - tail),
+        partial(finish_kernel, dp, tail),
         "finish",
         8,
-        510000000,
+        170000000,
         (plan, own_feed, merged, received, own_sum, other_sum),
-        [spec(pltpu.SMEM), vmem, vmem, vmem, spec(pl.ANY), spec(pl.ANY)],
+        [spec(pltpu.SMEM), hbm, vmem, vmem, hbm, hbm],
         (
             jax.ShapeDtypeStruct((2, mid, width // 2), BF16),
             jax.ShapeDtypeStruct((2, rows, half), F32),
             jax.ShapeDtypeStruct((2, 2 * half), F32),
             jax.ShapeDtypeStruct((3, 2, width), F32),
         ),
-        (vmem,) * 4,
-        [pltpu.VMEM((2, tail, 128), BF16), pltpu.SemaphoreType.DMA((2,))],
+        (hbm,) * 4,
+        [
+            pltpu.VMEM((rows, half), F32),
+            pltpu.VMEM((2, mid, width // 2), BF16),
+            pltpu.VMEM((tail, 128), BF16),
+            pltpu.VMEM((tail, 128), BF16),
+            pltpu.VMEM((2, 2 * half), F32),
+            pltpu.VMEM((3, 2, width), F32),
+            pltpu.SemaphoreType.DMA((8,)),
+        ],
         after,
     )
+
+
+ORDER = (
+    "back1",
+    "far",
+    "first",
+    "head",
+    "late",
+    "early",
+    "L2",
+    "E2",
+    "H1",
+    "L3",
+    "E3",
+    "H2",
+    "back0",
+    "L4",
+    "E4",
+    "H3",
+    "L5",
+    "E5",
+    "H4",
+    "L6",
+    "E6",
+    "H5",
+    "Lold_wide",
+    "Eold_wide",
+    "H6",
+    "Lnew",
+    "Lnew_own",
+    "Enew",
+    "Lnew_other",
+    "Enew_own",
+    "Hold_wide",
+    "finish",
+    "Hnew",
+    "Enew_other",
+    "Hnew_own",
+    "Hnew_other",
+)
+WAITS = {"far": ("near",), "L6": ("feed",)}
 
 
 class Sum:
@@ -1086,23 +1224,24 @@
         self.keep = keep
         self.come = self.swap(self.steps[0][1], send)
 
-    def advance(self, *after):
+    def advance(self, after):
         kind = self.steps[self.at][0]
         self.at += 1
         following, stage = self.steps[self.at]
         if kind == "gather":
-            self.keep = paired(self.keep, self.come, self.keep.shape[0] - self.tail, after)
+            rows = self.keep.shape[0] - self.tail
+            self.keep, mark = paired(self.keep, self.come, rows, after)
             self.tail = 0
             send = self.keep
         else:
             parts = 2 if following == "scatter" else 1
-            made = summed(self.keep, self.come, parts, self.tail, after)
+            made, mark = summed(self.keep, self.come, parts, self.tail, after)
             self.keep = made[0]
             send = made[-1]
             if following == "gather":
                 self.final = self.keep
         self.come = self.swap(stage, send)
-        return self.keep
+        return mark
 
 
 def body(
@@ -1135,7 +1274,7 @@
     def swap_cores(block):
         return lax.ppermute(block, AXES, [(i, i ^ 1) for i in range(devices)])
 
-    own, send, passed, grad2, slope, tap_grad, merged = section(
+    (own, send, passed, grad2, slope, normed, last_scale), mark = section(
         dp,
         plan,
         features,
@@ -1149,66 +1288,124 @@
     )
     other = swap_cores(send)
     near = swap(LATE, 0, passed)
-    passed = far_factors(dp, other, SIDE, width, ())
-    far = swap(LATE, 0, passed)
-    head_send = head_grads(dp, False, own, other, merging, (passed,))
-    head_keep = head_grads(dp, True, own, other, merging, (head_send, near))
-    head = Sum(swap, HEAD, last, head_send, head_keep, tail)
-    grad1 = back(1, grad2, weights, slope, None, (head_keep, far))
-    other_grad1 = swap_cores(grad1)
-    passed = first_factors(dp, own, other, grad1, other_grad1, SIDE, width, ())
-    first_far = swap(EARLY, 0, passed)
-    token = head.advance(passed)
-    late_blocks = late_grads(dp, width, own, other, near, far, (token,))
-    late = Sum(swap, LATE, last, *late_blocks)
-    token = head.advance(late.keep)
-    early_blocks = early_grads(
-        dp, width, own, other, grad1, other_grad1, first_far, (token,)
-    )
-    early = Sum(swap, EARLY, last, *early_blocks)
-    pieces = {"H": head, "L": late, "E": early}
-
-    def advance(order, *tokens):
-        for name in order:
-            tokens = (pieces[name].advance(*tokens),)
-        return tokens[0]
-
-    token = advance("LHELHE" + "LHE" * (last - 3), early.keep)
-    own_feed, sent = back(0, grad1, weights, tap_grad, merged, (token,))
-    received = lax.ppermute(sent, "pipe", [(0, 1), (1, 0)])
-    token = advance("LHELH", own_feed)
-    other_head = swap_cores(head.keep)
-    other_sum = swap_cores(head.final)
-    token = advance("EL", token)
-    other_late = swap_cores(late.keep)
-    merged_maps, features_grad, scale_grad, merging_grad = finish(
-        dp, plan, own_feed, merged, received, head.final, other_sum, (token,)
-    )
-    token = advance("E", merged_maps)
-    other_early = swap_cores(early.keep)
     kept = ((False, False), (True, False))
     came = ((False, True), (True, True))
-    head_out, done = widen_heads(dp, half, width, (head.keep, other_head), kept, None, (token,))
-    trunk_out, done = widen_trunk(
-        dp, 1, layers, half, (late.keep, other_late), kept, None, (done,)
-    )
-    trunk_out, done = widen_trunk(
-        dp, 0, layers, half, (early.keep, other_early), kept, trunk_out, (done, head.come)
-    )
-    head_out, done = widen_heads(
-        dp, half, width, (head.come, swap_cores(head.come)), came, head_out, (done, late.come)
-    )
-    trunk_out, done = widen_trunk(
-        dp, 1, layers, half, (late.come, swap_cores(late.come)), came, trunk_out, (done, early.come)
-    )
-    other_new = swap_cores(early.come)
-    trunk_out, done = widen_trunk(dp, 0, layers, half, (early.come,), came[:1], trunk_out, (done,))
-    trunk_out, done = widen_trunk(dp, 0, layers, half, (other_new,), came[1:], trunk_out, (done,))
+    got = {"before": None, "heads": None}
+    pieces = {}
+
+    def make_back1(after):
+        got["grad1"], mark = back(1, grad2, weights, slope, None, after)
+        got["other_grad1"] = swap_cores(got["grad1"])
+        return mark
+
+    def make_far(after):
+        passed, mark = far_factors(dp, other, SIDE, width, after)
+        got["far"] = swap(LATE, 0, passed)
+        return mark
+
+    def make_first(after):
+        grads = (got["grad1"], got["other_grad1"])
+        passed, mark = first_factors(dp, own, other, *grads, SIDE, width, after)
+        got["first"] = swap(EARLY, 0, passed)
+        return mark
+
+    def make_head(after):
+        blocks, mark = head_grads(
+            dp,
+            plan,
+            features,
+            head_weight,
+            normed,
+            norm_scale,
+            last_scale,
+            own,
+            other,
+            merging,
+            after,
+        )
+        pieces["H"] = Sum(swap, HEAD, last, *blocks[:2], tail)
+        got["maps"], got["tap_grad"] = blocks[2:]
+        return mark
+
+    def make_late(after):
+        blocks, mark = late_grads(dp, width, own, other, near, got["far"], after)
+        pieces["L"] = Sum(swap, LATE, last, *blocks)
+        return mark
+
+    def make_early(after):
+        grads = (got["grad1"], got["other_grad1"])
+        blocks, mark = early_grads(dp, width, own, other, *grads, got["first"], after)
+        pieces["E"] = Sum(swap, EARLY, last, *blocks)
+        return mark
+
+    def make_back0(after):
+        (got["feed"], sent), mark = back(
+            0, got["grad1"], weights, got["tap_grad"], got["maps"], after
+        )
+        got["received"] = lax.ppermute(sent, "pipe", [(0, 1), (1, 0)])
+        return mark
+
+    def make_finish(after):
+        sums = (pieces["H"].final, swap_cores(pieces["H"].final))
+        got["finish"], mark = finish(
+            dp, plan, got["feed"], got["maps"], got["received"], *sums, after
+        )
+        return mark
+
+    def widen(name, sources, kinds, after):
+        if name == "H":
+            got["heads"], mark = widen_heads(
+                dp, half, width, sources, kinds, got["heads"], after
+            )
+        else:
+            layer = 1 if name == "L" else 0
+            got["before"], mark = widen_trunk(
+                dp, layer, layers, half, sources, kinds, got["before"], after
+            )
+        return mark
+
+    make = {
+        "back1": make_back1,
+        "far": make_far,
+        "first": make_first,
+        "head": make_head,
+        "late": make_late,
+        "early": make_early,
+        "back0": make_back0,
+        "finish": make_finish,
+    }
+    for step in ORDER:
+        name, kind = step[0], step[1:]
+        waits = [mark]
+        for which in WAITS.get(step, ()):
+            come = {"near": near, "far": got.get("far"), "first": got.get("first")}
+            come["feed"] = got.get("received")
+            waits.append(pieces[which].come if which in pieces else come[which])
+        if step in make:
+            mark = make[step](waits)
+        elif kind == "new":
+            pieces[name].come, mark = held_back(pieces[name].come, waits)
+            got[name] = swap_cores(pieces[name].come)
+        elif kind == "old_wide":
+            sources = (pieces[name].keep, swap_cores(pieces[name].keep))
+            mark = widen(name, sources, kept, waits)
+        elif kind == "new_wide":
+            mark = widen(name, (pieces[name].come, got[name]), came, waits)
+        elif kind == "new_own":
+            mark = widen(name, (pieces[name].come,), came[:1], waits)
+        elif kind == "new_other":
+            mark = widen(name, (got[name],), came[1:], waits)
+        else:
+            mark = pieces[name].advance(waits)
+            if kind == "4":
+                for _ in range(3, last):
+                    mark = pieces[name].advance([mark])
+    merged_maps, features_grad, scale_grad, merging_grad = got["finish"]
     return (
         merged_maps,
         features_grad,
-        trunk_out.reshape(trunk_weight.shape),
-        head_out,
+        got["before"].reshape(trunk_weight.shape),
+        got["heads"],
         scale_grad,
         jnp.transpose(merging_grad, (1, 0, 2)),
     )

time: 184 us -> 167 us (0.908)
  waiting for transfers between devices: 86.6 us -> 65.4 us
    ppermute x22, waiting for transfers between devices: 83.2 us -> 64.2 us  [swap(): return lax.ppermute(block, AXES, route)]
    pallas_call x33 -> x37, Pallas kernels: 60.2 us -> 61.8 us  [call(): pl.pallas_call(run, out_shape=(*shapes, jax.ShapeDtypeStruct((8, 128), F3...]
  transfers between devices with their start and end apart: 32 -> 32, of which waited for: 15 -> 15; matrix products, arithmetic and copies ran while one was open for 0% -> 0% of each run, Pallas kernels for 24% -> 27%
where the time goes in v3:
time: 167 us
  waiting for transfers between devices  65.4 us (39%)
  Pallas kernels  61.8 us (37%)
  starting transfers between devices  35.8 us (21%)
  local copies, waits for them, and re-layouts  2.76 us (2%)
    ppermute x22, waiting for transfers between devices, swap(): return lax.ppermute(block, AXES, route)  64.2 us
    pallas_call x37, Pallas kernels, call(): pl.pallas_call(run, out_shape=(*shapes, jax.ShapeDtypeStruct((8, 128), F3...  61.8 us
    ppermute x22, starting transfers between devices, swap(): return lax.ppermute(block, AXES, route)  32.6 us
  transfers between devices with their start and end apart: 32, of which 15 were waited for; matrix products, arithmetic and copies ran while one was open for 0% of the time, Pallas kernels for 27%

profile of v3, /device:TPU:0, one launch (start us, length us, event | category | flops | bytes accessed | tf_op | source)
XLA Modules:
  0.0 167.0 jit_solution(16866823745468710078)
XLA Ops:
  0.6 11.8 %section.1 = (bf16[2080,256]{1,0:T(8,128)(2,1)}, bf16[2080,256]{1,0:T(8,128)(2,1)}, bf16[672,256]{1,0:T(8,128)(2,1)}, bf16[672,256]{1,0:T(8,128)(2,1)}, f32[336,...) custom-call(s32[1,2]{1,0:T(1,128)} %refs_0_.5, bf16[2,336,512]{2,1,0:T(8,128)(2,1)} %refs_1_.3, ...), custom_call_target="tpu_custom_call" | custom-call | flops 1150000000 | bytes 1024 | tf_op jit(solution)/shard_map/section/pallas_call | solution.py:83
  13.0 2.6 %collective-permute-start.2 = (bf16[672,256]{1,0:T(8,128)(2,1)}, bf16[672,256]{1,0:T(8,128)(2,1)S(1)}, u32[]{:S(2)}, u32[]{:S(2)}) collective-permute-start(bf16[672,256]{1,0:T(8,128)(2,1)} %get-tuple-element.107), channel_id=1, source_target_pairs={{0,16},{1,5},{2,18},{3,7},{4,20},{5,1},{6,22},{7,3},{8,24},{9,13},... | collective-permute-start | bytes 1032200 | tf_op jit(solution)/shard_map/ppermute | solution.py:1272
  15.6 4.6 %back.2 = (bf16[672,256]{1,0:T(8,128)(2,1)}, f32[8,128]{1,0:T(8,128)}) custom-call(bf16[672,256]{1,0:T(8,128)(2,1)} %get-tuple-element.98.refs_0_, bf16[2,4608,512]{2,1,0:T(8,128)(2,1)} %bitcast.8, f32[336,512]{1,0:T(8,128)} %get-tuple-element.99.refs_2_, f32[8,128]{1,0:T(8,128)} %get-tuple-element.100.refs_3_), custom_call_target="tpu_custom_call" | custom-call | flops 350000000 | bytes 1024 | tf_op jit(solution)/shard_map/back/pallas_call | solution.py:83
  21.0 0.7 copy-done.9
  22.2 0.9 first_factors.1
  23.2 1.8 %collective-permute-start.4 = (bf16[1344,256]{1,0:T(8,128)(2,1)S(1)}, bf16[1344,256]{1,0:T(8,128)(2,1)S(1)}, u32[]{:S(2)}, u32[]{:S(2)}) collective-permute-start(bf16[1344,256]{1,0:T(8,128)(2,1)S(1)} %get-tuple-element.114), channel_id=1, source_target_pairs={{0,2},{1,5},{2,0},{3,7},{4,6},{5,1},{6,4},{7,3},{8,10},{9,13},{10,... | collective-permute-start | bytes 2064392 | tf_op jit(solution)/shard_map/ppermute | solution.py:1272
  25.0 1.5 collective-permute-start.5
  26.5 2.0 %copy-done.1 = bf16[2,512,1792]{2,1,0:T(8,128)(2,1)S(1)} copy-done((bf16[2,512,1792]{2,1,0:T(8,128)(2,1)S(1)}, bf16[2,512,1792]{2,1,0:T(8,128)(2,1)}, u32[]{:S(2)}) %copy-start.1) | copy-done | bytes 3670040
  28.5 6.2 %head_grads.1 = (bf16[3808,128]{1,0:T(8,128)(2,1)S(1)}, bf16[3808,128]{1,0:T(8,128)(2,1)S(1)}, bf16[64,1792]{1,0:T(8,128)(2,1)S(1)}, f32[336,512]{1,0:T(8,128)S(1)}, f32[8,128]{1,0:T(8,128)S(1)}) custom-call(s32[1,2]{1,0:T(1,128)S(1)} %copy-done.8, bf16[2,336,512]{2,1,0:T(8,128)(2,1)S(1)} %copy-done.3, bf16[2,512,1792]{2,1,0:T(8,128)(2,1)S(1)} %copy-done.1, ...), custom_call_target="tpu_custom_call" | custom-call | flops 610000000 | bytes 1024 | tf_op jit(solution)/shard_map/head_grads/pallas_call | solution.py:83
  35.3 4.4 %late_grads.1 = (bf16[2304,128]{1,0:T(8,128)(2,1)S(1)}, bf16[2304,128]{1,0:T(8,128)(2,1)S(1)}, f32[8,128]{1,0:T(8,128)S(1)}) custom-call(bf16[2080,256]{1,0:T(8,128)(2,1)S(1)} %copy-done, bf16[2080,256]{1,0:T(8,128)(2,1)S(1)} %collective-permute-done.refs_0_.refs_1_.refs_7_, bf16[672,256]{1,0:T(8,128)(2,1)S(1)} %collective-permute-done.2.refs_2_, ...), custom_call_target="tpu_custom_call" | custom-call | flops 430000000 | bytes 1024 | tf_op jit(solution)/shard_map/late_grads/pallas_call | solution.py:83
  40.1 3.7 %early_grads.1 = (bf16[2304,128]{1,0:T(8,128)(2,1)S(1)}, bf16[2304,128]{1,0:T(8,128)(2,1)S(1)}, f32[8,128]{1,0:T(8,128)S(1)}) custom-call(bf16[2080,256]{1,0:T(8,128)(2,1)S(1)} %copy-done, bf16[2080,256]{1,0:T(8,128)(2,1)S(1)} %collective-permute-done.refs_0_.refs_1_.refs_7_, bf16[672,256]{1,0:T(8,128)(2,1)S(1)} %copy-done.2, ...), custom_call_target="tpu_custom_call" | custom-call | flops 370000000 | bytes 1024 | tf_op jit(solution)/shard_map/early_grads/pallas_call | solution.py:83
  43.8 1.8 %collective-permute-start.6 = (bf16[2304,128]{1,0:T(8,128)(2,1)S(1)}, bf16[2304,128]{1,0:T(8,128)(2,1)S(1)}, u32[]{:S(2)}, u32[]{:S(2)}) collective-permute-start(bf16[2304,128]{1,0:T(8,128)(2,1)S(1)} %get-tuple-element.119), channel_id=1, source_target_pairs={{0,16},{1,3},{2,18},{3,1},{4,20},{5,7},{6,22},{7,5},{8,24},{9,11},... | collective-permute-start | bytes 1769480 | tf_op jit(solution)/shard_map/ppermute | solution.py:1272
  45.6 4.6 %collective-permute-done.7.refs_1_ = bf16[2304,128]{1,0:T(8,128)(2,1)S(1)} collective-permute-done((bf16[2304,128]{1,0:T(8,128)(2,1)S(1)}, bf16[2304,128]{1,0:T(8,128)(2,1)S(1)}, u32[]{:S(2)}, u32[]{:S(2)}) %collective-permute-start.7) | collective-permute-done | bytes 589856 | tf_op jit(solution)/shard_map/ppermute | solution.py:1272
  50.3 2.1 %collective-permute-start.10 = (bf16[1152,128]{1,0:T(8,128)(2,1)S(1)}, bf16[1152,128]{1,0:T(8,128)(2,1)S(1)}, u32[]{:S(2)}, u32[]{:S(2)}) collective-permute-start(bf16[1152,128]{1,0:T(8,128)(2,1)S(1)} %get-tuple-element.130), channel_id=1, source_target_pairs={{0,4},{1,3},{2,6},{3,1},{4,0},{5,7},{6,2},{7,5},{8,12},{9,11},{10,... | collective-permute-start | bytes 884744 | tf_op jit(solution)/shard_map/ppermute | solution.py:1272
  52.4 9.3 %collective-permute-done.6.refs_1_ = bf16[2304,128]{1,0:T(8,128)(2,1)S(1)} collective-permute-done((bf16[2304,128]{1,0:T(8,128)(2,1)S(1)}, bf16[2304,128]{1,0:T(8,128)(2,1)S(1)}, u32[]{:S(2)}, u32[]{:S(2)}) %collective-permute-start.6) | collective-permute-done | bytes 589856 | tf_op jit(solution)/shard_map/ppermute | solution.py:1272
  61.8 1.8 %collective-permute-start.9 = (bf16[1152,128]{1,0:T(8,128)(2,1)S(1)}, bf16[1152,128]{1,0:T(8,128)(2,1)S(1)}, u32[]{:S(2)}, u32[]{:S(2)}) collective-permute-start(bf16[1152,128]{1,0:T(8,128)(2,1)S(1)} %get-tuple-element.128), channel_id=1, source_target_pairs={{0,4},{1,17},{2,6},{3,19},{4,0},{5,21},{6,2},{7,23},{8,12},{9,25},... | collective-permute-start | bytes 884744 | tf_op jit(solution)/shard_map/ppermute | solution.py:1272
  64.6 2.7 %collective-permute-start.14 = (bf16[1152,128]{1,0:T(8,128)(2,1)S(1)}, bf16[1152,128]{1,0:T(8,128)(2,1)S(1)}, u32[]{:S(2)}, u32[]{:S(2)}) collective-permute-start(bf16[1152,128]{1,0:T(8,128)(2,1)S(1)} %get-tuple-element.140.refs_0_), channel_id=1, source_target_pairs={{0,8},{1,9},{2,10},{3,11},{4,12},{5,13},{6,14},{7,15},{8,0},{9,1},... | collective-permute-start | bytes 884744 | tf_op jit(solution)/shard_map/ppermute | solution.py:1272
  67.3 4.3 %collective-permute-done.9.refs_1_ = bf16[1152,128]{1,0:T(8,128)(2,1)S(1)} collective-permute-done((bf16[1152,128]{1,0:T(8,128)(2,1)S(1)}, bf16[1152,128]{1,0:T(8,128)(2,1)S(1)}, u32[]{:S(2)}, u32[]{:S(2)}) %collective-permute-start.9) | collective-permute-done | bytes 294944 | tf_op jit(solution)/shard_map/ppermute | solution.py:1272
  71.7 2.8 %collective-permute-start.13 = (bf16[1152,128]{1,0:T(8,128)(2,1)S(1)}, bf16[1152,128]{1,0:T(8,128)(2,1)S(1)}, u32[]{:S(2)}, u32[]{:S(2)}) collective-permute-start(bf16[1152,128]{1,0:T(8,128)(2,1)S(1)} %get-tuple-element.139.refs_0_), channel_id=1, source_target_pairs={{0,8},{1,9},{2,10},{3,11},{4,12},{5,13},{6,14},{7,15},{8,0},{9,1},... | collective-permute-start | bytes 884744 | tf_op jit(solution)/shard_map/ppermute | solution.py:1272
  74.6 3.9 %back.3 = (f32[336,256]{1,0:T(8,128)S(1)}, bf16[1120,128]{1,0:T(8,128)(2,1)S(1)}, f32[8,128]{1,0:T(8,128)S(1)}) custom-call(bf16[672,256]{1,0:T(8,128)(2,1)S(1)} %copy-done.2, bf16[2,4608,512]{2,1,0:T(8,128)(2,1)} %bitcast.9, f32[336,512]{1,0:T(8,128)S(1)} %get-tuple-element.110.refs_2_, bf16[64,1792]{1,0:T(8,128)(2,1)S(1)} %get-tuple-element.111.refs_3_.refs_2_, ...), custom_call_target="tpu_custom_call" | custom-call | flops 350000000 | bytes 1024 | tf_op jit(solution)/shard_map/back/pallas_call | solution.py:83
  78.6 8.5 %collective-permute-done.14.refs_1_ = bf16[1152,128]{1,0:T(8,128)(2,1)S(1)} collective-permute-done((bf16[1152,128]{1,0:T(8,128)(2,1)S(1)}, bf16[1152,128]{1,0:T(8,128)(2,1)S(1)}, u32[]{:S(2)}, u32[]{:S(2)}) %collective-permute-start.14) | collective-permute-done | bytes 294944 | tf_op jit(solution)/shard_map/ppermute | solution.py:1272
  87.2 2.0 %collective-permute-start.12 = (bf16[1120,128]{1,0:T(8,128)(2,1)S(1)}, bf16[1120,128]{1,0:T(8,128)(2,1)S(1)}, u32[]{:S(2)}, u32[]{:S(2)}) collective-permute-start(bf16[1120,128]{1,0:T(8,128)(2,1)S(1)} %get-tuple-element.138), channel_id=1, source_target_pairs={{0,4},{1,3},{2,6},{3,1},{4,0},{5,7},{6,2},{7,5},{8,12},{9,11},{10,... | collective-permute-start | bytes 860168 | tf_op jit(solution)/shard_map/ppermute | solution.py:1272
  89.2 2.4 %collective-permute-done.13.refs_1_ = bf16[1152,128]{1,0:T(8,128)(2,1)S(1)} collective-permute-done((bf16[1152,128]{1,0:T(8,128)(2,1)S(1)}, bf16[1152,128]{1,0:T(8,128)(2,1)S(1)}, u32[]{:S(2)}, u32[]{:S(2)}) %collective-permute-start.13) | collective-permute-done | bytes 294944 | tf_op jit(solution)/shard_map/ppermute | solution.py:1272
  92.3 5.4 %collective-permute-done.12.refs_1_ = bf16[1120,128]{1,0:T(8,128)(2,1)S(1)} collective-permute-done((bf16[1120,128]{1,0:T(8,128)(2,1)S(1)}, bf16[1120,128]{1,0:T(8,128)(2,1)S(1)}, u32[]{:S(2)}, u32[]{:S(2)}) %collective-permute-start.12) | collective-permute-done | bytes 286752 | tf_op jit(solution)/shard_map/ppermute | solution.py:1272
  97.9 1.6 collective-permute-start.21
  99.5 1.4 collective-permute-done.16.refs_1_
  100.9 1.6 collective-permute-start.20
  102.6 1.3 collective-permute-start.15
  103.8 0.8 collective-permute-start.11
  104.6 9.9 %collective-permute-done.15.refs_1_ = bf16[1120,128]{1,0:T(8,128)(2,1)S(1)} collective-permute-done((bf16[1120,128]{1,0:T(8,128)(2,1)S(1)}, bf16[1120,128]{1,0:T(8,128)(2,1)S(1)}, u32[]{:S(2)}, u32[]{:S(2)}) %collective-permute-start.15) | collective-permute-done | bytes 286752 | tf_op jit(solution)/shard_map/ppermute | solution.py:1272
  114.6 0.9 collective-permute-done.11.refs_3_
  116.3 1.7 %collective-permute-start.27 = (bf16[4608,128]{1,0:T(8,128)(2,1)S(1)}, bf16[4608,128]{1,0:T(8,128)(2,1)S(1)}, u32[]{:S(2)}, u32[]{:S(2)}) collective-permute-start(bf16[4608,128]{1,0:T(8,128)(2,1)S(1)} %get-tuple-element.158.refs_0_), channel_id=1, source_target_pairs={{0,16},{1,5},{2,18},{3,7},{4,20},{5,1},{6,22},{7,3},{8,24},{9,13},... | collective-permute-start | bytes 3538952 | tf_op jit(solution)/shard_map/ppermute | solution.py:1272
  118.0 0.9 collective-permute-start.19
  118.9 8.8 %collective-permute-done.19.refs_1_ = bf16[1120,128]{1,0:T(8,128)(2,1)S(1)} collective-permute-done((bf16[1120,128]{1,0:T(8,128)(2,1)S(1)}, bf16[1120,128]{1,0:T(8,128)(2,1)S(1)}, u32[]{:S(2)}, u32[]{:S(2)}) %collective-permute-start.19) | collective-permute-done | bytes 286752 | tf_op jit(solution)/shard_map/ppermute | solution.py:1272
  127.8 2.1 %collective-permute-start.22 = (bf16[1792,128]{1,0:T(8,128)(2,1)S(1)}, bf16[1792,128]{1,0:T(8,128)(2,1)S(1)}, u32[]{:S(2)}, u32[]{:S(2)}) collective-permute-start(bf16[1792,128]{1,0:T(8,128)(2,1)S(1)} %get-tuple-element.156.refs_0_), channel_id=1, source_target_pairs={{0,2},{1,17},{2,0},{3,19},{4,6},{5,21},{6,4},{7,23},{8,10},{9,25},... | collective-permute-start | bytes 1376264 | tf_op jit(solution)/shard_map/ppermute | solution.py:1272
  130.0 2.9 %widen_trunk.6 = (f32[2,9,512,512]{3,2,1,0:T(8,128)}, f32[8,128]{1,0:T(8,128)S(1)}) custom-call(bf16[4608,128]{1,0:T(8,128)(2,1)S(1)} %get-tuple-element.158.refs_0_, bf16[4608,128]{1,0:T(8,128)(2,1)S(1)} %collective-permute-done.24.refs_1_, f32[8,128]{1,0:T(8,128)S(1)} %get-tuple-element.159.refs_2_), custom_call_target="tpu_custom_call" | custom-call | flops 290000000 | bytes 1024 | tf_op jit(solution)/shard_map/widen_trunk/pallas_call | solution.py:83
  132.9 2.9 %widen_trunk.7 = (f32[2,9,512,512]{3,2,1,0:T(8,128)}, f32[8,128]{1,0:T(8,128)S(1)}) custom-call(bf16[4608,128]{1,0:T(8,128)(2,1)S(1)} %get-tuple-element.157.refs_0_, bf16[4608,128]{1,0:T(8,128)(2,1)S(1)} %collective-permute-done.23.refs_1_, f32[2,9,512,512]{3,2,1,0:T(8,128)} %get-tuple-element.160.refs_2_, ...), custom_call_target="tpu_custom_call", output_to_operand_aliasing={{0}: (2, {})} | custom-call | flops 290000000 | bytes 1024 | tf_op jit(solution)/shard_map/widen_trunk/pallas_call | solution.py:83
  136.5 0.9 collective-permute-done.27.refs_0_
  137.9 1.7 %collective-permute-start.30 = (bf16[3584,128]{1,0:T(8,128)(2,1)S(1)}, bf16[3584,128]{1,0:T(8,128)(2,1)S(1)}, u32[]{:S(2)}, u32[]{:S(2)}) collective-permute-start(bf16[3584,128]{1,0:T(8,128)(2,1)S(1)} %get-tuple-element.163.refs_0_), channel_id=1, source_target_pairs={{0,16},{1,5},{2,18},{3,7},{4,20},{5,1},{6,22},{7,3},{8,24},{9,13},... | collective-permute-start | bytes 2752520 | tf_op jit(solution)/shard_map/ppermute | solution.py:1272
  139.6 1.8 %widen_trunk.8 = (f32[2,9,512,512]{3,2,1,0:T(8,128)}, f32[8,128]{1,0:T(8,128)S(1)}) custom-call(bf16[4608,128]{1,0:T(8,128)(2,1)S(1)} %get-tuple-element.165.refs_0_, f32[2,9,512,512]{3,2,1,0:T(8,128)} %get-tuple-element.166.refs_1_, f32[8,128]{1,0:T(8,128)S(1)} %get-tuple-element.167.refs_2_), custom_call_target="tpu_custom_call", output_to_operand_aliasing={{0}: (1, {})} | custom-call | flops 290000000 | bytes 1024 | tf_op jit(solution)/shard_map/widen_trunk/pallas_call | solution.py:83
  141.4 7.6 %collective-permute-done.26.refs_0_ = bf16[4608,128]{1,0:T(8,128)(2,1)S(1)} collective-permute-done((bf16[4608,128]{1,0:T(8,128)(2,1)S(1)}, bf16[4608,128]{1,0:T(8,128)(2,1)S(1)}, u32[]{:S(2)}, u32[]{:S(2)}) %collective-permute-start.26) | collective-permute-done | bytes 1179680 | tf_op jit(solution)/shard_map/ppermute | solution.py:1272
  149.6 1.8 %widen_trunk.9 = (f32[2,9,512,512]{3,2,1,0:T(8,128)}, f32[8,128]{1,0:T(8,128)S(1)}) custom-call(bf16[4608,128]{1,0:T(8,128)(2,1)S(1)} %collective-permute-done.28.refs_0_, f32[2,9,512,512]{3,2,1,0:T(8,128)} %get-tuple-element.170.refs_1_, f32[8,128]{1,0:T(8,128)S(1)} %get-tuple-element.171.refs_2_), custom_call_target="tpu_custom_call", output_to_operand_aliasing={{0}: (1, {})} | custom-call | flops 290000000 | bytes 1024 | tf_op jit(solution)/shard_map/widen_trunk/pallas_call | solution.py:83
  151.4 1.8 %widen_trunk.10 = (f32[2,9,512,512]{3,2,1,0:T(8,128)}, f32[8,128]{1,0:T(8,128)S(1)}) custom-call(bf16[4608,128]{1,0:T(8,128)(2,1)S(1)} %get-tuple-element.169.refs_0_, f32[2,9,512,512]{3,2,1,0:T(8,128)} %get-tuple-element.172.refs_1_, f32[8,128]{1,0:T(8,128)S(1)} %get-tuple-element.173.refs_2_), custom_call_target="tpu_custom_call", output_to_operand_aliasing={{0}: (1, {})} | custom-call | flops 290000000 | bytes 1024 | tf_op jit(solution)/shard_map/widen_trunk/pallas_call | solution.py:83
  153.2 4.4 %widen_heads.3 = (f32[2,512,1792]{2,1,0:T(8,128)}, f32[8,128]{1,0:T(8,128)S(1)}) custom-call(bf16[3584,128]{1,0:T(8,128)(2,1)S(1)} %get-tuple-element.163.refs_0_, bf16[3584,128]{1,0:T(8,128)(2,1)S(1)} %collective-permute-done.25.refs_1_, f32[8,128]{1,0:T(8,128)S(1)} %get-tuple-element.174.refs_2_), custom_call_target="tpu_custom_call" | custom-call | flops 440000000 | bytes 1024 | tf_op jit(solution)/shard_map/widen_heads/pallas_call | solution.py:83
  157.6 1.6 finish.1
  159.4 1.8 %widen_trunk.11 = (f32[2,9,512,512]{3,2,1,0:T(8,128)}, f32[8,128]{1,0:T(8,128)S(1)}) custom-call(bf16[4608,128]{1,0:T(8,128)(2,1)S(1)} %collective-permute-done.29.refs_0_, f32[2,9,512,512]{3,2,1,0:T(8,128)} %get-tuple-element.178.refs_1_, f32[8,128]{1,0:T(8,128)S(1)} %get-tuple-element.180.refs_2_), custom_call_target="tpu_custom_call", output_to_operand_aliasing={{0}: (1, {})} | custom-call | flops 290000000 | bytes 1024 | tf_op jit(solution)/shard_map/widen_trunk/pallas_call | solution.py:83
  161.2 2.5 %widen_heads.4 = (f32[2,512,1792]{2,1,0:T(8,128)}, f32[8,128]{1,0:T(8,128)S(1)}) custom-call(bf16[3584,128]{1,0:T(8,128)(2,1)S(1)} %get-tuple-element.182.refs_0_, f32[2,512,1792]{2,1,0:T(8,128)} %get-tuple-element.183.refs_1_, f32[8,128]{1,0:T(8,128)S(1)} %get-tuple-element.184.refs_2_), custom_call_target="tpu_custom_call", output_to_operand_aliasing={{0}: (1, {})} | custom-call | flops 440000000 | bytes 1024 | tf_op jit(solution)/shard_map/widen_heads/pallas_call | solution.py:83
  163.7 3.1 %widen_heads.5 = (f32[2,512,1792]{2,1,0:T(8,128)}, f32[8,128]{1,0:T(8,128)}) custom-call(bf16[3584,128]{1,0:T(8,128)(2,1)S(1)} %collective-permute-done.31.refs_0_, f32[2,512,1792]{2,1,0:T(8,128)} %get-tuple-element.185.refs_1_, f32[8,128]{1,0:T(8,128)S(1)} %get-tuple-element.186.refs_2_), custom_call_target="tpu_custom_call", output_to_operand_aliasing={{0}: (1, {})} | custom-call | flops 440000000 | bytes 1024 | tf_op jit(solution)/shard_map/widen_heads/pallas_call | solution.py:83
  (73 shorter events, 8.0 us)
Async XLA Ops:
  12.5 8.6 %collective-permute-start = (bf16[2080,256]{1,0:T(8,128)(2,1)}, bf16[2080,256]{1,0:T(8,128)(2,1)S(1)}, u32[]{:S(2)}, u32[]{:S(2)}) collective-permute-start(bf16[2080,256]{1,0:T(8,128)(2,1)} %get-tuple-element.105), channel_id=1, source_target_pairs={{0,1},{1,0},{2,3},{3,2},{4,5},{5,4},{6,7},{7,6},{8,9},{9,8},{10,11... | collective-permute-start | bytes 3194888 | tf_op jit(solution)/shard_map/ppermute | solution.py:1275
  13.0 8.0 %collective-permute-start.2 = (bf16[672,256]{1,0:T(8,128)(2,1)}, bf16[672,256]{1,0:T(8,128)(2,1)S(1)}, u32[]{:S(2)}, u32[]{:S(2)}) collective-permute-start(bf16[672,256]{1,0:T(8,128)(2,1)} %get-tuple-element.107), channel_id=1, source_target_pairs={{0,16},{1,5},{2,18},{3,7},{4,20},{5,1},{6,22},{7,3},{8,24},{9,13},... | collective-permute-start | bytes 1032200 | tf_op jit(solution)/shard_map/ppermute | solution.py:1272
  20.2 2.0 %copy-start = (bf16[2080,256]{1,0:T(8,128)(2,1)S(1)}, bf16[2080,256]{1,0:T(8,128)(2,1)}, u32[]{:S(2)}) copy-start(bf16[2080,256]{1,0:T(8,128)(2,1)} %get-tuple-element.104.refs_0_.refs_6_) | copy-start | bytes 3194884
  20.2 1.9 %copy-start.2 = (bf16[672,256]{1,0:T(8,128)(2,1)S(1)}, bf16[672,256]{1,0:T(8,128)(2,1)}, u32[]{:S(2)}) copy-start(bf16[672,256]{1,0:T(8,128)(2,1)} %get-tuple-element.101.refs_2_.refs_0_) | copy-start | bytes 1032196
  20.2 1.9 %collective-permute-start.1 = (bf16[672,256]{1,0:T(8,128)(2,1)}, bf16[672,256]{1,0:T(8,128)(2,1)S(1)}, u32[]{:S(2)}, u32[]{:S(2)}) collective-permute-start(bf16[672,256]{1,0:T(8,128)(2,1)} %get-tuple-element.101.refs_2_.refs_0_), channel_id=1, source_target_pairs={{0,1},{1,0},{2,3},{3,2},{4,5},{5,4},{6,7},{7,6},{8,9},{9,8},{10,11... | collective-permute-start | bytes 1032200 | tf_op jit(solution)/shard_map/ppermute | solution.py:1275
  21.0 0.7 copy-start.9
  22.2 4.3 %copy-start.3 = (bf16[2,336,512]{2,1,0:T(8,128)(2,1)S(1)}, bf16[2,336,512]{2,1,0:T(8,128)(2,1)}, u32[]{:S(2)}) copy-start(bf16[2,336,512]{2,1,0:T(8,128)(2,1)} %refs_1_.3) | copy-start | bytes 2064388
  22.2 4.3 %copy-start.4 = (bf16[2,144,512]{2,1,0:T(8,128)(2,1)S(1)}, bf16[2,144,512]{2,1,0:T(8,128)(2,1)}, u32[]{:S(2)}) copy-start(bf16[2,144,512]{2,1,0:T(8,128)(2,1)} %get-tuple-element.102.refs_3_) | copy-start | bytes 884740
  22.2 4.3 %copy-start.5 = (f32[2,3,1792]{2,0,1:T(2,128)S(1)}, f32[2,3,1792]{2,0,1:T(2,128)}, u32[]{:S(2)}) copy-start(f32[2,3,1792]{2,0,1:T(2,128)} %param.16) | copy-start | bytes 129028
  22.2 4.3 %copy-start.6 = (f32[8,512]{1,0:T(8,128)S(1)}, f32[8,512]{1,0:T(8,128)}, u32[]{:S(2)}) copy-start(f32[8,512]{1,0:T(8,128)} %get-tuple-element.103.refs_5_) | copy-start | bytes 49156
  22.2 4.3 %copy-start.7 = (f32[2,512]{1,0:T(2,128)S(1)}, f32[2,512]{1,0:T(2,128)}, u32[]{:S(2)}) copy-start(f32[2,512]{1,0:T(2,128)} %refs_4_.3) | copy-start | bytes 12292
  22.2 4.3 %copy-start.8 = (s32[1,2]{1,0:T(1,128)S(1)}, s32[1,2]{1,0:T(1,128)}, u32[]{:S(2)}) copy-start(s32[1,2]{1,0:T(1,128)} %refs_0_.5) | copy-start | bytes 28
  23.2 16.9 %collective-permute-start.4 = (bf16[1344,256]{1,0:T(8,128)(2,1)S(1)}, bf16[1344,256]{1,0:T(8,128)(2,1)S(1)}, u32[]{:S(2)}, u32[]{:S(2)}) collective-permute-start(bf16[1344,256]{1,0:T(8,128)(2,1)S(1)} %get-tuple-element.114), channel_id=1, source_target_pairs={{0,2},{1,5},{2,0},{3,7},{4,6},{5,1},{6,4},{7,3},{8,10},{9,13},{10,... | collective-permute-start | bytes 2064392 | tf_op jit(solution)/shard_map/ppermute | solution.py:1272
  25.0 10.3 %collective-permute-start.5 = (bf16[672,256]{1,0:T(8,128)(2,1)S(1)}, bf16[672,256]{1,0:T(8,128)(2,1)S(1)}, u32[]{:S(2)}, u32[]{:S(2)}) collective-permute-start(bf16[672,256]{1,0:T(8,128)(2,1)S(1)} %get-tuple-element.115), channel_id=1, source_target_pairs={{0,16},{1,5},{2,18},{3,7},{4,20},{5,1},{6,22},{7,3},{8,24},{9,13},... | collective-permute-start | bytes 1032200 | tf_op jit(solution)/shard_map/ppermute | solution.py:1272
  26.5 2.0 %copy-start.1 = (bf16[2,512,1792]{2,1,0:T(8,128)(2,1)S(1)}, bf16[2,512,1792]{2,1,0:T(8,128)(2,1)}, u32[]{:S(2)}) copy-start(bf16[2,512,1792]{2,1,0:T(8,128)(2,1)} %refs_2_.1) | copy-start | bytes 11010052
  34.7 28.9 %collective-permute-start.3 = (bf16[3808,128]{1,0:T(8,128)(2,1)S(1)}, bf16[3808,128]{1,0:T(8,128)(2,1)S(1)}, u32[]{:S(2)}, u32[]{:S(2)}) collective-permute-start(bf16[3808,128]{1,0:T(8,128)(2,1)S(1)} %get-tuple-element.113), channel_id=1, source_target_pairs={{0,16},{1,5},{2,18},{3,7},{4,20},{5,1},{6,22},{7,3},{8,24},{9,13},... | collective-permute-start | bytes 2924552 | tf_op jit(solution)/shard_map/ppermute | solution.py:1272
  39.7 10.5 %collective-permute-start.7 = (bf16[2304,128]{1,0:T(8,128)(2,1)S(1)}, bf16[2304,128]{1,0:T(8,128)(2,1)S(1)}, u32[]{:S(2)}, u32[]{:S(2)}) collective-permute-start(bf16[2304,128]{1,0:T(8,128)(2,1)S(1)} %get-tuple-element.121), channel_id=1, source_target_pairs={{0,2},{1,17},{2,0},{3,19},{4,6},{5,21},{6,4},{7,23},{8,10},{9,25},... | collective-permute-start | bytes 1769480 | tf_op jit(solution)/shard_map/ppermute | solution.py:1272
  43.8 17.9 %collective-permute-start.6 = (bf16[2304,128]{1,0:T(8,128)(2,1)S(1)}, bf16[2304,128]{1,0:T(8,128)(2,1)S(1)}, u32[]{:S(2)}, u32[]{:S(2)}) collective-permute-start(bf16[2304,128]{1,0:T(8,128)(2,1)S(1)} %get-tuple-element.119), channel_id=1, source_target_pairs={{0,16},{1,3},{2,18},{3,1},{4,20},{5,7},{6,22},{7,5},{8,24},{9,11},... | collective-permute-start | bytes 1769480 | tf_op jit(solution)/shard_map/ppermute | solution.py:1272
  50.3 14.3 %collective-permute-start.10 = (bf16[1152,128]{1,0:T(8,128)(2,1)S(1)}, bf16[1152,128]{1,0:T(8,128)(2,1)S(1)}, u32[]{:S(2)}, u32[]{:S(2)}) collective-permute-start(bf16[1152,128]{1,0:T(8,128)(2,1)S(1)} %get-tuple-element.130), channel_id=1, source_target_pairs={{0,4},{1,3},{2,6},{3,1},{4,0},{5,7},{6,2},{7,5},{8,12},{9,11},{10,... | collective-permute-start | bytes 884744 | tf_op jit(solution)/shard_map/ppermute | solution.py:1272
  61.8 9.8 %collective-permute-start.9 = (bf16[1152,128]{1,0:T(8,128)(2,1)S(1)}, bf16[1152,128]{1,0:T(8,128)(2,1)S(1)}, u32[]{:S(2)}, u32[]{:S(2)}) collective-permute-start(bf16[1152,128]{1,0:T(8,128)(2,1)S(1)} %get-tuple-element.128), channel_id=1, source_target_pairs={{0,4},{1,17},{2,6},{3,19},{4,0},{5,21},{6,2},{7,23},{8,12},{9,25},... | collective-permute-start | bytes 884744 | tf_op jit(solution)/shard_map/ppermute | solution.py:1272
  63.9 10.5 %collective-permute-start.8 = (bf16[2016,128]{1,0:T(8,128)(2,1)S(1)}, bf16[2016,128]{1,0:T(8,128)(2,1)S(1)}, u32[]{:S(2)}, u32[]{:S(2)}) collective-permute-start(bf16[2016,128]{1,0:T(8,128)(2,1)S(1)} %get-tuple-element.126), channel_id=1, source_target_pairs={{0,2},{1,17},{2,0},{3,19},{4,6},{5,21},{6,4},{7,23},{8,10},{9,25},... | collective-permute-start | bytes 1548296 | tf_op jit(solution)/shard_map/ppermute | solution.py:1272
  64.6 22.4 %collective-permute-start.14 = (bf16[1152,128]{1,0:T(8,128)(2,1)S(1)}, bf16[1152,128]{1,0:T(8,128)(2,1)S(1)}, u32[]{:S(2)}, u32[]{:S(2)}) collective-permute-start(bf16[1152,128]{1,0:T(8,128)(2,1)S(1)} %get-tuple-element.140.refs_0_), channel_id=1, source_target_pairs={{0,8},{1,9},{2,10},{3,11},{4,12},{5,13},{6,14},{7,15},{8,0},{9,1},... | collective-permute-start | bytes 884744 | tf_op jit(solution)/shard_map/ppermute | solution.py:1272
  71.7 19.9 %collective-permute-start.13 = (bf16[1152,128]{1,0:T(8,128)(2,1)S(1)}, bf16[1152,128]{1,0:T(8,128)(2,1)S(1)}, u32[]{:S(2)}, u32[]{:S(2)}) collective-permute-start(bf16[1152,128]{1,0:T(8,128)(2,1)S(1)} %get-tuple-element.139.refs_0_), channel_id=1, source_target_pairs={{0,8},{1,9},{2,10},{3,11},{4,12},{5,13},{6,14},{7,15},{8,0},{9,1},... | collective-permute-start | bytes 884744 | tf_op jit(solution)/shard_map/ppermute | solution.py:1272
  87.1 10.7 %collective-permute-start.17 = (bf16[1152,128]{1,0:T(8,128)(2,1)S(1)}, bf16[1152,128]{1,0:T(8,128)(2,1)S(1)}, u32[]{:S(2)}, u32[]{:S(2)}) collective-permute-start(bf16[1152,128]{1,0:T(8,128)(2,1)S(1)} %get-tuple-element.146.refs_0_), channel_id=1, source_target_pairs={{0,4},{1,3},{2,6},{3,1},{4,0},{5,7},{6,2},{7,5},{8,12},{9,11},{10,... | collective-permute-start | bytes 884744 | tf_op jit(solution)/shard_map/ppermute | solution.py:1272
  87.2 10.6 %collective-permute-start.12 = (bf16[1120,128]{1,0:T(8,128)(2,1)S(1)}, bf16[1120,128]{1,0:T(8,128)(2,1)S(1)}, u32[]{:S(2)}, u32[]{:S(2)}) collective-permute-start(bf16[1120,128]{1,0:T(8,128)(2,1)S(1)} %get-tuple-element.138), channel_id=1, source_target_pairs={{0,4},{1,3},{2,6},{3,1},{4,0},{5,7},{6,2},{7,5},{8,12},{9,11},{10,... | collective-permute-start | bytes 860168 | tf_op jit(solution)/shard_map/ppermute | solution.py:1272
  91.6 9.2 %collective-permute-start.16 = (bf16[1152,128]{1,0:T(8,128)(2,1)S(1)}, bf16[1152,128]{1,0:T(8,128)(2,1)S(1)}, u32[]{:S(2)}, u32[]{:S(2)}) collective-permute-start(bf16[1152,128]{1,0:T(8,128)(2,1)S(1)} %get-tuple-element.145.refs_0_), channel_id=1, source_target_pairs={{0,4},{1,17},{2,6},{3,19},{4,0},{5,21},{6,2},{7,23},{8,12},{9,25},... | collective-permute-start | bytes 884744 | tf_op jit(solution)/shard_map/ppermute | solution.py:1272
  97.9 17.6 %collective-permute-start.21 = (bf16[2304,128]{1,0:T(8,128)(2,1)S(1)}, bf16[2304,128]{1,0:T(8,128)(2,1)S(1)}, u32[]{:S(2)}, u32[]{:S(2)}) collective-permute-start(bf16[2304,128]{1,0:T(8,128)(2,1)S(1)} %get-tuple-element.152.refs_0_), channel_id=1, source_target_pairs={{0,2},{1,17},{2,0},{3,19},{4,6},{5,21},{6,4},{7,23},{8,10},{9,25},... | collective-permute-start | bytes 1769480 | tf_op jit(solution)/shard_map/ppermute | solution.py:1272
  100.9 14.7 %collective-permute-start.20 = (bf16[2304,128]{1,0:T(8,128)(2,1)S(1)}, bf16[2304,128]{1,0:T(8,128)(2,1)S(1)}, u32[]{:S(2)}, u32[]{:S(2)}) collective-permute-start(bf16[2304,128]{1,0:T(8,128)(2,1)S(1)} %get-tuple-element.151.refs_0_), channel_id=1, source_target_pairs={{0,16},{1,3},{2,18},{3,1},{4,20},{5,7},{6,22},{7,5},{8,24},{9,11},... | collective-permute-start | bytes 1769480 | tf_op jit(solution)/shard_map/ppermute | solution.py:1272
  102.6 11.9 %collective-permute-start.15 = (bf16[1120,128]{1,0:T(8,128)(2,1)S(1)}, bf16[1120,128]{1,0:T(8,128)(2,1)S(1)}, u32[]{:S(2)}, u32[]{:S(2)}) collective-permute-start(bf16[1120,128]{1,0:T(8,128)(2,1)S(1)} %get-tuple-element.144.refs_0_), channel_id=1, source_target_pairs={{0,8},{1,9},{2,10},{3,11},{4,12},{5,13},{6,14},{7,15},{8,0},{9,1},... | collective-permute-start | bytes 860168 | tf_op jit(solution)/shard_map/ppermute | solution.py:1272
  103.8 11.6 %collective-permute-start.11 = (bf16[1120,128]{1,0:T(8,128)(2,1)S(1)}, bf16[1120,128]{1,0:T(8,128)(2,1)S(1)}, u32[]{:S(2)}, u32[]{:S(2)}) collective-permute-start(bf16[1120,128]{1,0:T(8,128)(2,1)S(1)} %get-tuple-element.136), channel_id=1, source_target_pairs={{0,16},{16,0},{1,17},{17,1},{2,18},{18,2},{3,19},{19,3},{4,20},{20... | collective-permute-start | bytes 860168 | tf_op jit(solution)/shard_map/ppermute | solution.py:1345
  115.5 14.5 %collective-permute-start.24 = (bf16[4608,128]{1,0:T(8,128)(2,1)S(1)}, bf16[4608,128]{1,0:T(8,128)(2,1)S(1)}, u32[]{:S(2)}, u32[]{:S(2)}) collective-permute-start(bf16[4608,128]{1,0:T(8,128)(2,1)S(1)} %get-tuple-element.158.refs_0_), channel_id=1, source_target_pairs={{0,1},{1,0},{2,3},{3,2},{4,5},{5,4},{6,7},{7,6},{8,9},{9,8},{10,11... | collective-permute-start | bytes 3538952 | tf_op jit(solution)/shard_map/ppermute | solution.py:1275
  115.7 17.2 %collective-permute-start.23 = (bf16[4608,128]{1,0:T(8,128)(2,1)S(1)}, bf16[4608,128]{1,0:T(8,128)(2,1)S(1)}, u32[]{:S(2)}, u32[]{:S(2)}) collective-permute-start(bf16[4608,128]{1,0:T(8,128)(2,1)S(1)} %get-tuple-element.157.refs_0_), channel_id=1, source_target_pairs={{0,1},{1,0},{2,3},{3,2},{4,5},{5,4},{6,7},{7,6},{8,9},{9,8},{10,11... | collective-permute-start | bytes 3538952 | tf_op jit(solution)/shard_map/ppermute | solution.py:1275
  116.3 21.1 %collective-permute-start.27 = (bf16[4608,128]{1,0:T(8,128)(2,1)S(1)}, bf16[4608,128]{1,0:T(8,128)(2,1)S(1)}, u32[]{:S(2)}, u32[]{:S(2)}) collective-permute-start(bf16[4608,128]{1,0:T(8,128)(2,1)S(1)} %get-tuple-element.158.refs_0_), channel_id=1, source_target_pairs={{0,16},{1,5},{2,18},{3,7},{4,20},{5,1},{6,22},{7,3},{8,24},{9,13},... | collective-permute-start | bytes 3538952 | tf_op jit(solution)/shard_map/ppermute | solution.py:1272
  118.0 9.8 %collective-permute-start.19 = (bf16[1120,128]{1,0:T(8,128)(2,1)S(1)}, bf16[1120,128]{1,0:T(8,128)(2,1)S(1)}, u32[]{:S(2)}, u32[]{:S(2)}) collective-permute-start(bf16[1120,128]{1,0:T(8,128)(2,1)S(1)} %get-tuple-element.150.refs_0_.refs_4_), channel_id=1, source_target_pairs={{0,4},{1,3},{2,6},{3,1},{4,0},{5,7},{6,2},{7,5},{8,12},{9,11},{10,... | collective-permute-start | bytes 860168 | tf_op jit(solution)/shard_map/ppermute | solution.py:1272
  127.8 8.6 %collective-permute-start.22 = (bf16[1792,128]{1,0:T(8,128)(2,1)S(1)}, bf16[1792,128]{1,0:T(8,128)(2,1)S(1)}, u32[]{:S(2)}, u32[]{:S(2)}) collective-permute-start(bf16[1792,128]{1,0:T(8,128)(2,1)S(1)} %get-tuple-element.156.refs_0_), channel_id=1, source_target_pairs={{0,2},{1,17},{2,0},{3,19},{4,6},{5,21},{6,4},{7,23},{8,10},{9,25},... | collective-permute-start | bytes 1376264 | tf_op jit(solution)/shard_map/ppermute | solution.py:1272
  130.0 19.1 %collective-permute-start.26 = (bf16[4608,128]{1,0:T(8,128)(2,1)S(1)}, bf16[4608,128]{1,0:T(8,128)(2,1)S(1)}, u32[]{:S(2)}, u32[]{:S(2)}) collective-permute-start(bf16[4608,128]{1,0:T(8,128)(2,1)S(1)} %get-tuple-element.157.refs_0_), channel_id=1, source_target_pairs={{0,2},{1,5},{2,0},{3,7},{4,6},{5,1},{6,4},{7,3},{8,10},{9,13},{10,... | collective-permute-start | bytes 3538952 | tf_op jit(solution)/shard_map/ppermute | solution.py:1272
  137.4 12.2 %collective-permute-start.28 = (bf16[4608,128]{1,0:T(8,128)(2,1)S(1)}, bf16[4608,128]{1,0:T(8,128)(2,1)S(1)}, u32[]{:S(2)}, u32[]{:S(2)}) collective-permute-start(bf16[4608,128]{1,0:T(8,128)(2,1)S(1)} %get-tuple-element.165.refs_0_), channel_id=1, source_target_pairs={{0,1},{1,0},{2,3},{3,2},{4,5},{5,4},{6,7},{7,6},{8,9},{9,8},{10,11... | collective-permute-start | bytes 3538952 | tf_op jit(solution)/shard_map/ppermute | solution.py:1275
  137.4 15.8 %collective-permute-start.25 = (bf16[3584,128]{1,0:T(8,128)(2,1)S(1)}, bf16[3584,128]{1,0:T(8,128)(2,1)S(1)}, u32[]{:S(2)}, u32[]{:S(2)}) collective-permute-start(bf16[3584,128]{1,0:T(8,128)(2,1)S(1)} %get-tuple-element.163.refs_0_), channel_id=1, source_target_pairs={{0,1},{1,0},{2,3},{3,2},{4,5},{5,4},{6,7},{7,6},{8,9},{9,8},{10,11... | collective-permute-start | bytes 2752520 | tf_op jit(solution)/shard_map/ppermute | solution.py:1275
  137.9 21.3 %collective-permute-start.30 = (bf16[3584,128]{1,0:T(8,128)(2,1)S(1)}, bf16[3584,128]{1,0:T(8,128)(2,1)S(1)}, u32[]{:S(2)}, u32[]{:S(2)}) collective-permute-start(bf16[3584,128]{1,0:T(8,128)(2,1)S(1)} %get-tuple-element.163.refs_0_), channel_id=1, source_target_pairs={{0,16},{1,5},{2,18},{3,7},{4,20},{5,1},{6,22},{7,3},{8,24},{9,13},... | collective-permute-start | bytes 2752520 | tf_op jit(solution)/shard_map/ppermute | solution.py:1272
  149.1 10.3 %collective-permute-start.29 = (bf16[4608,128]{1,0:T(8,128)(2,1)S(1)}, bf16[4608,128]{1,0:T(8,128)(2,1)S(1)}, u32[]{:S(2)}, u32[]{:S(2)}) collective-permute-start(bf16[4608,128]{1,0:T(8,128)(2,1)S(1)} %get-tuple-element.169.refs_0_), channel_id=1, source_target_pairs={{0,1},{1,0},{2,3},{3,2},{4,5},{5,4},{6,7},{7,6},{8,9},{9,8},{10,11... | collective-permute-start | bytes 3538952 | tf_op jit(solution)/shard_map/ppermute | solution.py:1275
  149.1 8.5 %collective-permute-start.18 = (bf16[1120,128]{1,0:T(8,128)(2,1)S(1)}, bf16[1120,128]{1,0:T(8,128)(2,1)S(1)}, u32[]{:S(2)}, u32[]{:S(2)}) collective-permute-start(bf16[1120,128]{1,0:T(8,128)(2,1)S(1)} %get-tuple-element.150.refs_0_.refs_4_), channel_id=1, source_target_pairs={{0,1},{1,0},{2,3},{3,2},{4,5},{5,4},{6,7},{7,6},{8,9},{9,8},{10,11... | collective-permute-start | bytes 860168 | tf_op jit(solution)/shard_map/ppermute | solution.py:1275
  159.3 4.5 %collective-permute-start.31 = (bf16[3584,128]{1,0:T(8,128)(2,1)S(1)}, bf16[3584,128]{1,0:T(8,128)(2,1)S(1)}, u32[]{:S(2)}, u32[]{:S(2)}) collective-permute-start(bf16[3584,128]{1,0:T(8,128)(2,1)S(1)} %get-tuple-element.182.refs_0_), channel_id=1, source_target_pairs={{0,1},{1,0},{2,3},{3,2},{4,5},{5,4},{6,7},{7,6},{8,9},{9,8},{10,11... | collective-permute-start | bytes 2752520 | tf_op jit(solution)/shard_map/ppermute | solution.py:1275

commit v4 on v3

--- a/solution.py
+++ b/solution.py
@@ -1200,10 +1200,10 @@
     "H6",
     "Lnew",
     "Lnew_own",
+    "Hold_wide",
     "Enew",
     "Lnew_other",
     "Enew_own",
-    "Hold_wide",
     "finish",
     "Hnew",
     "Enew_other",

time: 167 us -> 165 us (0.988)
  waiting for transfers between devices: 65.4 us -> 61.5 us
    ppermute x22, waiting for transfers between devices: 64.2 us -> 60.3 us  [swap(): return lax.ppermute(block, AXES, route)]
  transfers between devices with their start and end apart: 32 -> 32, of which waited for: 15 -> 15; matrix products, arithmetic and copies ran while one was open for 0% -> 0% of each run, Pallas kernels for 27% -> 28%
where the time goes in v4:
time: 165 us
  Pallas kernels  61.8 us (37%)
  waiting for transfers between devices  61.5 us (37%)
  starting transfers between devices  37.3 us (23%)
  local copies, waits for them, and re-layouts  2.76 us (2%)
    pallas_call x37, Pallas kernels, call(): pl.pallas_call(run, out_shape=(*shapes, jax.ShapeDtypeStruct((8, 128), F3...  61.8 us
    ppermute x22, waiting for transfers between devices, swap(): return lax.ppermute(block, AXES, route)  60.3 us
    ppermute x22, starting transfers between devices, swap(): return lax.ppermute(block, AXES, route)  32.5 us
    ppermute x9, starting transfers between devices, swap_cores(): return lax.ppermute(block, AXES, [(i, i ^ 1) for i in range(devices)])  4.09 us
  transfers between devices with their start and end apart: 32, of which 15 were waited for; matrix products, arithmetic and copies ran while one was open for 0% of the time, Pallas kernels for 28%

profile of v4, /device:TPU:0, one launch (start us, length us, event | category | flops | bytes accessed | tf_op | source)
XLA Modules:
  0.0 164.6 jit_solution(14612235481544985668)
XLA Ops:
  0.6 11.8 %section.1 = (bf16[2080,256]{1,0:T(8,128)(2,1)}, bf16[2080,256]{1,0:T(8,128)(2,1)}, bf16[672,256]{1,0:T(8,128)(2,1)}, bf16[672,256]{1,0:T(8,128)(2,1)}, f32[336,...) custom-call(s32[1,2]{1,0:T(1,128)} %refs_0_.5, bf16[2,336,512]{2,1,0:T(8,128)(2,1)} %refs_1_.3, ...), custom_call_target="tpu_custom_call" | custom-call | flops 1150000000 | bytes 1024 | tf_op jit(solution)/shard_map/section/pallas_call | solution.py:83
  13.0 2.6 %collective-permute-start.2 = (bf16[672,256]{1,0:T(8,128)(2,1)}, bf16[672,256]{1,0:T(8,128)(2,1)S(1)}, u32[]{:S(2)}, u32[]{:S(2)}) collective-permute-start(bf16[672,256]{1,0:T(8,128)(2,1)} %get-tuple-element.107), channel_id=1, source_target_pairs={{0,16},{1,5},{2,18},{3,7},{4,20},{5,1},{6,22},{7,3},{8,24},{9,13},... | collective-permute-start | bytes 1032200 | tf_op jit(solution)/shard_map/ppermute | solution.py:1272
  15.6 4.6 %back.2 = (bf16[672,256]{1,0:T(8,128)(2,1)}, f32[8,128]{1,0:T(8,128)}) custom-call(bf16[672,256]{1,0:T(8,128)(2,1)} %get-tuple-element.98.refs_0_, bf16[2,4608,512]{2,1,0:T(8,128)(2,1)} %bitcast.8, f32[336,512]{1,0:T(8,128)} %get-tuple-element.99.refs_2_, f32[8,128]{1,0:T(8,128)} %get-tuple-element.100.refs_3_), custom_call_target="tpu_custom_call" | custom-call | flops 350000000 | bytes 1024 | tf_op jit(solution)/shard_map/back/pallas_call | solution.py:83
  22.2 0.9 first_factors.1
  23.2 1.8 %collective-permute-start.4 = (bf16[1344,256]{1,0:T(8,128)(2,1)S(1)}, bf16[1344,256]{1,0:T(8,128)(2,1)S(1)}, u32[]{:S(2)}, u32[]{:S(2)}) collective-permute-start(bf16[1344,256]{1,0:T(8,128)(2,1)S(1)} %get-tuple-element.114), channel_id=1, source_target_pairs={{0,2},{1,5},{2,0},{3,7},{4,6},{5,1},{6,4},{7,3},{8,10},{9,13},{10,... | collective-permute-start | bytes 2064392 | tf_op jit(solution)/shard_map/ppermute | solution.py:1272
  25.0 1.5 collective-permute-start.5
  26.5 2.0 %copy-done.1 = bf16[2,512,1792]{2,1,0:T(8,128)(2,1)S(1)} copy-done((bf16[2,512,1792]{2,1,0:T(8,128)(2,1)S(1)}, bf16[2,512,1792]{2,1,0:T(8,128)(2,1)}, u32[]{:S(2)}) %copy-start.1) | copy-done | bytes 3670040
  28.5 6.2 %head_grads.1 = (bf16[3808,128]{1,0:T(8,128)(2,1)S(1)}, bf16[3808,128]{1,0:T(8,128)(2,1)S(1)}, bf16[64,1792]{1,0:T(8,128)(2,1)S(1)}, f32[336,512]{1,0:T(8,128)S(1)}, f32[8,128]{1,0:T(8,128)S(1)}) custom-call(s32[1,2]{1,0:T(1,128)S(1)} %copy-done.8, bf16[2,336,512]{2,1,0:T(8,128)(2,1)S(1)} %copy-done.3, bf16[2,512,1792]{2,1,0:T(8,128)(2,1)S(1)} %copy-done.1, ...), custom_call_target="tpu_custom_call" | custom-call | flops 610000000 | bytes 1024 | tf_op jit(solution)/shard_map/head_grads/pallas_call | solution.py:83
  35.3 4.4 %late_grads.1 = (bf16[2304,128]{1,0:T(8,128)(2,1)S(1)}, bf16[2304,128]{1,0:T(8,128)(2,1)S(1)}, f32[8,128]{1,0:T(8,128)S(1)}) custom-call(bf16[2080,256]{1,0:T(8,128)(2,1)S(1)} %copy-done, bf16[2080,256]{1,0:T(8,128)(2,1)S(1)} %collective-permute-done.refs_0_.refs_1_.refs_7_, bf16[672,256]{1,0:T(8,128)(2,1)S(1)} %collective-permute-done.2.refs_2_, ...), custom_call_target="tpu_custom_call" | custom-call | flops 430000000 | bytes 1024 | tf_op jit(solution)/shard_map/late_grads/pallas_call | solution.py:83
  40.1 3.7 %early_grads.1 = (bf16[2304,128]{1,0:T(8,128)(2,1)S(1)}, bf16[2304,128]{1,0:T(8,128)(2,1)S(1)}, f32[8,128]{1,0:T(8,128)S(1)}) custom-call(bf16[2080,256]{1,0:T(8,128)(2,1)S(1)} %copy-done, bf16[2080,256]{1,0:T(8,128)(2,1)S(1)} %collective-permute-done.refs_0_.refs_1_.refs_7_, bf16[672,256]{1,0:T(8,128)(2,1)S(1)} %copy-done.2, ...), custom_call_target="tpu_custom_call" | custom-call | flops 370000000 | bytes 1024 | tf_op jit(solution)/shard_map/early_grads/pallas_call | solution.py:83
  43.8 1.8 %collective-permute-start.6 = (bf16[2304,128]{1,0:T(8,128)(2,1)S(1)}, bf16[2304,128]{1,0:T(8,128)(2,1)S(1)}, u32[]{:S(2)}, u32[]{:S(2)}) collective-permute-start(bf16[2304,128]{1,0:T(8,128)(2,1)S(1)} %get-tuple-element.119), channel_id=1, source_target_pairs={{0,16},{1,3},{2,18},{3,1},{4,20},{5,7},{6,22},{7,5},{8,24},{9,11},... | collective-permute-start | bytes 1769480 | tf_op jit(solution)/shard_map/ppermute | solution.py:1272
  45.6 4.6 %collective-permute-done.7.refs_1_ = bf16[2304,128]{1,0:T(8,128)(2,1)S(1)} collective-permute-done((bf16[2304,128]{1,0:T(8,128)(2,1)S(1)}, bf16[2304,128]{1,0:T(8,128)(2,1)S(1)}, u32[]{:S(2)}, u32[]{:S(2)}) %collective-permute-start.7) | collective-permute-done | bytes 589856 | tf_op jit(solution)/shard_map/ppermute | solution.py:1272
  50.3 2.1 %collective-permute-start.10 = (bf16[1152,128]{1,0:T(8,128)(2,1)S(1)}, bf16[1152,128]{1,0:T(8,128)(2,1)S(1)}, u32[]{:S(2)}, u32[]{:S(2)}) collective-permute-start(bf16[1152,128]{1,0:T(8,128)(2,1)S(1)} %get-tuple-element.130), channel_id=1, source_target_pairs={{0,4},{1,3},{2,6},{3,1},{4,0},{5,7},{6,2},{7,5},{8,12},{9,11},{10,... | collective-permute-start | bytes 884744 | tf_op jit(solution)/shard_map/ppermute | solution.py:1272
  52.4 9.3 %collective-permute-done.6.refs_1_ = bf16[2304,128]{1,0:T(8,128)(2,1)S(1)} collective-permute-done((bf16[2304,128]{1,0:T(8,128)(2,1)S(1)}, bf16[2304,128]{1,0:T(8,128)(2,1)S(1)}, u32[]{:S(2)}, u32[]{:S(2)}) %collective-permute-start.6) | collective-permute-done | bytes 589856 | tf_op jit(solution)/shard_map/ppermute | solution.py:1272
  61.8 1.8 %collective-permute-start.9 = (bf16[1152,128]{1,0:T(8,128)(2,1)S(1)}, bf16[1152,128]{1,0:T(8,128)(2,1)S(1)}, u32[]{:S(2)}, u32[]{:S(2)}) collective-permute-start(bf16[1152,128]{1,0:T(8,128)(2,1)S(1)} %get-tuple-element.128), channel_id=1, source_target_pairs={{0,4},{1,17},{2,6},{3,19},{4,0},{5,21},{6,2},{7,23},{8,12},{9,25},... | collective-permute-start | bytes 884744 | tf_op jit(solution)/shard_map/ppermute | solution.py:1272
  64.6 2.7 %collective-permute-start.14 = (bf16[1152,128]{1,0:T(8,128)(2,1)S(1)}, bf16[1152,128]{1,0:T(8,128)(2,1)S(1)}, u32[]{:S(2)}, u32[]{:S(2)}) collective-permute-start(bf16[1152,128]{1,0:T(8,128)(2,1)S(1)} %get-tuple-element.140.refs_0_), channel_id=1, source_target_pairs={{0,8},{1,9},{2,10},{3,11},{4,12},{5,13},{6,14},{7,15},{8,0},{9,1},... | collective-permute-start | bytes 884744 | tf_op jit(solution)/shard_map/ppermute | solution.py:1272
  67.3 4.3 %collective-permute-done.9.refs_1_ = bf16[1152,128]{1,0:T(8,128)(2,1)S(1)} collective-permute-done((bf16[1152,128]{1,0:T(8,128)(2,1)S(1)}, bf16[1152,128]{1,0:T(8,128)(2,1)S(1)}, u32[]{:S(2)}, u32[]{:S(2)}) %collective-permute-start.9) | collective-permute-done | bytes 294944 | tf_op jit(solution)/shard_map/ppermute | solution.py:1272
  71.7 2.8 %collective-permute-start.13 = (bf16[1152,128]{1,0:T(8,128)(2,1)S(1)}, bf16[1152,128]{1,0:T(8,128)(2,1)S(1)}, u32[]{:S(2)}, u32[]{:S(2)}) collective-permute-start(bf16[1152,128]{1,0:T(8,128)(2,1)S(1)} %get-tuple-element.139.refs_0_), channel_id=1, source_target_pairs={{0,8},{1,9},{2,10},{3,11},{4,12},{5,13},{6,14},{7,15},{8,0},{9,1},... | collective-permute-start | bytes 884744 | tf_op jit(solution)/shard_map/ppermute | solution.py:1272
  74.6 3.9 %back.3 = (f32[336,256]{1,0:T(8,128)S(1)}, bf16[1120,128]{1,0:T(8,128)(2,1)S(1)}, f32[8,128]{1,0:T(8,128)S(1)}) custom-call(bf16[672,256]{1,0:T(8,128)(2,1)S(1)} %copy-done.2, bf16[2,4608,512]{2,1,0:T(8,128)(2,1)} %bitcast.9, f32[336,512]{1,0:T(8,128)S(1)} %get-tuple-element.110.refs_2_, bf16[64,1792]{1,0:T(8,128)(2,1)S(1)} %get-tuple-element.111.refs_3_.refs_2_, ...), custom_call_target="tpu_custom_call" | custom-call | flops 350000000 | bytes 1024 | tf_op jit(solution)/shard_map/back/pallas_call | solution.py:83
  78.6 8.5 %collective-permute-done.14.refs_1_ = bf16[1152,128]{1,0:T(8,128)(2,1)S(1)} collective-permute-done((bf16[1152,128]{1,0:T(8,128)(2,1)S(1)}, bf16[1152,128]{1,0:T(8,128)(2,1)S(1)}, u32[]{:S(2)}, u32[]{:S(2)}) %collective-permute-start.14) | collective-permute-done | bytes 294944 | tf_op jit(solution)/shard_map/ppermute | solution.py:1272
  87.2 2.0 %collective-permute-start.12 = (bf16[1120,128]{1,0:T(8,128)(2,1)S(1)}, bf16[1120,128]{1,0:T(8,128)(2,1)S(1)}, u32[]{:S(2)}, u32[]{:S(2)}) collective-permute-start(bf16[1120,128]{1,0:T(8,128)(2,1)S(1)} %get-tuple-element.138), channel_id=1, source_target_pairs={{0,4},{1,3},{2,6},{3,1},{4,0},{5,7},{6,2},{7,5},{8,12},{9,11},{10,... | collective-permute-start | bytes 860168 | tf_op jit(solution)/shard_map/ppermute | solution.py:1272
  89.2 2.4 %collective-permute-done.13.refs_1_ = bf16[1152,128]{1,0:T(8,128)(2,1)S(1)} collective-permute-done((bf16[1152,128]{1,0:T(8,128)(2,1)S(1)}, bf16[1152,128]{1,0:T(8,128)(2,1)S(1)}, u32[]{:S(2)}, u32[]{:S(2)}) %collective-permute-start.13) | collective-permute-done | bytes 294944 | tf_op jit(solution)/shard_map/ppermute | solution.py:1272
  92.3 5.4 %collective-permute-done.12.refs_1_ = bf16[1120,128]{1,0:T(8,128)(2,1)S(1)} collective-permute-done((bf16[1120,128]{1,0:T(8,128)(2,1)S(1)}, bf16[1120,128]{1,0:T(8,128)(2,1)S(1)}, u32[]{:S(2)}, u32[]{:S(2)}) %collective-permute-start.12) | collective-permute-done | bytes 286752 | tf_op jit(solution)/shard_map/ppermute | solution.py:1272
  97.9 1.6 collective-permute-start.20
  99.5 1.4 collective-permute-done.16.refs_1_
  100.9 1.6 collective-permute-start.19
  102.6 1.3 collective-permute-start.15
  103.8 0.7 collective-permute-start.11
  104.6 9.9 %collective-permute-done.15.refs_1_ = bf16[1120,128]{1,0:T(8,128)(2,1)S(1)} collective-permute-done((bf16[1120,128]{1,0:T(8,128)(2,1)S(1)}, bf16[1120,128]{1,0:T(8,128)(2,1)S(1)}, u32[]{:S(2)}, u32[]{:S(2)}) %collective-permute-start.15) | collective-permute-done | bytes 286752 | tf_op jit(solution)/shard_map/ppermute | solution.py:1272
  114.5 0.9 collective-permute-done.11.refs_3_
  116.3 1.7 %collective-permute-start.27 = (bf16[4608,128]{1,0:T(8,128)(2,1)S(1)}, bf16[4608,128]{1,0:T(8,128)(2,1)S(1)}, u32[]{:S(2)}, u32[]{:S(2)}) collective-permute-start(bf16[4608,128]{1,0:T(8,128)(2,1)S(1)} %get-tuple-element.158.refs_0_), channel_id=1, source_target_pairs={{0,16},{1,5},{2,18},{3,7},{4,20},{5,1},{6,22},{7,3},{8,24},{9,13},... | collective-permute-start | bytes 3538952 | tf_op jit(solution)/shard_map/ppermute | solution.py:1272
  118.0 0.9 collective-permute-start.22
  118.9 8.8 %collective-permute-done.22.refs_1_ = bf16[1120,128]{1,0:T(8,128)(2,1)S(1)} collective-permute-done((bf16[1120,128]{1,0:T(8,128)(2,1)S(1)}, bf16[1120,128]{1,0:T(8,128)(2,1)S(1)}, u32[]{:S(2)}, u32[]{:S(2)}) %collective-permute-start.22) | collective-permute-done | bytes 286752 | tf_op jit(solution)/shard_map/ppermute | solution.py:1272
  127.8 2.1 %collective-permute-start.23 = (bf16[1792,128]{1,0:T(8,128)(2,1)S(1)}, bf16[1792,128]{1,0:T(8,128)(2,1)S(1)}, u32[]{:S(2)}, u32[]{:S(2)}) collective-permute-start(bf16[1792,128]{1,0:T(8,128)(2,1)S(1)} %get-tuple-element.157.refs_0_), channel_id=1, source_target_pairs={{0,2},{1,17},{2,0},{3,19},{4,6},{5,21},{6,4},{7,23},{8,10},{9,25},... | collective-permute-start | bytes 1376264 | tf_op jit(solution)/shard_map/ppermute | solution.py:1272
  130.0 2.9 %widen_trunk.6 = (f32[2,9,512,512]{3,2,1,0:T(8,128)}, f32[8,128]{1,0:T(8,128)S(1)}) custom-call(bf16[4608,128]{1,0:T(8,128)(2,1)S(1)} %get-tuple-element.158.refs_0_, bf16[4608,128]{1,0:T(8,128)(2,1)S(1)} %collective-permute-done.25.refs_1_, f32[8,128]{1,0:T(8,128)S(1)} %get-tuple-element.159.refs_2_), custom_call_target="tpu_custom_call" | custom-call | flops 290000000 | bytes 1024 | tf_op jit(solution)/shard_map/widen_trunk/pallas_call | solution.py:83
  132.9 2.9 %widen_trunk.7 = (f32[2,9,512,512]{3,2,1,0:T(8,128)}, f32[8,128]{1,0:T(8,128)S(1)}) custom-call(bf16[4608,128]{1,0:T(8,128)(2,1)S(1)} %get-tuple-element.155.refs_0_, bf16[4608,128]{1,0:T(8,128)(2,1)S(1)} %collective-permute-done.24.refs_1_, f32[2,9,512,512]{3,2,1,0:T(8,128)} %get-tuple-element.160.refs_2_, ...), custom_call_target="tpu_custom_call", output_to_operand_aliasing={{0}: (2, {})} | custom-call | flops 290000000 | bytes 1024 | tf_op jit(solution)/shard_map/widen_trunk/pallas_call | solution.py:83
  136.5 0.8 collective-permute-done.27.refs_0_
  137.4 1.7 %collective-permute-start.30 = (bf16[3584,128]{1,0:T(8,128)(2,1)S(1)}, bf16[3584,128]{1,0:T(8,128)(2,1)S(1)}, u32[]{:S(2)}, u32[]{:S(2)}) collective-permute-start(bf16[3584,128]{1,0:T(8,128)(2,1)S(1)} %get-tuple-element.163.refs_0_), channel_id=1, source_target_pairs={{0,16},{1,5},{2,18},{3,7},{4,20},{5,1},{6,22},{7,3},{8,24},{9,13},... | collective-permute-start | bytes 2752520 | tf_op jit(solution)/shard_map/ppermute | solution.py:1272
  139.1 1.8 %widen_trunk.8 = (f32[2,9,512,512]{3,2,1,0:T(8,128)}, f32[8,128]{1,0:T(8,128)S(1)}) custom-call(bf16[4608,128]{1,0:T(8,128)(2,1)S(1)} %get-tuple-element.165.refs_0_, f32[2,9,512,512]{3,2,1,0:T(8,128)} %get-tuple-element.166.refs_1_, f32[8,128]{1,0:T(8,128)S(1)} %get-tuple-element.167.refs_2_), custom_call_target="tpu_custom_call", output_to_operand_aliasing={{0}: (1, {})} | custom-call | flops 290000000 | bytes 1024 | tf_op jit(solution)/shard_map/widen_trunk/pallas_call | solution.py:83
  140.9 4.4 %widen_heads.3 = (f32[2,512,1792]{2,1,0:T(8,128)}, f32[8,128]{1,0:T(8,128)S(1)}) custom-call(bf16[3584,128]{1,0:T(8,128)(2,1)S(1)} %get-tuple-element.163.refs_0_, bf16[3584,128]{1,0:T(8,128)(2,1)S(1)} %collective-permute-done.26.refs_1_, f32[8,128]{1,0:T(8,128)S(1)} %get-tuple-element.168.refs_2_), custom_call_target="tpu_custom_call" | custom-call | flops 440000000 | bytes 1024 | tf_op jit(solution)/shard_map/widen_heads/pallas_call | solution.py:83
  145.3 3.7 %collective-permute-done.21.refs_0_ = bf16[4608,128]{1,0:T(8,128)(2,1)S(1)} collective-permute-done((bf16[4608,128]{1,0:T(8,128)(2,1)S(1)}, bf16[4608,128]{1,0:T(8,128)(2,1)S(1)}, u32[]{:S(2)}, u32[]{:S(2)}) %collective-permute-start.21) | collective-permute-done | bytes 1179680 | tf_op jit(solution)/shard_map/ppermute | solution.py:1272
  149.6 1.8 %widen_trunk.9 = (f32[2,9,512,512]{3,2,1,0:T(8,128)}, f32[8,128]{1,0:T(8,128)S(1)}) custom-call(bf16[4608,128]{1,0:T(8,128)(2,1)S(1)} %collective-permute-done.28.refs_0_, f32[2,9,512,512]{3,2,1,0:T(8,128)} %get-tuple-element.171.refs_1_, f32[8,128]{1,0:T(8,128)S(1)} %get-tuple-element.172.refs_2_), custom_call_target="tpu_custom_call", output_to_operand_aliasing={{0}: (1, {})} | custom-call | flops 290000000 | bytes 1024 | tf_op jit(solution)/shard_map/widen_trunk/pallas_call | solution.py:83
  151.3 1.8 %widen_trunk.10 = (f32[2,9,512,512]{3,2,1,0:T(8,128)}, f32[8,128]{1,0:T(8,128)S(1)}) custom-call(bf16[4608,128]{1,0:T(8,128)(2,1)S(1)} %get-tuple-element.170.refs_0_, f32[2,9,512,512]{3,2,1,0:T(8,128)} %get-tuple-element.173.refs_1_, f32[8,128]{1,0:T(8,128)S(1)} %get-tuple-element.174.refs_2_), custom_call_target="tpu_custom_call", output_to_operand_aliasing={{0}: (1, {})} | custom-call | flops 290000000 | bytes 1024 | tf_op jit(solution)/shard_map/widen_trunk/pallas_call | solution.py:83
  153.2 1.6 finish.1
  154.8 2.1 %collective-permute-start.31 = (bf16[3584,128]{1,0:T(8,128)(2,1)S(1)}, bf16[3584,128]{1,0:T(8,128)(2,1)S(1)}, u32[]{:S(2)}, u32[]{:S(2)}) collective-permute-start(bf16[3584,128]{1,0:T(8,128)(2,1)S(1)} %get-tuple-element.182.refs_0_), channel_id=1, source_target_pairs={{0,1},{1,0},{2,3},{3,2},{4,5},{5,4},{6,7},{7,6},{8,9},{9,8},{10,11... | collective-permute-start | bytes 2752520 | tf_op jit(solution)/shard_map/ppermute | solution.py:1275
  156.9 1.8 %widen_trunk.11 = (f32[2,9,512,512]{3,2,1,0:T(8,128)}, f32[8,128]{1,0:T(8,128)S(1)}) custom-call(bf16[4608,128]{1,0:T(8,128)(2,1)S(1)} %collective-permute-done.29.refs_0_, f32[2,9,512,512]{3,2,1,0:T(8,128)} %get-tuple-element.178.refs_1_, f32[8,128]{1,0:T(8,128)S(1)} %get-tuple-element.180.refs_2_), custom_call_target="tpu_custom_call", output_to_operand_aliasing={{0}: (1, {})} | custom-call | flops 290000000 | bytes 1024 | tf_op jit(solution)/shard_map/widen_trunk/pallas_call | solution.py:83
  158.7 2.5 %widen_heads.4 = (f32[2,512,1792]{2,1,0:T(8,128)}, f32[8,128]{1,0:T(8,128)S(1)}) custom-call(bf16[3584,128]{1,0:T(8,128)(2,1)S(1)} %get-tuple-element.182.refs_0_, f32[2,512,1792]{2,1,0:T(8,128)} %get-tuple-element.183.refs_1_, f32[8,128]{1,0:T(8,128)S(1)} %get-tuple-element.184.refs_2_), custom_call_target="tpu_custom_call", output_to_operand_aliasing={{0}: (1, {})} | custom-call | flops 440000000 | bytes 1024 | tf_op jit(solution)/shard_map/widen_heads/pallas_call | solution.py:83
  161.3 3.1 %widen_heads.5 = (f32[2,512,1792]{2,1,0:T(8,128)}, f32[8,128]{1,0:T(8,128)}) custom-call(bf16[3584,128]{1,0:T(8,128)(2,1)S(1)} %collective-permute-done.31.refs_0_, f32[2,512,1792]{2,1,0:T(8,128)} %get-tuple-element.185.refs_1_, f32[8,128]{1,0:T(8,128)S(1)} %get-tuple-element.186.refs_2_), custom_call_target="tpu_custom_call", output_to_operand_aliasing={{0}: (1, {})} | custom-call | flops 440000000 | bytes 1024 | tf_op jit(solution)/shard_map/widen_heads/pallas_call | solution.py:83
  (73 shorter events, 8.2 us)
Async XLA Ops:
  12.5 8.6 %collective-permute-start = (bf16[2080,256]{1,0:T(8,128)(2,1)}, bf16[2080,256]{1,0:T(8,128)(2,1)S(1)}, u32[]{:S(2)}, u32[]{:S(2)}) collective-permute-start(bf16[2080,256]{1,0:T(8,128)(2,1)} %get-tuple-element.105), channel_id=1, source_target_pairs={{0,1},{1,0},{2,3},{3,2},{4,5},{5,4},{6,7},{7,6},{8,9},{9,8},{10,11... | collective-permute-start | bytes 3194888 | tf_op jit(solution)/shard_map/ppermute | solution.py:1275
  13.0 8.0 %collective-permute-start.2 = (bf16[672,256]{1,0:T(8,128)(2,1)}, bf16[672,256]{1,0:T(8,128)(2,1)S(1)}, u32[]{:S(2)}, u32[]{:S(2)}) collective-permute-start(bf16[672,256]{1,0:T(8,128)(2,1)} %get-tuple-element.107), channel_id=1, source_target_pairs={{0,16},{1,5},{2,18},{3,7},{4,20},{5,1},{6,22},{7,3},{8,24},{9,13},... | collective-permute-start | bytes 1032200 | tf_op jit(solution)/shard_map/ppermute | solution.py:1272
  20.2 2.0 %copy-start = (bf16[2080,256]{1,0:T(8,128)(2,1)S(1)}, bf16[2080,256]{1,0:T(8,128)(2,1)}, u32[]{:S(2)}) copy-start(bf16[2080,256]{1,0:T(8,128)(2,1)} %get-tuple-element.104.refs_0_.refs_6_) | copy-start | bytes 3194884
  20.2 1.9 %copy-start.2 = (bf16[672,256]{1,0:T(8,128)(2,1)S(1)}, bf16[672,256]{1,0:T(8,128)(2,1)}, u32[]{:S(2)}) copy-start(bf16[672,256]{1,0:T(8,128)(2,1)} %get-tuple-element.101.refs_2_.refs_0_) | copy-start | bytes 1032196
  20.2 1.9 %collective-permute-start.1 = (bf16[672,256]{1,0:T(8,128)(2,1)}, bf16[672,256]{1,0:T(8,128)(2,1)S(1)}, u32[]{:S(2)}, u32[]{:S(2)}) collective-permute-start(bf16[672,256]{1,0:T(8,128)(2,1)} %get-tuple-element.101.refs_2_.refs_0_), channel_id=1, source_target_pairs={{0,1},{1,0},{2,3},{3,2},{4,5},{5,4},{6,7},{7,6},{8,9},{9,8},{10,11... | collective-permute-start | bytes 1032200 | tf_op jit(solution)/shard_map/ppermute | solution.py:1275
  21.0 0.7 copy-start.9
  22.2 4.3 %copy-start.3 = (bf16[2,336,512]{2,1,0:T(8,128)(2,1)S(1)}, bf16[2,336,512]{2,1,0:T(8,128)(2,1)}, u32[]{:S(2)}) copy-start(bf16[2,336,512]{2,1,0:T(8,128)(2,1)} %refs_1_.3) | copy-start | bytes 2064388
  22.2 4.3 %copy-start.4 = (bf16[2,144,512]{2,1,0:T(8,128)(2,1)S(1)}, bf16[2,144,512]{2,1,0:T(8,128)(2,1)}, u32[]{:S(2)}) copy-start(bf16[2,144,512]{2,1,0:T(8,128)(2,1)} %get-tuple-element.102.refs_3_) | copy-start | bytes 884740
  22.2 4.3 %copy-start.5 = (f32[2,3,1792]{2,0,1:T(2,128)S(1)}, f32[2,3,1792]{2,0,1:T(2,128)}, u32[]{:S(2)}) copy-start(f32[2,3,1792]{2,0,1:T(2,128)} %param.16) | copy-start | bytes 129028
  22.2 4.3 %copy-start.6 = (f32[8,512]{1,0:T(8,128)S(1)}, f32[8,512]{1,0:T(8,128)}, u32[]{:S(2)}) copy-start(f32[8,512]{1,0:T(8,128)} %get-tuple-element.103.refs_5_) | copy-start | bytes 49156
  22.2 4.3 %copy-start.7 = (f32[2,512]{1,0:T(2,128)S(1)}, f32[2,512]{1,0:T(2,128)}, u32[]{:S(2)}) copy-start(f32[2,512]{1,0:T(2,128)} %refs_4_.3) | copy-start | bytes 12292
  22.2 4.3 %copy-start.8 = (s32[1,2]{1,0:T(1,128)S(1)}, s32[1,2]{1,0:T(1,128)}, u32[]{:S(2)}) copy-start(s32[1,2]{1,0:T(1,128)} %refs_0_.5) | copy-start | bytes 28
  23.2 16.9 %collective-permute-start.4 = (bf16[1344,256]{1,0:T(8,128)(2,1)S(1)}, bf16[1344,256]{1,0:T(8,128)(2,1)S(1)}, u32[]{:S(2)}, u32[]{:S(2)}) collective-permute-start(bf16[1344,256]{1,0:T(8,128)(2,1)S(1)} %get-tuple-element.114), channel_id=1, source_target_pairs={{0,2},{1,5},{2,0},{3,7},{4,6},{5,1},{6,4},{7,3},{8,10},{9,13},{10,... | collective-permute-start | bytes 2064392 | tf_op jit(solution)/shard_map/ppermute | solution.py:1272
  25.0 10.3 %collective-permute-start.5 = (bf16[672,256]{1,0:T(8,128)(2,1)S(1)}, bf16[672,256]{1,0:T(8,128)(2,1)S(1)}, u32[]{:S(2)}, u32[]{:S(2)}) collective-permute-start(bf16[672,256]{1,0:T(8,128)(2,1)S(1)} %get-tuple-element.115), channel_id=1, source_target_pairs={{0,16},{1,5},{2,18},{3,7},{4,20},{5,1},{6,22},{7,3},{8,24},{9,13},... | collective-permute-start | bytes 1032200 | tf_op jit(solution)/shard_map/ppermute | solution.py:1272
  26.5 2.0 %copy-start.1 = (bf16[2,512,1792]{2,1,0:T(8,128)(2,1)S(1)}, bf16[2,512,1792]{2,1,0:T(8,128)(2,1)}, u32[]{:S(2)}) copy-start(bf16[2,512,1792]{2,1,0:T(8,128)(2,1)} %refs_2_.1) | copy-start | bytes 11010052
  34.7 28.9 %collective-permute-start.3 = (bf16[3808,128]{1,0:T(8,128)(2,1)S(1)}, bf16[3808,128]{1,0:T(8,128)(2,1)S(1)}, u32[]{:S(2)}, u32[]{:S(2)}) collective-permute-start(bf16[3808,128]{1,0:T(8,128)(2,1)S(1)} %get-tuple-element.113), channel_id=1, source_target_pairs={{0,16},{1,5},{2,18},{3,7},{4,20},{5,1},{6,22},{7,3},{8,24},{9,13},... | collective-permute-start | bytes 2924552 | tf_op jit(solution)/shard_map/ppermute | solution.py:1272
  39.7 10.5 %collective-permute-start.7 = (bf16[2304,128]{1,0:T(8,128)(2,1)S(1)}, bf16[2304,128]{1,0:T(8,128)(2,1)S(1)}, u32[]{:S(2)}, u32[]{:S(2)}) collective-permute-start(bf16[2304,128]{1,0:T(8,128)(2,1)S(1)} %get-tuple-element.121), channel_id=1, source_target_pairs={{0,2},{1,17},{2,0},{3,19},{4,6},{5,21},{6,4},{7,23},{8,10},{9,25},... | collective-permute-start | bytes 1769480 | tf_op jit(solution)/shard_map/ppermute | solution.py:1272
  43.8 17.9 %collective-permute-start.6 = (bf16[2304,128]{1,0:T(8,128)(2,1)S(1)}, bf16[2304,128]{1,0:T(8,128)(2,1)S(1)}, u32[]{:S(2)}, u32[]{:S(2)}) collective-permute-start(bf16[2304,128]{1,0:T(8,128)(2,1)S(1)} %get-tuple-element.119), channel_id=1, source_target_pairs={{0,16},{1,3},{2,18},{3,1},{4,20},{5,7},{6,22},{7,5},{8,24},{9,11},... | collective-permute-start | bytes 1769480 | tf_op jit(solution)/shard_map/ppermute | solution.py:1272
  50.3 14.2 %collective-permute-start.10 = (bf16[1152,128]{1,0:T(8,128)(2,1)S(1)}, bf16[1152,128]{1,0:T(8,128)(2,1)S(1)}, u32[]{:S(2)}, u32[]{:S(2)}) collective-permute-start(bf16[1152,128]{1,0:T(8,128)(2,1)S(1)} %get-tuple-element.130), channel_id=1, source_target_pairs={{0,4},{1,3},{2,6},{3,1},{4,0},{5,7},{6,2},{7,5},{8,12},{9,11},{10,... | collective-permute-start | bytes 884744 | tf_op jit(solution)/shard_map/ppermute | solution.py:1272
  61.8 9.8 %collective-permute-start.9 = (bf16[1152,128]{1,0:T(8,128)(2,1)S(1)}, bf16[1152,128]{1,0:T(8,128)(2,1)S(1)}, u32[]{:S(2)}, u32[]{:S(2)}) collective-permute-start(bf16[1152,128]{1,0:T(8,128)(2,1)S(1)} %get-tuple-element.128), channel_id=1, source_target_pairs={{0,4},{1,17},{2,6},{3,19},{4,0},{5,21},{6,2},{7,23},{8,12},{9,25},... | collective-permute-start | bytes 884744 | tf_op jit(solution)/shard_map/ppermute | solution.py:1272
  63.9 10.6 %collective-permute-start.8 = (bf16[2016,128]{1,0:T(8,128)(2,1)S(1)}, bf16[2016,128]{1,0:T(8,128)(2,1)S(1)}, u32[]{:S(2)}, u32[]{:S(2)}) collective-permute-start(bf16[2016,128]{1,0:T(8,128)(2,1)S(1)} %get-tuple-element.126), channel_id=1, source_target_pairs={{0,2},{1,17},{2,0},{3,19},{4,6},{5,21},{6,4},{7,23},{8,10},{9,25},... | collective-permute-start | bytes 1548296 | tf_op jit(solution)/shard_map/ppermute | solution.py:1272
  64.6 22.4 %collective-permute-start.14 = (bf16[1152,128]{1,0:T(8,128)(2,1)S(1)}, bf16[1152,128]{1,0:T(8,128)(2,1)S(1)}, u32[]{:S(2)}, u32[]{:S(2)}) collective-permute-start(bf16[1152,128]{1,0:T(8,128)(2,1)S(1)} %get-tuple-element.140.refs_0_), channel_id=1, source_target_pairs={{0,8},{1,9},{2,10},{3,11},{4,12},{5,13},{6,14},{7,15},{8,0},{9,1},... | collective-permute-start | bytes 884744 | tf_op jit(solution)/shard_map/ppermute | solution.py:1272
  71.7 19.9 %collective-permute-start.13 = (bf16[1152,128]{1,0:T(8,128)(2,1)S(1)}, bf16[1152,128]{1,0:T(8,128)(2,1)S(1)}, u32[]{:S(2)}, u32[]{:S(2)}) collective-permute-start(bf16[1152,128]{1,0:T(8,128)(2,1)S(1)} %get-tuple-element.139.refs_0_), channel_id=1, source_target_pairs={{0,8},{1,9},{2,10},{3,11},{4,12},{5,13},{6,14},{7,15},{8,0},{9,1},... | collective-permute-start | bytes 884744 | tf_op jit(solution)/shard_map/ppermute | solution.py:1272
  87.1 10.7 %collective-permute-start.17 = (bf16[1152,128]{1,0:T(8,128)(2,1)S(1)}, bf16[1152,128]{1,0:T(8,128)(2,1)S(1)}, u32[]{:S(2)}, u32[]{:S(2)}) collective-permute-start(bf16[1152,128]{1,0:T(8,128)(2,1)S(1)} %get-tuple-element.146.refs_0_), channel_id=1, source_target_pairs={{0,4},{1,3},{2,6},{3,1},{4,0},{5,7},{6,2},{7,5},{8,12},{9,11},{10,... | collective-permute-start | bytes 884744 | tf_op jit(solution)/shard_map/ppermute | solution.py:1272
  87.2 10.6 %collective-permute-start.12 = (bf16[1120,128]{1,0:T(8,128)(2,1)S(1)}, bf16[1120,128]{1,0:T(8,128)(2,1)S(1)}, u32[]{:S(2)}, u32[]{:S(2)}) collective-permute-start(bf16[1120,128]{1,0:T(8,128)(2,1)S(1)} %get-tuple-element.138), channel_id=1, source_target_pairs={{0,4},{1,3},{2,6},{3,1},{4,0},{5,7},{6,2},{7,5},{8,12},{9,11},{10,... | collective-permute-start | bytes 860168 | tf_op jit(solution)/shard_map/ppermute | solution.py:1272
  91.6 9.2 %collective-permute-start.16 = (bf16[1152,128]{1,0:T(8,128)(2,1)S(1)}, bf16[1152,128]{1,0:T(8,128)(2,1)S(1)}, u32[]{:S(2)}, u32[]{:S(2)}) collective-permute-start(bf16[1152,128]{1,0:T(8,128)(2,1)S(1)} %get-tuple-element.145.refs_0_), channel_id=1, source_target_pairs={{0,4},{1,17},{2,6},{3,19},{4,0},{5,21},{6,2},{7,23},{8,12},{9,25},... | collective-permute-start | bytes 884744 | tf_op jit(solution)/shard_map/ppermute | solution.py:1272
  97.9 17.6 %collective-permute-start.20 = (bf16[2304,128]{1,0:T(8,128)(2,1)S(1)}, bf16[2304,128]{1,0:T(8,128)(2,1)S(1)}, u32[]{:S(2)}, u32[]{:S(2)}) collective-permute-start(bf16[2304,128]{1,0:T(8,128)(2,1)S(1)} %get-tuple-element.152.refs_0_), channel_id=1, source_target_pairs={{0,2},{1,17},{2,0},{3,19},{4,6},{5,21},{6,4},{7,23},{8,10},{9,25},... | collective-permute-start | bytes 1769480 | tf_op jit(solution)/shard_map/ppermute | solution.py:1272
  100.9 14.7 %collective-permute-start.19 = (bf16[2304,128]{1,0:T(8,128)(2,1)S(1)}, bf16[2304,128]{1,0:T(8,128)(2,1)S(1)}, u32[]{:S(2)}, u32[]{:S(2)}) collective-permute-start(bf16[2304,128]{1,0:T(8,128)(2,1)S(1)} %get-tuple-element.151.refs_0_), channel_id=1, source_target_pairs={{0,16},{1,3},{2,18},{3,1},{4,20},{5,7},{6,22},{7,5},{8,24},{9,11},... | collective-permute-start | bytes 1769480 | tf_op jit(solution)/shard_map/ppermute | solution.py:1272
  102.6 11.9 %collective-permute-start.15 = (bf16[1120,128]{1,0:T(8,128)(2,1)S(1)}, bf16[1120,128]{1,0:T(8,128)(2,1)S(1)}, u32[]{:S(2)}, u32[]{:S(2)}) collective-permute-start(bf16[1120,128]{1,0:T(8,128)(2,1)S(1)} %get-tuple-element.144.refs_0_), channel_id=1, source_target_pairs={{0,8},{1,9},{2,10},{3,11},{4,12},{5,13},{6,14},{7,15},{8,0},{9,1},... | collective-permute-start | bytes 860168 | tf_op jit(solution)/shard_map/ppermute | solution.py:1272
  103.8 11.6 %collective-permute-start.11 = (bf16[1120,128]{1,0:T(8,128)(2,1)S(1)}, bf16[1120,128]{1,0:T(8,128)(2,1)S(1)}, u32[]{:S(2)}, u32[]{:S(2)}) collective-permute-start(bf16[1120,128]{1,0:T(8,128)(2,1)S(1)} %get-tuple-element.136), channel_id=1, source_target_pairs={{0,16},{16,0},{1,17},{17,1},{2,18},{18,2},{3,19},{19,3},{4,20},{20... | collective-permute-start | bytes 860168 | tf_op jit(solution)/shard_map/ppermute | solution.py:1345
  115.5 14.5 %collective-permute-start.25 = (bf16[4608,128]{1,0:T(8,128)(2,1)S(1)}, bf16[4608,128]{1,0:T(8,128)(2,1)S(1)}, u32[]{:S(2)}, u32[]{:S(2)}) collective-permute-start(bf16[4608,128]{1,0:T(8,128)(2,1)S(1)} %get-tuple-element.158.refs_0_), channel_id=1, source_target_pairs={{0,1},{1,0},{2,3},{3,2},{4,5},{5,4},{6,7},{7,6},{8,9},{9,8},{10,11... | collective-permute-start | bytes 3538952 | tf_op jit(solution)/shard_map/ppermute | solution.py:1275
  115.7 17.2 %collective-permute-start.24 = (bf16[4608,128]{1,0:T(8,128)(2,1)S(1)}, bf16[4608,128]{1,0:T(8,128)(2,1)S(1)}, u32[]{:S(2)}, u32[]{:S(2)}) collective-permute-start(bf16[4608,128]{1,0:T(8,128)(2,1)S(1)} %get-tuple-element.155.refs_0_), channel_id=1, source_target_pairs={{0,1},{1,0},{2,3},{3,2},{4,5},{5,4},{6,7},{7,6},{8,9},{9,8},{10,11... | collective-permute-start | bytes 3538952 | tf_op jit(solution)/shard_map/ppermute | solution.py:1275
  116.3 21.1 %collective-permute-start.27 = (bf16[4608,128]{1,0:T(8,128)(2,1)S(1)}, bf16[4608,128]{1,0:T(8,128)(2,1)S(1)}, u32[]{:S(2)}, u32[]{:S(2)}) collective-permute-start(bf16[4608,128]{1,0:T(8,128)(2,1)S(1)} %get-tuple-element.158.refs_0_), channel_id=1, source_target_pairs={{0,16},{1,5},{2,18},{3,7},{4,20},{5,1},{6,22},{7,3},{8,24},{9,13},... | collective-permute-start | bytes 3538952 | tf_op jit(solution)/shard_map/ppermute | solution.py:1272
  118.0 9.8 %collective-permute-start.22 = (bf16[1120,128]{1,0:T(8,128)(2,1)S(1)}, bf16[1120,128]{1,0:T(8,128)(2,1)S(1)}, u32[]{:S(2)}, u32[]{:S(2)}) collective-permute-start(bf16[1120,128]{1,0:T(8,128)(2,1)S(1)} %get-tuple-element.150.refs_0_.refs_4_), channel_id=1, source_target_pairs={{0,4},{1,3},{2,6},{3,1},{4,0},{5,7},{6,2},{7,5},{8,12},{9,11},{10,... | collective-permute-start | bytes 860168 | tf_op jit(solution)/shard_map/ppermute | solution.py:1272
  127.8 8.6 %collective-permute-start.23 = (bf16[1792,128]{1,0:T(8,128)(2,1)S(1)}, bf16[1792,128]{1,0:T(8,128)(2,1)S(1)}, u32[]{:S(2)}, u32[]{:S(2)}) collective-permute-start(bf16[1792,128]{1,0:T(8,128)(2,1)S(1)} %get-tuple-element.157.refs_0_), channel_id=1, source_target_pairs={{0,2},{1,17},{2,0},{3,19},{4,6},{5,21},{6,4},{7,23},{8,10},{9,25},... | collective-permute-start | bytes 1376264 | tf_op jit(solution)/shard_map/ppermute | solution.py:1272
  129.9 19.1 %collective-permute-start.21 = (bf16[4608,128]{1,0:T(8,128)(2,1)S(1)}, bf16[4608,128]{1,0:T(8,128)(2,1)S(1)}, u32[]{:S(2)}, u32[]{:S(2)}) collective-permute-start(bf16[4608,128]{1,0:T(8,128)(2,1)S(1)} %get-tuple-element.155.refs_0_), channel_id=1, source_target_pairs={{0,2},{1,5},{2,0},{3,7},{4,6},{5,1},{6,4},{7,3},{8,10},{9,13},{10,... | collective-permute-start | bytes 3538952 | tf_op jit(solution)/shard_map/ppermute | solution.py:1272
  136.5 4.4 %collective-permute-start.26 = (bf16[3584,128]{1,0:T(8,128)(2,1)S(1)}, bf16[3584,128]{1,0:T(8,128)(2,1)S(1)}, u32[]{:S(2)}, u32[]{:S(2)}) collective-permute-start(bf16[3584,128]{1,0:T(8,128)(2,1)S(1)} %get-tuple-element.163.refs_0_), channel_id=1, source_target_pairs={{0,1},{1,0},{2,3},{3,2},{4,5},{5,4},{6,7},{7,6},{8,9},{9,8},{10,11... | collective-permute-start | bytes 2752520 | tf_op jit(solution)/shard_map/ppermute | solution.py:1275
  137.4 12.2 %collective-permute-start.28 = (bf16[4608,128]{1,0:T(8,128)(2,1)S(1)}, bf16[4608,128]{1,0:T(8,128)(2,1)S(1)}, u32[]{:S(2)}, u32[]{:S(2)}) collective-permute-start(bf16[4608,128]{1,0:T(8,128)(2,1)S(1)} %get-tuple-element.165.refs_0_), channel_id=1, source_target_pairs={{0,1},{1,0},{2,3},{3,2},{4,5},{5,4},{6,7},{7,6},{8,9},{9,8},{10,11... | collective-permute-start | bytes 3538952 | tf_op jit(solution)/shard_map/ppermute | solution.py:1275
  137.4 17.4 %collective-permute-start.30 = (bf16[3584,128]{1,0:T(8,128)(2,1)S(1)}, bf16[3584,128]{1,0:T(8,128)(2,1)S(1)}, u32[]{:S(2)}, u32[]{:S(2)}) collective-permute-start(bf16[3584,128]{1,0:T(8,128)(2,1)S(1)} %get-tuple-element.163.refs_0_), channel_id=1, source_target_pairs={{0,16},{1,5},{2,18},{3,7},{4,20},{5,1},{6,22},{7,3},{8,24},{9,13},... | collective-permute-start | bytes 2752520 | tf_op jit(solution)/shard_map/ppermute | solution.py:1272
  149.0 7.9 %collective-permute-start.29 = (bf16[4608,128]{1,0:T(8,128)(2,1)S(1)}, bf16[4608,128]{1,0:T(8,128)(2,1)S(1)}, u32[]{:S(2)}, u32[]{:S(2)}) collective-permute-start(bf16[4608,128]{1,0:T(8,128)(2,1)S(1)} %get-tuple-element.170.refs_0_), channel_id=1, source_target_pairs={{0,1},{1,0},{2,3},{3,2},{4,5},{5,4},{6,7},{7,6},{8,9},{9,8},{10,11... | collective-permute-start | bytes 3538952 | tf_op jit(solution)/shard_map/ppermute | solution.py:1275
  149.0 4.1 %collective-permute-start.18 = (bf16[1120,128]{1,0:T(8,128)(2,1)S(1)}, bf16[1120,128]{1,0:T(8,128)(2,1)S(1)}, u32[]{:S(2)}, u32[]{:S(2)}) collective-permute-start(bf16[1120,128]{1,0:T(8,128)(2,1)S(1)} %get-tuple-element.150.refs_0_.refs_4_), channel_id=1, source_target_pairs={{0,1},{1,0},{2,3},{3,2},{4,5},{5,4},{6,7},{7,6},{8,9},{9,8},{10,11... | collective-permute-start | bytes 860168 | tf_op jit(solution)/shard_map/ppermute | solution.py:1275
  154.8 6.4 %collective-permute-start.31 = (bf16[3584,128]{1,0:T(8,128)(2,1)S(1)}, bf16[3584,128]{1,0:T(8,128)(2,1)S(1)}, u32[]{:S(2)}, u32[]{:S(2)}) collective-permute-start(bf16[3584,128]{1,0:T(8,128)(2,1)S(1)} %get-tuple-element.182.refs_0_), channel_id=1, source_target_pairs={{0,1},{1,0},{2,3},{3,2},{4,5},{5,4},{6,7},{7,6},{8,9},{9,8},{10,11... | collective-permute-start | bytes 2752520 | tf_op jit(solution)/shard_map/ppermute | solution.py:1275

commit v5 on v4

--- a/solution.py
+++ b/solution.py
@@ -1207,8 +1207,7 @@
     "finish",
     "Hnew",
     "Enew_other",
-    "Hnew_own",
-    "Hnew_other",
+    "Hnew_wide",
 )
 WAITS = {"far": ("near",), "L6": ("feed",)}
 

time: 165 us -> 164 us (level)
    pallas_call x37 -> x36, Pallas kernels: 61.8 us -> 61 us  [call(): pl.pallas_call(run, out_shape=(*shapes, jax.ShapeDtypeStruct((8, 128), F3...]
  transfers between devices with their start and end apart: 32 -> 32, of which waited for: 15 -> 17; matrix products, arithmetic and copies ran while one was open for 0% -> 0% of each run, Pallas kernels for 28% -> 26%
where the time goes in v5:
time: 164 us
  waiting for transfers between devices  61.7 us (38%)
  Pallas kernels  61 us (37%)
  starting transfers between devices  37.5 us (23%)
  local copies, waits for them, and re-layouts  2.76 us (2%)
    pallas_call x36, Pallas kernels, call(): pl.pallas_call(run, out_shape=(*shapes, jax.ShapeDtypeStruct((8, 128), F3...  61 us
    ppermute x22, waiting for transfers between devices, swap(): return lax.ppermute(block, AXES, route)  60.1 us
    ppermute x22, starting transfers between devices, swap(): return lax.ppermute(block, AXES, route)  32.2 us
    ppermute x9, starting transfers between devices, swap_cores(): return lax.ppermute(block, AXES, [(i, i ^ 1) for i in range(devices)])  4.52 us
  transfers between devices with their start and end apart: 32, of which 17 were waited for; matrix products, arithmetic and copies ran while one was open for 0% of the time, Pallas kernels for 26%

profile of v5, /device:TPU:0, one launch (start us, length us, event | category | flops | bytes accessed | tf_op | source)
XLA Modules:
  0.0 164.1 jit_solution(2404901237625981680)
XLA Ops:
  0.6 11.8 %section.1 = (bf16[2080,256]{1,0:T(8,128)(2,1)}, bf16[2080,256]{1,0:T(8,128)(2,1)}, bf16[672,256]{1,0:T(8,128)(2,1)}, bf16[672,256]{1,0:T(8,128)(2,1)}, f32[336,...) custom-call(s32[1,2]{1,0:T(1,128)} %refs_0_.5, bf16[2,336,512]{2,1,0:T(8,128)(2,1)} %refs_1_.3, ...), custom_call_target="tpu_custom_call" | custom-call | flops 1150000000 | bytes 1024 | tf_op jit(solution)/shard_map/section/pallas_call | solution.py:83
  13.0 2.6 %collective-permute-start.2 = (bf16[672,256]{1,0:T(8,128)(2,1)}, bf16[672,256]{1,0:T(8,128)(2,1)S(1)}, u32[]{:S(2)}, u32[]{:S(2)}) collective-permute-start(bf16[672,256]{1,0:T(8,128)(2,1)} %get-tuple-element.105), channel_id=1, source_target_pairs={{0,16},{1,5},{2,18},{3,7},{4,20},{5,1},{6,22},{7,3},{8,24},{9,13},... | collective-permute-start | bytes 1032200 | tf_op jit(solution)/shard_map/ppermute | solution.py:1271
  15.6 4.6 %back.2 = (bf16[672,256]{1,0:T(8,128)(2,1)}, f32[8,128]{1,0:T(8,128)}) custom-call(bf16[672,256]{1,0:T(8,128)(2,1)} %get-tuple-element.96.refs_0_, bf16[2,4608,512]{2,1,0:T(8,128)(2,1)} %bitcast.8, f32[336,512]{1,0:T(8,128)} %get-tuple-element.97.refs_2_, f32[8,128]{1,0:T(8,128)} %get-tuple-element.98.refs_3_), custom_call_target="tpu_custom_call" | custom-call | flops 350000000 | bytes 1024 | tf_op jit(solution)/shard_map/back/pallas_call | solution.py:83
  21.0 0.7 copy-done.9
  22.2 0.9 first_factors.1
  23.2 1.8 %collective-permute-start.4 = (bf16[1344,256]{1,0:T(8,128)(2,1)S(1)}, bf16[1344,256]{1,0:T(8,128)(2,1)S(1)}, u32[]{:S(2)}, u32[]{:S(2)}) collective-permute-start(bf16[1344,256]{1,0:T(8,128)(2,1)S(1)} %get-tuple-element.112), channel_id=1, source_target_pairs={{0,2},{1,5},{2,0},{3,7},{4,6},{5,1},{6,4},{7,3},{8,10},{9,13},{10,... | collective-permute-start | bytes 2064392 | tf_op jit(solution)/shard_map/ppermute | solution.py:1271
  25.0 1.5 collective-permute-start.5
  26.5 2.0 %copy-done.1 = bf16[2,512,1792]{2,1,0:T(8,128)(2,1)S(1)} copy-done((bf16[2,512,1792]{2,1,0:T(8,128)(2,1)S(1)}, bf16[2,512,1792]{2,1,0:T(8,128)(2,1)}, u32[]{:S(2)}) %copy-start.1) | copy-done | bytes 3670040
  28.6 6.2 %head_grads.1 = (bf16[3808,128]{1,0:T(8,128)(2,1)S(1)}, bf16[3808,128]{1,0:T(8,128)(2,1)S(1)}, bf16[64,1792]{1,0:T(8,128)(2,1)S(1)}, f32[336,512]{1,0:T(8,128)S(1)}, f32[8,128]{1,0:T(8,128)S(1)}) custom-call(s32[1,2]{1,0:T(1,128)S(1)} %copy-done.8, bf16[2,336,512]{2,1,0:T(8,128)(2,1)S(1)} %copy-done.3, bf16[2,512,1792]{2,1,0:T(8,128)(2,1)S(1)} %copy-done.1, ...), custom_call_target="tpu_custom_call" | custom-call | flops 610000000 | bytes 1024 | tf_op jit(solution)/shard_map/head_grads/pallas_call | solution.py:83
  35.3 4.4 %late_grads.1 = (bf16[2304,128]{1,0:T(8,128)(2,1)S(1)}, bf16[2304,128]{1,0:T(8,128)(2,1)S(1)}, f32[8,128]{1,0:T(8,128)S(1)}) custom-call(bf16[2080,256]{1,0:T(8,128)(2,1)S(1)} %copy-done, bf16[2080,256]{1,0:T(8,128)(2,1)S(1)} %collective-permute-done.refs_0_.refs_1_.refs_7_, bf16[672,256]{1,0:T(8,128)(2,1)S(1)} %collective-permute-done.2.refs_2_, ...), custom_call_target="tpu_custom_call" | custom-call | flops 430000000 | bytes 1024 | tf_op jit(solution)/shard_map/late_grads/pallas_call | solution.py:83
  40.0 3.7 %early_grads.1 = (bf16[2304,128]{1,0:T(8,128)(2,1)S(1)}, bf16[2304,128]{1,0:T(8,128)(2,1)S(1)}, f32[8,128]{1,0:T(8,128)S(1)}) custom-call(bf16[2080,256]{1,0:T(8,128)(2,1)S(1)} %copy-done, bf16[2080,256]{1,0:T(8,128)(2,1)S(1)} %collective-permute-done.refs_0_.refs_1_.refs_7_, bf16[672,256]{1,0:T(8,128)(2,1)S(1)} %copy-done.2, ...), custom_call_target="tpu_custom_call" | custom-call | flops 370000000 | bytes 1024 | tf_op jit(solution)/shard_map/early_grads/pallas_call | solution.py:83
  43.8 1.8 %collective-permute-start.6 = (bf16[2304,128]{1,0:T(8,128)(2,1)S(1)}, bf16[2304,128]{1,0:T(8,128)(2,1)S(1)}, u32[]{:S(2)}, u32[]{:S(2)}) collective-permute-start(bf16[2304,128]{1,0:T(8,128)(2,1)S(1)} %get-tuple-element.117), channel_id=1, source_target_pairs={{0,16},{1,3},{2,18},{3,1},{4,20},{5,7},{6,22},{7,5},{8,24},{9,11},... | collective-permute-start | bytes 1769480 | tf_op jit(solution)/shard_map/ppermute | solution.py:1271
  45.6 4.6 %collective-permute-done.7.refs_1_ = bf16[2304,128]{1,0:T(8,128)(2,1)S(1)} collective-permute-done((bf16[2304,128]{1,0:T(8,128)(2,1)S(1)}, bf16[2304,128]{1,0:T(8,128)(2,1)S(1)}, u32[]{:S(2)}, u32[]{:S(2)}) %collective-permute-start.7) | collective-permute-done | bytes 589856 | tf_op jit(solution)/shard_map/ppermute | solution.py:1271
  50.3 2.0 %collective-permute-start.10 = (bf16[1152,128]{1,0:T(8,128)(2,1)S(1)}, bf16[1152,128]{1,0:T(8,128)(2,1)S(1)}, u32[]{:S(2)}, u32[]{:S(2)}) collective-permute-start(bf16[1152,128]{1,0:T(8,128)(2,1)S(1)} %get-tuple-element.128), channel_id=1, source_target_pairs={{0,4},{1,3},{2,6},{3,1},{4,0},{5,7},{6,2},{7,5},{8,12},{9,11},{10,... | collective-permute-start | bytes 884744 | tf_op jit(solution)/shard_map/ppermute | solution.py:1271
  52.4 9.4 %collective-permute-done.6.refs_1_ = bf16[2304,128]{1,0:T(8,128)(2,1)S(1)} collective-permute-done((bf16[2304,128]{1,0:T(8,128)(2,1)S(1)}, bf16[2304,128]{1,0:T(8,128)(2,1)S(1)}, u32[]{:S(2)}, u32[]{:S(2)}) %collective-permute-start.6) | collective-permute-done | bytes 589856 | tf_op jit(solution)/shard_map/ppermute | solution.py:1271
  61.9 1.8 %collective-permute-start.9 = (bf16[1152,128]{1,0:T(8,128)(2,1)S(1)}, bf16[1152,128]{1,0:T(8,128)(2,1)S(1)}, u32[]{:S(2)}, u32[]{:S(2)}) collective-permute-start(bf16[1152,128]{1,0:T(8,128)(2,1)S(1)} %get-tuple-element.126), channel_id=1, source_target_pairs={{0,4},{1,17},{2,6},{3,19},{4,0},{5,21},{6,2},{7,23},{8,12},{9,25},... | collective-permute-start | bytes 884744 | tf_op jit(solution)/shard_map/ppermute | solution.py:1271
  64.6 2.7 %collective-permute-start.14 = (bf16[1152,128]{1,0:T(8,128)(2,1)S(1)}, bf16[1152,128]{1,0:T(8,128)(2,1)S(1)}, u32[]{:S(2)}, u32[]{:S(2)}) collective-permute-start(bf16[1152,128]{1,0:T(8,128)(2,1)S(1)} %get-tuple-element.138.refs_0_), channel_id=1, source_target_pairs={{0,8},{1,9},{2,10},{3,11},{4,12},{5,13},{6,14},{7,15},{8,0},{9,1},... | collective-permute-start | bytes 884744 | tf_op jit(solution)/shard_map/ppermute | solution.py:1271
  67.2 4.6 %collective-permute-done.9.refs_1_ = bf16[1152,128]{1,0:T(8,128)(2,1)S(1)} collective-permute-done((bf16[1152,128]{1,0:T(8,128)(2,1)S(1)}, bf16[1152,128]{1,0:T(8,128)(2,1)S(1)}, u32[]{:S(2)}, u32[]{:S(2)}) %collective-permute-start.9) | collective-permute-done | bytes 294944 | tf_op jit(solution)/shard_map/ppermute | solution.py:1271
  71.9 2.5 %collective-permute-start.13 = (bf16[1152,128]{1,0:T(8,128)(2,1)S(1)}, bf16[1152,128]{1,0:T(8,128)(2,1)S(1)}, u32[]{:S(2)}, u32[]{:S(2)}) collective-permute-start(bf16[1152,128]{1,0:T(8,128)(2,1)S(1)} %get-tuple-element.137.refs_0_), channel_id=1, source_target_pairs={{0,8},{1,9},{2,10},{3,11},{4,12},{5,13},{6,14},{7,15},{8,0},{9,1},... | collective-permute-start | bytes 884744 | tf_op jit(solution)/shard_map/ppermute | solution.py:1271
  74.6 3.9 %back.3 = (f32[336,256]{1,0:T(8,128)S(1)}, bf16[1120,128]{1,0:T(8,128)(2,1)S(1)}, f32[8,128]{1,0:T(8,128)S(1)}) custom-call(bf16[672,256]{1,0:T(8,128)(2,1)S(1)} %copy-done.2, bf16[2,4608,512]{2,1,0:T(8,128)(2,1)} %bitcast.9, f32[336,512]{1,0:T(8,128)S(1)} %get-tuple-element.108.refs_2_, bf16[64,1792]{1,0:T(8,128)(2,1)S(1)} %get-tuple-element.109.refs_3_.refs_2_, ...), custom_call_target="tpu_custom_call" | custom-call | flops 350000000 | bytes 1024 | tf_op jit(solution)/shard_map/back/pallas_call | solution.py:83
  78.5 8.5 %collective-permute-done.14.refs_1_ = bf16[1152,128]{1,0:T(8,128)(2,1)S(1)} collective-permute-done((bf16[1152,128]{1,0:T(8,128)(2,1)S(1)}, bf16[1152,128]{1,0:T(8,128)(2,1)S(1)}, u32[]{:S(2)}, u32[]{:S(2)}) %collective-permute-start.14) | collective-permute-done | bytes 294944 | tf_op jit(solution)/shard_map/ppermute | solution.py:1271
  87.2 2.0 %collective-permute-start.12 = (bf16[1120,128]{1,0:T(8,128)(2,1)S(1)}, bf16[1120,128]{1,0:T(8,128)(2,1)S(1)}, u32[]{:S(2)}, u32[]{:S(2)}) collective-permute-start(bf16[1120,128]{1,0:T(8,128)(2,1)S(1)} %get-tuple-element.136), channel_id=1, source_target_pairs={{0,4},{1,3},{2,6},{3,1},{4,0},{5,7},{6,2},{7,5},{8,12},{9,11},{10,... | collective-permute-start | bytes 860168 | tf_op jit(solution)/shard_map/ppermute | solution.py:1271
  89.2 2.4 %collective-permute-done.13.refs_1_ = bf16[1152,128]{1,0:T(8,128)(2,1)S(1)} collective-permute-done((bf16[1152,128]{1,0:T(8,128)(2,1)S(1)}, bf16[1152,128]{1,0:T(8,128)(2,1)S(1)}, u32[]{:S(2)}, u32[]{:S(2)}) %collective-permute-start.13) | collective-permute-done | bytes 294944 | tf_op jit(solution)/shard_map/ppermute | solution.py:1271
  92.3 5.4 %collective-permute-done.12.refs_1_ = bf16[1120,128]{1,0:T(8,128)(2,1)S(1)} collective-permute-done((bf16[1120,128]{1,0:T(8,128)(2,1)S(1)}, bf16[1120,128]{1,0:T(8,128)(2,1)S(1)}, u32[]{:S(2)}, u32[]{:S(2)}) %collective-permute-start.12) | collective-permute-done | bytes 286752 | tf_op jit(solution)/shard_map/ppermute | solution.py:1271
  97.8 1.6 collective-permute-start.20
  99.5 1.4 collective-permute-done.16.refs_1_
  100.9 1.6 collective-permute-start.19
  102.5 1.3 collective-permute-start.15
  103.8 0.8 collective-permute-start.11
  104.6 9.9 %collective-permute-done.15.refs_1_ = bf16[1120,128]{1,0:T(8,128)(2,1)S(1)} collective-permute-done((bf16[1120,128]{1,0:T(8,128)(2,1)S(1)}, bf16[1120,128]{1,0:T(8,128)(2,1)S(1)}, u32[]{:S(2)}, u32[]{:S(2)}) %collective-permute-start.15) | collective-permute-done | bytes 286752 | tf_op jit(solution)/shard_map/ppermute | solution.py:1271
  114.5 0.9 collective-permute-done.11.refs_3_
  116.2 1.7 %collective-permute-start.27 = (bf16[4608,128]{1,0:T(8,128)(2,1)S(1)}, bf16[4608,128]{1,0:T(8,128)(2,1)S(1)}, u32[]{:S(2)}, u32[]{:S(2)}) collective-permute-start(bf16[4608,128]{1,0:T(8,128)(2,1)S(1)} %get-tuple-element.156.refs_0_), channel_id=1, source_target_pairs={{0,16},{1,5},{2,18},{3,7},{4,20},{5,1},{6,22},{7,3},{8,24},{9,13},... | collective-permute-start | bytes 3538952 | tf_op jit(solution)/shard_map/ppermute | solution.py:1271
  118.0 0.9 collective-permute-start.22
  118.9 8.8 %collective-permute-done.22.refs_1_ = bf16[1120,128]{1,0:T(8,128)(2,1)S(1)} collective-permute-done((bf16[1120,128]{1,0:T(8,128)(2,1)S(1)}, bf16[1120,128]{1,0:T(8,128)(2,1)S(1)}, u32[]{:S(2)}, u32[]{:S(2)}) %collective-permute-start.22) | collective-permute-done | bytes 286752 | tf_op jit(solution)/shard_map/ppermute | solution.py:1271
  127.8 2.1 %collective-permute-start.23 = (bf16[1792,128]{1,0:T(8,128)(2,1)S(1)}, bf16[1792,128]{1,0:T(8,128)(2,1)S(1)}, u32[]{:S(2)}, u32[]{:S(2)}) collective-permute-start(bf16[1792,128]{1,0:T(8,128)(2,1)S(1)} %get-tuple-element.155.refs_0_), channel_id=1, source_target_pairs={{0,2},{1,17},{2,0},{3,19},{4,6},{5,21},{6,4},{7,23},{8,10},{9,25},... | collective-permute-start | bytes 1376264 | tf_op jit(solution)/shard_map/ppermute | solution.py:1271
  130.0 2.9 %widen_trunk.6 = (f32[2,9,512,512]{3,2,1,0:T(8,128)}, f32[8,128]{1,0:T(8,128)S(1)}) custom-call(bf16[4608,128]{1,0:T(8,128)(2,1)S(1)} %get-tuple-element.156.refs_0_, bf16[4608,128]{1,0:T(8,128)(2,1)S(1)} %collective-permute-done.25.refs_1_, f32[8,128]{1,0:T(8,128)S(1)} %get-tuple-element.157.refs_2_), custom_call_target="tpu_custom_call" | custom-call | flops 290000000 | bytes 1024 | tf_op jit(solution)/shard_map/widen_trunk/pallas_call | solution.py:83
  132.9 2.9 %widen_trunk.7 = (f32[2,9,512,512]{3,2,1,0:T(8,128)}, f32[8,128]{1,0:T(8,128)S(1)}) custom-call(bf16[4608,128]{1,0:T(8,128)(2,1)S(1)} %get-tuple-element.153.refs_0_, bf16[4608,128]{1,0:T(8,128)(2,1)S(1)} %collective-permute-done.24.refs_1_, f32[2,9,512,512]{3,2,1,0:T(8,128)} %get-tuple-element.158.refs_2_, ...), custom_call_target="tpu_custom_call", output_to_operand_aliasing={{0}: (2, {})} | custom-call | flops 290000000 | bytes 1024 | tf_op jit(solution)/shard_map/widen_trunk/pallas_call | solution.py:83
  136.4 0.9 collective-permute-done.27.refs_0_
  137.9 1.7 %collective-permute-start.30 = (bf16[3584,128]{1,0:T(8,128)(2,1)S(1)}, bf16[3584,128]{1,0:T(8,128)(2,1)S(1)}, u32[]{:S(2)}, u32[]{:S(2)}) collective-permute-start(bf16[3584,128]{1,0:T(8,128)(2,1)S(1)} %get-tuple-element.161.refs_0_), channel_id=1, source_target_pairs={{0,16},{1,5},{2,18},{3,7},{4,20},{5,1},{6,22},{7,3},{8,24},{9,13},... | collective-permute-start | bytes 2752520 | tf_op jit(solution)/shard_map/ppermute | solution.py:1271
  139.6 1.8 %widen_trunk.8 = (f32[2,9,512,512]{3,2,1,0:T(8,128)}, f32[8,128]{1,0:T(8,128)S(1)}) custom-call(bf16[4608,128]{1,0:T(8,128)(2,1)S(1)} %get-tuple-element.163.refs_0_, f32[2,9,512,512]{3,2,1,0:T(8,128)} %get-tuple-element.164.refs_1_, f32[8,128]{1,0:T(8,128)S(1)} %get-tuple-element.165.refs_2_), custom_call_target="tpu_custom_call", output_to_operand_aliasing={{0}: (1, {})} | custom-call | flops 290000000 | bytes 1024 | tf_op jit(solution)/shard_map/widen_trunk/pallas_call | solution.py:83
  141.5 4.3 %widen_heads.2 = (f32[2,512,1792]{2,1,0:T(8,128)}, f32[8,128]{1,0:T(8,128)S(1)}) custom-call(bf16[3584,128]{1,0:T(8,128)(2,1)S(1)} %get-tuple-element.161.refs_0_, bf16[3584,128]{1,0:T(8,128)(2,1)S(1)} %collective-permute-done.26.refs_1_, f32[8,128]{1,0:T(8,128)S(1)} %get-tuple-element.166.refs_2_), custom_call_target="tpu_custom_call" | custom-call | flops 440000000 | bytes 1024 | tf_op jit(solution)/shard_map/widen_heads/pallas_call | solution.py:83
  145.9 3.2 %collective-permute-done.21.refs_0_ = bf16[4608,128]{1,0:T(8,128)(2,1)S(1)} collective-permute-done((bf16[4608,128]{1,0:T(8,128)(2,1)S(1)}, bf16[4608,128]{1,0:T(8,128)(2,1)S(1)}, u32[]{:S(2)}, u32[]{:S(2)}) %collective-permute-start.21) | collective-permute-done | bytes 1179680 | tf_op jit(solution)/shard_map/ppermute | solution.py:1271
  149.0 1.8 %widen_trunk.9 = (f32[2,9,512,512]{3,2,1,0:T(8,128)}, f32[8,128]{1,0:T(8,128)S(1)}) custom-call(bf16[4608,128]{1,0:T(8,128)(2,1)S(1)} %collective-permute-done.28.refs_0_, f32[2,9,512,512]{3,2,1,0:T(8,128)} %get-tuple-element.169.refs_1_, f32[8,128]{1,0:T(8,128)S(1)} %get-tuple-element.170.refs_2_), custom_call_target="tpu_custom_call", output_to_operand_aliasing={{0}: (1, {})} | custom-call | flops 290000000 | bytes 1024 | tf_op jit(solution)/shard_map/widen_trunk/pallas_call | solution.py:83
  150.9 1.8 %widen_trunk.10 = (f32[2,9,512,512]{3,2,1,0:T(8,128)}, f32[8,128]{1,0:T(8,128)S(1)}) custom-call(bf16[4608,128]{1,0:T(8,128)(2,1)S(1)} %get-tuple-element.168.refs_0_, f32[2,9,512,512]{3,2,1,0:T(8,128)} %get-tuple-element.171.refs_1_, f32[8,128]{1,0:T(8,128)S(1)} %get-tuple-element.172.refs_2_), custom_call_target="tpu_custom_call", output_to_operand_aliasing={{0}: (1, {})} | custom-call | flops 290000000 | bytes 1024 | tf_op jit(solution)/shard_map/widen_trunk/pallas_call | solution.py:83
  152.7 1.6 %finish.1 = (bf16[2,64,896]{2,1,0:T(8,128)(2,1)}, f32[2,336,256]{2,1,0:T(8,128)}, f32[2,512]{1,0:T(2,128)}, f32[3,2,1792]{2,1,0:T(2,128)}, f32[8,128]{1,0:T(8,128)S(1)}) custom-call(s32[1,2]{1,0:T(1,128)S(1)} %copy-done.8, f32[336,256]{1,0:T(8,128)S(1)} %get-tuple-element.133.refs_1_, bf16[64,1792]{1,0:T(8,128)(2,1)S(1)} %get-tuple-element.109.refs_3_.refs_2_, ...), custom_call_target="tpu_custom_call" | custom-call | flops 170000000 | bytes 1024 | tf_op jit(solution)/shard_map/finish/pallas_call | solution.py:83
  154.3 2.6 %collective-permute-start.31 = (bf16[3584,128]{1,0:T(8,128)(2,1)S(1)}, bf16[3584,128]{1,0:T(8,128)(2,1)S(1)}, u32[]{:S(2)}, u32[]{:S(2)}) collective-permute-start(bf16[3584,128]{1,0:T(8,128)(2,1)S(1)} %get-tuple-element.180.refs_0_), channel_id=1, source_target_pairs={{0,1},{1,0},{2,3},{3,2},{4,5},{5,4},{6,7},{7,6},{8,9},{9,8},{10,11... | collective-permute-start | bytes 2752520 | tf_op jit(solution)/shard_map/ppermute | solution.py:1274
  156.9 1.8 %widen_trunk.11 = (f32[2,9,512,512]{3,2,1,0:T(8,128)}, f32[8,128]{1,0:T(8,128)S(1)}) custom-call(bf16[4608,128]{1,0:T(8,128)(2,1)S(1)} %collective-permute-done.29.refs_0_, f32[2,9,512,512]{3,2,1,0:T(8,128)} %get-tuple-element.176.refs_1_, f32[8,128]{1,0:T(8,128)S(1)} %get-tuple-element.178.refs_2_), custom_call_target="tpu_custom_call", output_to_operand_aliasing={{0}: (1, {})} | custom-call | flops 290000000 | bytes 1024 | tf_op jit(solution)/shard_map/widen_trunk/pallas_call | solution.py:83
  159.0 4.9 %widen_heads.3 = (f32[2,512,1792]{2,1,0:T(8,128)}, f32[8,128]{1,0:T(8,128)}) custom-call(bf16[3584,128]{1,0:T(8,128)(2,1)S(1)} %get-tuple-element.180.refs_0_, bf16[3584,128]{1,0:T(8,128)(2,1)S(1)} %collective-permute-done.31.refs_1_, f32[2,512,1792]{2,1,0:T(8,128)} %get-tuple-element.181.refs_2_, ...), custom_call_target="tpu_custom_call", output_to_operand_aliasing={{0}: (2, {})} | custom-call | flops 440000000 | bytes 1024 | tf_op jit(solution)/shard_map/widen_heads/pallas_call | solution.py:83
  (72 shorter events, 7.8 us)
Async XLA Ops:
  12.4 8.6 %collective-permute-start = (bf16[2080,256]{1,0:T(8,128)(2,1)}, bf16[2080,256]{1,0:T(8,128)(2,1)S(1)}, u32[]{:S(2)}, u32[]{:S(2)}) collective-permute-start(bf16[2080,256]{1,0:T(8,128)(2,1)} %get-tuple-element.103), channel_id=1, source_target_pairs={{0,1},{1,0},{2,3},{3,2},{4,5},{5,4},{6,7},{7,6},{8,9},{9,8},{10,11... | collective-permute-start | bytes 3194888 | tf_op jit(solution)/shard_map/ppermute | solution.py:1274
  13.0 8.0 %collective-permute-start.2 = (bf16[672,256]{1,0:T(8,128)(2,1)}, bf16[672,256]{1,0:T(8,128)(2,1)S(1)}, u32[]{:S(2)}, u32[]{:S(2)}) collective-permute-start(bf16[672,256]{1,0:T(8,128)(2,1)} %get-tuple-element.105), channel_id=1, source_target_pairs={{0,16},{1,5},{2,18},{3,7},{4,20},{5,1},{6,22},{7,3},{8,24},{9,13},... | collective-permute-start | bytes 1032200 | tf_op jit(solution)/shard_map/ppermute | solution.py:1271
  20.2 2.0 %copy-start = (bf16[2080,256]{1,0:T(8,128)(2,1)S(1)}, bf16[2080,256]{1,0:T(8,128)(2,1)}, u32[]{:S(2)}) copy-start(bf16[2080,256]{1,0:T(8,128)(2,1)} %get-tuple-element.102.refs_0_.refs_6_) | copy-start | bytes 3194884
  20.2 1.9 %copy-start.2 = (bf16[672,256]{1,0:T(8,128)(2,1)S(1)}, bf16[672,256]{1,0:T(8,128)(2,1)}, u32[]{:S(2)}) copy-start(bf16[672,256]{1,0:T(8,128)(2,1)} %get-tuple-element.99.refs_2_.refs_0_) | copy-start | bytes 1032196
  20.2 1.9 %collective-permute-start.1 = (bf16[672,256]{1,0:T(8,128)(2,1)}, bf16[672,256]{1,0:T(8,128)(2,1)S(1)}, u32[]{:S(2)}, u32[]{:S(2)}) collective-permute-start(bf16[672,256]{1,0:T(8,128)(2,1)} %get-tuple-element.99.refs_2_.refs_0_), channel_id=1, source_target_pairs={{0,1},{1,0},{2,3},{3,2},{4,5},{5,4},{6,7},{7,6},{8,9},{9,8},{10,11... | collective-permute-start | bytes 1032200 | tf_op jit(solution)/shard_map/ppermute | solution.py:1274
  21.0 0.7 copy-start.9
  22.2 4.3 %copy-start.3 = (bf16[2,336,512]{2,1,0:T(8,128)(2,1)S(1)}, bf16[2,336,512]{2,1,0:T(8,128)(2,1)}, u32[]{:S(2)}) copy-start(bf16[2,336,512]{2,1,0:T(8,128)(2,1)} %refs_1_.3) | copy-start | bytes 2064388
  22.2 4.3 %copy-start.4 = (bf16[2,144,512]{2,1,0:T(8,128)(2,1)S(1)}, bf16[2,144,512]{2,1,0:T(8,128)(2,1)}, u32[]{:S(2)}) copy-start(bf16[2,144,512]{2,1,0:T(8,128)(2,1)} %get-tuple-element.100.refs_3_) | copy-start | bytes 884740
  22.2 4.3 %copy-start.5 = (f32[2,3,1792]{2,0,1:T(2,128)S(1)}, f32[2,3,1792]{2,0,1:T(2,128)}, u32[]{:S(2)}) copy-start(f32[2,3,1792]{2,0,1:T(2,128)} %param.16) | copy-start | bytes 129028
  22.2 4.3 %copy-start.6 = (f32[8,512]{1,0:T(8,128)S(1)}, f32[8,512]{1,0:T(8,128)}, u32[]{:S(2)}) copy-start(f32[8,512]{1,0:T(8,128)} %get-tuple-element.101.refs_5_) | copy-start | bytes 49156
  22.2 4.3 %copy-start.7 = (f32[2,512]{1,0:T(2,128)S(1)}, f32[2,512]{1,0:T(2,128)}, u32[]{:S(2)}) copy-start(f32[2,512]{1,0:T(2,128)} %refs_4_.3) | copy-start | bytes 12292
  22.2 4.3 %copy-start.8 = (s32[1,2]{1,0:T(1,128)S(1)}, s32[1,2]{1,0:T(1,128)}, u32[]{:S(2)}) copy-start(s32[1,2]{1,0:T(1,128)} %refs_0_.5) | copy-start | bytes 28
  23.2 16.9 %collective-permute-start.4 = (bf16[1344,256]{1,0:T(8,128)(2,1)S(1)}, bf16[1344,256]{1,0:T(8,128)(2,1)S(1)}, u32[]{:S(2)}, u32[]{:S(2)}) collective-permute-start(bf16[1344,256]{1,0:T(8,128)(2,1)S(1)} %get-tuple-element.112), channel_id=1, source_target_pairs={{0,2},{1,5},{2,0},{3,7},{4,6},{5,1},{6,4},{7,3},{8,10},{9,13},{10,... | collective-permute-start | bytes 2064392 | tf_op jit(solution)/shard_map/ppermute | solution.py:1271
  25.0 10.3 %collective-permute-start.5 = (bf16[672,256]{1,0:T(8,128)(2,1)S(1)}, bf16[672,256]{1,0:T(8,128)(2,1)S(1)}, u32[]{:S(2)}, u32[]{:S(2)}) collective-permute-start(bf16[672,256]{1,0:T(8,128)(2,1)S(1)} %get-tuple-element.113), channel_id=1, source_target_pairs={{0,16},{1,5},{2,18},{3,7},{4,20},{5,1},{6,22},{7,3},{8,24},{9,13},... | collective-permute-start | bytes 1032200 | tf_op jit(solution)/shard_map/ppermute | solution.py:1271
  26.5 2.0 %copy-start.1 = (bf16[2,512,1792]{2,1,0:T(8,128)(2,1)S(1)}, bf16[2,512,1792]{2,1,0:T(8,128)(2,1)}, u32[]{:S(2)}) copy-start(bf16[2,512,1792]{2,1,0:T(8,128)(2,1)} %refs_2_.1) | copy-start | bytes 11010052
  34.7 28.9 %collective-permute-start.3 = (bf16[3808,128]{1,0:T(8,128)(2,1)S(1)}, bf16[3808,128]{1,0:T(8,128)(2,1)S(1)}, u32[]{:S(2)}, u32[]{:S(2)}) collective-permute-start(bf16[3808,128]{1,0:T(8,128)(2,1)S(1)} %get-tuple-element.111), channel_id=1, source_target_pairs={{0,16},{1,5},{2,18},{3,7},{4,20},{5,1},{6,22},{7,3},{8,24},{9,13},... | collective-permute-start | bytes 2924552 | tf_op jit(solution)/shard_map/ppermute | solution.py:1271
  39.7 10.5 %collective-permute-start.7 = (bf16[2304,128]{1,0:T(8,128)(2,1)S(1)}, bf16[2304,128]{1,0:T(8,128)(2,1)S(1)}, u32[]{:S(2)}, u32[]{:S(2)}) collective-permute-start(bf16[2304,128]{1,0:T(8,128)(2,1)S(1)} %get-tuple-element.119), channel_id=1, source_target_pairs={{0,2},{1,17},{2,0},{3,19},{4,6},{5,21},{6,4},{7,23},{8,10},{9,25},... | collective-permute-start | bytes 1769480 | tf_op jit(solution)/shard_map/ppermute | solution.py:1271
  43.8 18.0 %collective-permute-start.6 = (bf16[2304,128]{1,0:T(8,128)(2,1)S(1)}, bf16[2304,128]{1,0:T(8,128)(2,1)S(1)}, u32[]{:S(2)}, u32[]{:S(2)}) collective-permute-start(bf16[2304,128]{1,0:T(8,128)(2,1)S(1)} %get-tuple-element.117), channel_id=1, source_target_pairs={{0,16},{1,3},{2,18},{3,1},{4,20},{5,7},{6,22},{7,5},{8,24},{9,11},... | collective-permute-start | bytes 1769480 | tf_op jit(solution)/shard_map/ppermute | solution.py:1271
  50.3 14.2 %collective-permute-start.10 = (bf16[1152,128]{1,0:T(8,128)(2,1)S(1)}, bf16[1152,128]{1,0:T(8,128)(2,1)S(1)}, u32[]{:S(2)}, u32[]{:S(2)}) collective-permute-start(bf16[1152,128]{1,0:T(8,128)(2,1)S(1)} %get-tuple-element.128), channel_id=1, source_target_pairs={{0,4},{1,3},{2,6},{3,1},{4,0},{5,7},{6,2},{7,5},{8,12},{9,11},{10,... | collective-permute-start | bytes 884744 | tf_op jit(solution)/shard_map/ppermute | solution.py:1271
  61.9 9.9 %collective-permute-start.9 = (bf16[1152,128]{1,0:T(8,128)(2,1)S(1)}, bf16[1152,128]{1,0:T(8,128)(2,1)S(1)}, u32[]{:S(2)}, u32[]{:S(2)}) collective-permute-start(bf16[1152,128]{1,0:T(8,128)(2,1)S(1)} %get-tuple-element.126), channel_id=1, source_target_pairs={{0,4},{1,17},{2,6},{3,19},{4,0},{5,21},{6,2},{7,23},{8,12},{9,25},... | collective-permute-start | bytes 884744 | tf_op jit(solution)/shard_map/ppermute | solution.py:1271
  63.9 10.5 %collective-permute-start.8 = (bf16[2016,128]{1,0:T(8,128)(2,1)S(1)}, bf16[2016,128]{1,0:T(8,128)(2,1)S(1)}, u32[]{:S(2)}, u32[]{:S(2)}) collective-permute-start(bf16[2016,128]{1,0:T(8,128)(2,1)S(1)} %get-tuple-element.124), channel_id=1, source_target_pairs={{0,2},{1,17},{2,0},{3,19},{4,6},{5,21},{6,4},{7,23},{8,10},{9,25},... | collective-permute-start | bytes 1548296 | tf_op jit(solution)/shard_map/ppermute | solution.py:1271
  64.6 22.5 %collective-permute-start.14 = (bf16[1152,128]{1,0:T(8,128)(2,1)S(1)}, bf16[1152,128]{1,0:T(8,128)(2,1)S(1)}, u32[]{:S(2)}, u32[]{:S(2)}) collective-permute-start(bf16[1152,128]{1,0:T(8,128)(2,1)S(1)} %get-tuple-element.138.refs_0_), channel_id=1, source_target_pairs={{0,8},{1,9},{2,10},{3,11},{4,12},{5,13},{6,14},{7,15},{8,0},{9,1},... | collective-permute-start | bytes 884744 | tf_op jit(solution)/shard_map/ppermute | solution.py:1271
  71.9 19.7 %collective-permute-start.13 = (bf16[1152,128]{1,0:T(8,128)(2,1)S(1)}, bf16[1152,128]{1,0:T(8,128)(2,1)S(1)}, u32[]{:S(2)}, u32[]{:S(2)}) collective-permute-start(bf16[1152,128]{1,0:T(8,128)(2,1)S(1)} %get-tuple-element.137.refs_0_), channel_id=1, source_target_pairs={{0,8},{1,9},{2,10},{3,11},{4,12},{5,13},{6,14},{7,15},{8,0},{9,1},... | collective-permute-start | bytes 884744 | tf_op jit(solution)/shard_map/ppermute | solution.py:1271
  87.1 10.7 %collective-permute-start.17 = (bf16[1152,128]{1,0:T(8,128)(2,1)S(1)}, bf16[1152,128]{1,0:T(8,128)(2,1)S(1)}, u32[]{:S(2)}, u32[]{:S(2)}) collective-permute-start(bf16[1152,128]{1,0:T(8,128)(2,1)S(1)} %get-tuple-element.144.refs_0_), channel_id=1, source_target_pairs={{0,4},{1,3},{2,6},{3,1},{4,0},{5,7},{6,2},{7,5},{8,12},{9,11},{10,... | collective-permute-start | bytes 884744 | tf_op jit(solution)/shard_map/ppermute | solution.py:1271
  87.2 10.5 %collective-permute-start.12 = (bf16[1120,128]{1,0:T(8,128)(2,1)S(1)}, bf16[1120,128]{1,0:T(8,128)(2,1)S(1)}, u32[]{:S(2)}, u32[]{:S(2)}) collective-permute-start(bf16[1120,128]{1,0:T(8,128)(2,1)S(1)} %get-tuple-element.136), channel_id=1, source_target_pairs={{0,4},{1,3},{2,6},{3,1},{4,0},{5,7},{6,2},{7,5},{8,12},{9,11},{10,... | collective-permute-start | bytes 860168 | tf_op jit(solution)/shard_map/ppermute | solution.py:1271
  91.6 9.2 %collective-permute-start.16 = (bf16[1152,128]{1,0:T(8,128)(2,1)S(1)}, bf16[1152,128]{1,0:T(8,128)(2,1)S(1)}, u32[]{:S(2)}, u32[]{:S(2)}) collective-permute-start(bf16[1152,128]{1,0:T(8,128)(2,1)S(1)} %get-tuple-element.143.refs_0_), channel_id=1, source_target_pairs={{0,4},{1,17},{2,6},{3,19},{4,0},{5,21},{6,2},{7,23},{8,12},{9,25},... | collective-permute-start | bytes 884744 | tf_op jit(solution)/shard_map/ppermute | solution.py:1271
  97.8 17.6 %collective-permute-start.20 = (bf16[2304,128]{1,0:T(8,128)(2,1)S(1)}, bf16[2304,128]{1,0:T(8,128)(2,1)S(1)}, u32[]{:S(2)}, u32[]{:S(2)}) collective-permute-start(bf16[2304,128]{1,0:T(8,128)(2,1)S(1)} %get-tuple-element.150.refs_0_), channel_id=1, source_target_pairs={{0,2},{1,17},{2,0},{3,19},{4,6},{5,21},{6,4},{7,23},{8,10},{9,25},... | collective-permute-start | bytes 1769480 | tf_op jit(solution)/shard_map/ppermute | solution.py:1271
  100.9 14.7 %collective-permute-start.19 = (bf16[2304,128]{1,0:T(8,128)(2,1)S(1)}, bf16[2304,128]{1,0:T(8,128)(2,1)S(1)}, u32[]{:S(2)}, u32[]{:S(2)}) collective-permute-start(bf16[2304,128]{1,0:T(8,128)(2,1)S(1)} %get-tuple-element.149.refs_0_), channel_id=1, source_target_pairs={{0,16},{1,3},{2,18},{3,1},{4,20},{5,7},{6,22},{7,5},{8,24},{9,11},... | collective-permute-start | bytes 1769480 | tf_op jit(solution)/shard_map/ppermute | solution.py:1271
  102.5 11.9 %collective-permute-start.15 = (bf16[1120,128]{1,0:T(8,128)(2,1)S(1)}, bf16[1120,128]{1,0:T(8,128)(2,1)S(1)}, u32[]{:S(2)}, u32[]{:S(2)}) collective-permute-start(bf16[1120,128]{1,0:T(8,128)(2,1)S(1)} %get-tuple-element.142.refs_0_), channel_id=1, source_target_pairs={{0,8},{1,9},{2,10},{3,11},{4,12},{5,13},{6,14},{7,15},{8,0},{9,1},... | collective-permute-start | bytes 860168 | tf_op jit(solution)/shard_map/ppermute | solution.py:1271
  103.8 11.6 %collective-permute-start.11 = (bf16[1120,128]{1,0:T(8,128)(2,1)S(1)}, bf16[1120,128]{1,0:T(8,128)(2,1)S(1)}, u32[]{:S(2)}, u32[]{:S(2)}) collective-permute-start(bf16[1120,128]{1,0:T(8,128)(2,1)S(1)} %get-tuple-element.134), channel_id=1, source_target_pairs={{0,16},{16,0},{1,17},{17,1},{2,18},{18,2},{3,19},{19,3},{4,20},{20... | collective-permute-start | bytes 860168 | tf_op jit(solution)/shard_map/ppermute | solution.py:1344
  115.5 14.5 %collective-permute-start.25 = (bf16[4608,128]{1,0:T(8,128)(2,1)S(1)}, bf16[4608,128]{1,0:T(8,128)(2,1)S(1)}, u32[]{:S(2)}, u32[]{:S(2)}) collective-permute-start(bf16[4608,128]{1,0:T(8,128)(2,1)S(1)} %get-tuple-element.156.refs_0_), channel_id=1, source_target_pairs={{0,1},{1,0},{2,3},{3,2},{4,5},{5,4},{6,7},{7,6},{8,9},{9,8},{10,11... | collective-permute-start | bytes 3538952 | tf_op jit(solution)/shard_map/ppermute | solution.py:1274
  115.7 17.2 %collective-permute-start.24 = (bf16[4608,128]{1,0:T(8,128)(2,1)S(1)}, bf16[4608,128]{1,0:T(8,128)(2,1)S(1)}, u32[]{:S(2)}, u32[]{:S(2)}) collective-permute-start(bf16[4608,128]{1,0:T(8,128)(2,1)S(1)} %get-tuple-element.153.refs_0_), channel_id=1, source_target_pairs={{0,1},{1,0},{2,3},{3,2},{4,5},{5,4},{6,7},{7,6},{8,9},{9,8},{10,11... | collective-permute-start | bytes 3538952 | tf_op jit(solution)/shard_map/ppermute | solution.py:1274
  116.2 21.1 %collective-permute-start.27 = (bf16[4608,128]{1,0:T(8,128)(2,1)S(1)}, bf16[4608,128]{1,0:T(8,128)(2,1)S(1)}, u32[]{:S(2)}, u32[]{:S(2)}) collective-permute-start(bf16[4608,128]{1,0:T(8,128)(2,1)S(1)} %get-tuple-element.156.refs_0_), channel_id=1, source_target_pairs={{0,16},{1,5},{2,18},{3,7},{4,20},{5,1},{6,22},{7,3},{8,24},{9,13},... | collective-permute-start | bytes 3538952 | tf_op jit(solution)/shard_map/ppermute | solution.py:1271
  118.0 9.8 %collective-permute-start.22 = (bf16[1120,128]{1,0:T(8,128)(2,1)S(1)}, bf16[1120,128]{1,0:T(8,128)(2,1)S(1)}, u32[]{:S(2)}, u32[]{:S(2)}) collective-permute-start(bf16[1120,128]{1,0:T(8,128)(2,1)S(1)} %get-tuple-element.148.refs_0_.refs_4_), channel_id=1, source_target_pairs={{0,4},{1,3},{2,6},{3,1},{4,0},{5,7},{6,2},{7,5},{8,12},{9,11},{10,... | collective-permute-start | bytes 860168 | tf_op jit(solution)/shard_map/ppermute | solution.py:1271
  127.8 8.6 %collective-permute-start.23 = (bf16[1792,128]{1,0:T(8,128)(2,1)S(1)}, bf16[1792,128]{1,0:T(8,128)(2,1)S(1)}, u32[]{:S(2)}, u32[]{:S(2)}) collective-permute-start(bf16[1792,128]{1,0:T(8,128)(2,1)S(1)} %get-tuple-element.155.refs_0_), channel_id=1, source_target_pairs={{0,2},{1,17},{2,0},{3,19},{4,6},{5,21},{6,4},{7,23},{8,10},{9,25},... | collective-permute-start | bytes 1376264 | tf_op jit(solution)/shard_map/ppermute | solution.py:1271
  129.9 19.1 %collective-permute-start.21 = (bf16[4608,128]{1,0:T(8,128)(2,1)S(1)}, bf16[4608,128]{1,0:T(8,128)(2,1)S(1)}, u32[]{:S(2)}, u32[]{:S(2)}) collective-permute-start(bf16[4608,128]{1,0:T(8,128)(2,1)S(1)} %get-tuple-element.153.refs_0_), channel_id=1, source_target_pairs={{0,2},{1,5},{2,0},{3,7},{4,6},{5,1},{6,4},{7,3},{8,10},{9,13},{10,... | collective-permute-start | bytes 3538952 | tf_op jit(solution)/shard_map/ppermute | solution.py:1271
  137.4 11.7 %collective-permute-start.28 = (bf16[4608,128]{1,0:T(8,128)(2,1)S(1)}, bf16[4608,128]{1,0:T(8,128)(2,1)S(1)}, u32[]{:S(2)}, u32[]{:S(2)}) collective-permute-start(bf16[4608,128]{1,0:T(8,128)(2,1)S(1)} %get-tuple-element.163.refs_0_), channel_id=1, source_target_pairs={{0,1},{1,0},{2,3},{3,2},{4,5},{5,4},{6,7},{7,6},{8,9},{9,8},{10,11... | collective-permute-start | bytes 3538952 | tf_op jit(solution)/shard_map/ppermute | solution.py:1274
  137.4 4.2 %collective-permute-start.26 = (bf16[3584,128]{1,0:T(8,128)(2,1)S(1)}, bf16[3584,128]{1,0:T(8,128)(2,1)S(1)}, u32[]{:S(2)}, u32[]{:S(2)}) collective-permute-start(bf16[3584,128]{1,0:T(8,128)(2,1)S(1)} %get-tuple-element.161.refs_0_), channel_id=1, source_target_pairs={{0,1},{1,0},{2,3},{3,2},{4,5},{5,4},{6,7},{7,6},{8,9},{9,8},{10,11... | collective-permute-start | bytes 2752520 | tf_op jit(solution)/shard_map/ppermute | solution.py:1274
  137.9 16.5 %collective-permute-start.30 = (bf16[3584,128]{1,0:T(8,128)(2,1)S(1)}, bf16[3584,128]{1,0:T(8,128)(2,1)S(1)}, u32[]{:S(2)}, u32[]{:S(2)}) collective-permute-start(bf16[3584,128]{1,0:T(8,128)(2,1)S(1)} %get-tuple-element.161.refs_0_), channel_id=1, source_target_pairs={{0,16},{1,5},{2,18},{3,7},{4,20},{5,1},{6,22},{7,3},{8,24},{9,13},... | collective-permute-start | bytes 2752520 | tf_op jit(solution)/shard_map/ppermute | solution.py:1271
  139.6 13.1 %collective-permute-start.18 = (bf16[1120,128]{1,0:T(8,128)(2,1)S(1)}, bf16[1120,128]{1,0:T(8,128)(2,1)S(1)}, u32[]{:S(2)}, u32[]{:S(2)}) collective-permute-start(bf16[1120,128]{1,0:T(8,128)(2,1)S(1)} %get-tuple-element.148.refs_0_.refs_4_), channel_id=1, source_target_pairs={{0,1},{1,0},{2,3},{3,2},{4,5},{5,4},{6,7},{7,6},{8,9},{9,8},{10,11... | collective-permute-start | bytes 860168 | tf_op jit(solution)/shard_map/ppermute | solution.py:1274
  149.0 7.9 %collective-permute-start.29 = (bf16[4608,128]{1,0:T(8,128)(2,1)S(1)}, bf16[4608,128]{1,0:T(8,128)(2,1)S(1)}, u32[]{:S(2)}, u32[]{:S(2)}) collective-permute-start(bf16[4608,128]{1,0:T(8,128)(2,1)S(1)} %get-tuple-element.168.refs_0_), channel_id=1, source_target_pairs={{0,1},{1,0},{2,3},{3,2},{4,5},{5,4},{6,7},{7,6},{8,9},{9,8},{10,11... | collective-permute-start | bytes 3538952 | tf_op jit(solution)/shard_map/ppermute | solution.py:1274
  154.3 4.7 %collective-permute-start.31 = (bf16[3584,128]{1,0:T(8,128)(2,1)S(1)}, bf16[3584,128]{1,0:T(8,128)(2,1)S(1)}, u32[]{:S(2)}, u32[]{:S(2)}) collective-permute-start(bf16[3584,128]{1,0:T(8,128)(2,1)S(1)} %get-tuple-element.180.refs_0_), channel_id=1, source_target_pairs={{0,1},{1,0},{2,3},{3,2},{4,5},{5,4},{6,7},{7,6},{8,9},{9,8},{10,11... | collective-permute-start | bytes 2752520 | tf_op jit(solution)/shard_map/ppermute | solution.py:1274
